TPU v7x, 32 devices: a whole 2x2x4 slice. The times are simulated.
32 devices in a mesh: wide: 8 (over z, y), narrow: 4 (over x, core).
Axes of the slice: x: 2, y: 2, z: 4, core: 2. Of those that a mesh axis runs over, the one named last changes fastest.
Arguments:
- ends: bfloat16 [16384, 1024], P(('wide', 'narrow')), may hold values from -6 to 6
- lengths: int32 [4, 2, 3], replicated, may hold values from 1 to 896, 1024 in all within a row
- w_qkv: bfloat16 [2, 1024, 3072], P(None, None, 'narrow'), may hold values from -0.1875 to 0.1875
- w_out: bfloat16 [2, 1024, 1024], P(None, None, 'narrow'), may hold values from -0.1875 to 0.1875
- w_up: bfloat16 [2, 1024, 4096], P(None, None, 'narrow'), may hold values from -0.1875 to 0.1875
- b_up: bfloat16 [2, 4096], P(None, 'narrow'), may hold values from -3 to 3
- w_down: bfloat16 [2, 4096, 1024], P(None, None, 'narrow'), may hold values from -0.09375 to 0.09375
- norm_gain: bfloat16 [2, 4, 1024], P(None, None, 'narrow'), may hold values from 0.5 to 1.5
- norm_bias: bfloat16 [2, 4, 1024], P(None, None, 'narrow'), may hold values from -1.75 to 1.75
Outputs:
- ends_out: bfloat16 [16384, 1024], P(('wide', 'narrow'))
- grad_qkv: float32 [2, 1024, 3072], P(None, None, 'narrow')
- grad_out: float32 [2, 1024, 1024], P(None, None, 'narrow')
- grad_up: float32 [2, 1024, 4096], P(None, None, 'narrow')
- grad_up_bias: float32 [2, 4096], P(None, 'narrow')
- grad_down: float32 [2, 4096, 1024], P(None, None, 'narrow')
- grad_gain: float32 [2, 4, 1024], P(None, None, 'narrow')
- grad_bias: float32 [2, 4, 1024], P(None, None, 'narrow')
Inputs may be any that keep to these rules, and one draw needn't show every extreme that they name: Each row of 3 document lengths sums to 1024; its longest is exactly 896, at a position drawn from the seed.
All inputs are finite; a program needn't handle non-finite values.
Results may differ from a plain program's by a relative error of at most 0.018.
Values may be sent and summed in bfloat16 or wider, within the bound.
A program may use at most 640 MiB of HBM per device.

v0:
```python
import math

import jax
import jax.numpy as jnp
from jax import lax
from jax.sharding import PartitionSpec as P

H = 16
HD = 64
MICRO = 2


EPSILON = 1e-05
MASKED = -1e30


def from_behind(block, axis, distance):
    devices = range(lax.axis_size(axis))
    route = [(i - distance, i) for i in devices if i - distance in devices]
    return lax.ppermute(block, axis, route)


def as_sent(shard):
    return jax.tree.map(lambda a: a.astype(jnp.bfloat16) if a.dtype == jnp.float32 else a, shard)


def layer_norm(values, gain_row, shift_row):
    center = jnp.mean(values, axis=-1, keepdims=True)
    centred = values - center
    spread = jnp.mean(centred * centred, axis=-1, keepdims=True)
    return centred * lax.rsqrt(spread + EPSILON) * gain_row + shift_row


def rotate(field, places):
    halfway = field.shape[-1] // 2
    ladder = jnp.arange(halfway, dtype=jnp.float32) * (2.0 / field.shape[-1])
    inverse = jnp.exp(-math.log(10000.0) * ladder)
    angles = places[:, None] * inverse[None, :]
    cosine = jnp.cos(angles)[:, None, :]
    sine_value = jnp.sin(angles)[:, None, :]
    first = field[..., :halfway]
    second = field[..., halfway:]
    return jnp.concatenate(
        [first * cosine - second * sine_value, second * cosine + first * sine_value], axis=-1
    )


def rotate_rows(matrix, places):
    row_count = matrix.shape[0]
    return rotate(matrix.reshape(row_count, H, HD), places).reshape(row_count, H * HD)


def doc_tables(lengths_row, places):
    closing = jnp.cumsum(lengths_row)
    passed = (places[:, None] >= closing[None, :]).astype(jnp.int32)
    doc_number = jnp.sum(passed, axis=1)
    opening = jnp.sum(passed * lengths_row[None, :], axis=1)
    return (doc_number, places - opening)


def smooth(values):
    return jax.nn.gelu(values, approximate=False)


def when(active, action, *operands):

    def nothing(*inner):
        return jax.tree.map(jnp.zeros_like, action(*inner))

    return lax.cond(active, action, nothing, *operands)


def by_heads(matrix):
    return matrix.reshape(matrix.shape[0], H, HD).transpose(1, 0, 2)


def from_heads(tensor):
    return tensor.transpose(1, 0, 2).reshape(tensor.shape[1], H * HD)


def head_part(resid, w_qkv, gains, shifts, offsets):
    normed = layer_norm(resid, gains[0], shifts[0]).astype(jnp.bfloat16)
    projected = jnp.dot(normed, w_qkv, preferred_element_type=jnp.float32)
    query, keys_own, values_own = jnp.split(projected, 3, axis=1)
    query = rotate_rows(query, offsets).astype(jnp.bfloat16)
    keys_own = rotate_rows(keys_own, offsets).astype(jnp.bfloat16)
    return (query, keys_own, values_own.astype(jnp.bfloat16))


def attend_forward(query, keys_all, values_all, allowed):

    def one_head(triple):
        q_head, k_head, v_head = triple
        scores = jnp.dot(q_head, k_head.T, preferred_element_type=jnp.float32) * HD ** (-0.5)
        scores = jnp.where(allowed, scores, MASKED)
        summit = jnp.max(scores, axis=1, keepdims=True)
        weights = jnp.exp(scores - summit)
        totals = jnp.sum(weights, axis=1, keepdims=True)
        chances = (weights / totals).astype(jnp.bfloat16)
        mixture = jnp.dot(chances, v_head, preferred_element_type=jnp.float32)
        return (mixture, (summit + jnp.log(totals))[:, 0])

    mixture, log_totals = lax.map(
        one_head, (by_heads(query), by_heads(keys_all), by_heads(values_all))
    )
    return (from_heads(mixture), log_totals)


def rest_part(
    resid, query, keys_all, values_all, allowed, w_out, w_up, b_up, w_down, gains, shifts
):
    mixture, log_totals = attend_forward(query, keys_all, values_all, allowed)
    mixture = mixture.astype(jnp.bfloat16)
    branch = jnp.dot(mixture, w_out, preferred_element_type=jnp.float32)
    middle = resid + layer_norm(branch, gains[1], shifts[1])
    normed = layer_norm(middle, gains[2], shifts[2]).astype(jnp.bfloat16)
    hidden = jnp.dot(normed, w_up, preferred_element_type=jnp.float32) + b_up
    activated = smooth(hidden).astype(jnp.bfloat16)
    second = jnp.dot(activated, w_down, preferred_element_type=jnp.float32)
    result = middle + layer_norm(second, gains[3], shifts[3])
    return (result, mixture, log_totals, branch, middle, hidden, second)


def tail_back(
    grad_result, middle, branch, hidden, second, mixture, w_out, w_up, w_down, gains, shifts
):
    grad_second, gain_three, shift_three = jax.vjp(layer_norm, second, gains[3], shifts[3])[1](
        grad_result
    )
    grad_second = grad_second.astype(jnp.bfloat16)
    activated = smooth(hidden).astype(jnp.bfloat16)
    grad_down = jnp.dot(activated.T, grad_second, preferred_element_type=jnp.float32)
    grad_act = jnp.dot(grad_second, w_down.T, preferred_element_type=jnp.float32)
    grad_hidden = jax.vjp(smooth, hidden)[1](grad_act)[0].astype(jnp.bfloat16)
    grad_bias_up = jnp.sum(grad_hidden.astype(jnp.float32), axis=0)
    normed = layer_norm(middle, gains[2], shifts[2]).astype(jnp.bfloat16)
    grad_up = jnp.dot(normed.T, grad_hidden, preferred_element_type=jnp.float32)
    grad_normed = jnp.dot(grad_hidden, w_up.T, preferred_element_type=jnp.float32)
    grad_middle, gain_two, shift_two = jax.vjp(layer_norm, middle, gains[2], shifts[2])[1](
        grad_normed
    )
    grad_middle = grad_result + grad_middle
    grad_branch, gain_one, shift_one = jax.vjp(layer_norm, branch, gains[1], shifts[1])[1](
        grad_middle
    )
    grad_branch = grad_branch.astype(jnp.bfloat16)
    grad_attn_out = jnp.dot(mixture.T, grad_branch, preferred_element_type=jnp.float32)
    grad_mixture = jnp.dot(grad_branch, w_out.T, preferred_element_type=jnp.float32).astype(
        jnp.bfloat16
    )
    return (
        grad_middle,
        grad_mixture,
        (grad_attn_out, grad_up, grad_bias_up, grad_down),
        (gain_one, gain_two, gain_three),
        (shift_one, shift_two, shift_three),
    )


def attend_backward(query, keys_all, values_all, allowed, log_totals, grad_mixture):

    def one_head(bundle):
        q_head, k_head, v_head, lse_head, g_head = bundle
        scores = jnp.dot(q_head, k_head.T, preferred_element_type=jnp.float32) * HD ** (-0.5)
        scores = jnp.where(allowed, scores, MASKED)
        chances = jnp.exp(scores - lse_head[:, None])
        grad_prob = jnp.dot(g_head, v_head.T, preferred_element_type=jnp.float32)
        row_inner = jnp.sum(grad_prob * chances, axis=1, keepdims=True)
        grad_score = (chances * (grad_prob - row_inner)).astype(jnp.bfloat16)
        grad_query = jnp.dot(grad_score, k_head, preferred_element_type=jnp.float32) * HD ** (-0.5)
        grad_keys = jnp.dot(grad_score.T, q_head, preferred_element_type=jnp.float32) * HD ** (-0.5)
        grad_values = jnp.dot(
            chances.astype(jnp.bfloat16).T, g_head, preferred_element_type=jnp.float32
        )
        return (grad_query, grad_keys, grad_values)

    grad_query, grad_keys, grad_values = lax.map(
        one_head,
        (
            by_heads(query),
            by_heads(keys_all),
            by_heads(values_all),
            log_totals,
            by_heads(grad_mixture),
        ),
    )
    return (from_heads(grad_query), from_heads(grad_keys), from_heads(grad_values))


def head_back(
    resid, grad_middle, grad_query, grad_keys, grad_values, w_qkv, gains, shifts, offsets
):
    grad_query = rotate_rows(grad_query, -offsets)
    grad_keys = rotate_rows(grad_keys, -offsets)
    grad_projected = jnp.concatenate([grad_query, grad_keys, grad_values], axis=1).astype(
        jnp.bfloat16
    )
    normed = layer_norm(resid, gains[0], shifts[0]).astype(jnp.bfloat16)
    grad_qkv = jnp.dot(normed.T, grad_projected, preferred_element_type=jnp.float32)
    grad_normed = jnp.dot(grad_projected, w_qkv.T, preferred_element_type=jnp.float32)
    grad_resid, gain_zero, shift_zero = jax.vjp(layer_norm, resid, gains[0], shifts[0])[1](
        grad_normed
    )
    return (grad_middle + grad_resid, grad_qkv, gain_zero, shift_zero)


def put(stack, item, micro_at, active):
    former = lax.dynamic_index_in_dim(stack, micro_at, 0, keepdims=False)
    return lax.dynamic_update_index_in_dim(stack, jnp.where(active, item, former), micro_at, 0)


def fetch(stack, micro_at):
    return lax.dynamic_index_in_dim(stack, micro_at, 0, keepdims=False)


def on_device(ends, lengths, w_qkv, w_out, w_up, b_up, w_down, norm_gain, norm_bias):
    halfway = lax.axis_size("wide") // 2
    wide_at = lax.axis_index("wide")
    section = wide_at // halfway
    group_at = wide_at % halfway
    narrow_at = lax.axis_index("narrow")
    row_count = ends.shape[0] // MICRO
    width = ends.shape[1]
    stream_len = row_count * lax.axis_size("narrow")
    blocks = ends.reshape(MICRO, row_count, width)

    def mine(stack):
        return lax.dynamic_index_in_dim(stack, section, 0, keepdims=False)

    full_qkv, full_out, full_up, full_bias, full_down, full_gain, full_shift = (
        lax.all_gather(mine(w_qkv), "narrow", axis=1, tiled=True),
        lax.all_gather(mine(w_out), "narrow", axis=1, tiled=True),
        lax.all_gather(mine(w_up), "narrow", axis=1, tiled=True),
        lax.all_gather(mine(b_up), "narrow", axis=0, tiled=True),
        lax.all_gather(mine(w_down), "narrow", axis=1, tiled=True),
        lax.all_gather(mine(norm_gain), "narrow", axis=1, tiled=True),
        lax.all_gather(mine(norm_bias), "narrow", axis=1, tiled=True),
    )
    gains = full_gain.astype(jnp.float32)
    shifts = full_shift.astype(jnp.float32)
    doc_lengths = lax.dynamic_index_in_dim(lengths, group_at, 0, keepdims=False)
    key_places = jnp.arange(stream_len, dtype=jnp.int32)
    query_places = narrow_at * row_count + jnp.arange(row_count, dtype=jnp.int32)

    def tables(micro_at):
        lengths_now = fetch(doc_lengths, micro_at)
        key_doc = doc_tables(lengths_now, key_places)[0]
        query_doc, query_offset = doc_tables(lengths_now, query_places)
        allowed = (key_places[None, :] <= query_places[:, None]) & (
            key_doc[None, :] == query_doc[:, None]
        )
        return (allowed, query_offset.astype(jnp.float32))

    float_rows = jnp.zeros((MICRO, row_count, width), jnp.float32)
    half_rows = jnp.zeros((MICRO, row_count, width), jnp.bfloat16)
    stored = [
        float_rows,
        half_rows,
        half_rows,
        half_rows,
        half_rows,
        jnp.zeros((MICRO, H, row_count), jnp.float32),
        float_rows,
        float_rows,
        jnp.zeros((MICRO, row_count, full_up.shape[1]), jnp.float32),
        float_rows,
    ]
    results = half_rows
    arrived = jnp.zeros((row_count, width), jnp.bfloat16)
    for step_at in range(MICRO + 1):
        lag_at = step_at - section
        active = (lag_at >= 0) & (lag_at < MICRO)
        micro_at = jnp.clip(lag_at, 0, MICRO - 1)
        allowed, offsets = tables(micro_at)
        entry = jnp.where(section == 0, fetch(blocks, micro_at), arrived).astype(jnp.float32)
        query, keys_own, values_own = when(
            active, head_part, entry, full_qkv, gains, shifts, offsets
        )
        keys_all, values_all = (
            lax.all_gather(keys_own, "narrow", axis=0, tiled=True),
            lax.all_gather(values_own, "narrow", axis=0, tiled=True),
        )
        outcome = when(
            active,
            rest_part,
            entry,
            query,
            keys_all,
            values_all,
            allowed,
            full_out,
            full_up,
            full_bias,
            full_down,
            gains,
            shifts,
        )
        sent = outcome[0].astype(jnp.bfloat16)
        arrived = from_behind(sent, "wide", halfway)
        fresh = (entry, query, keys_own, values_own) + tuple(outcome[1:])
        stored = [put(stack, item, micro_at, active) for stack, item in zip(stored, fresh)]
        results = put(results, sent, micro_at, active & (section == 1))
    arrived = jnp.zeros((row_count, width), jnp.bfloat16)
    summed = None
    for step_at in range(MICRO + 1):
        lag_at = step_at - 1 + section
        active = (lag_at >= 0) & (lag_at < MICRO)
        micro_at = jnp.clip(lag_at, 0, MICRO - 1)
        allowed, offsets = tables(micro_at)
        incoming = jnp.where(section == 1, fetch(blocks, micro_at), arrived).astype(jnp.float32)
        resid, query, keys_own, values_own, mixture, log_totals, branch, middle, hidden, second = [
            fetch(stack, micro_at) for stack in stored
        ]
        grad_middle, grad_mixture, matrices, gain_parts, shift_parts = when(
            active,
            tail_back,
            incoming,
            middle,
            branch,
            hidden,
            second,
            mixture,
            full_out,
            full_up,
            full_down,
            gains,
            shifts,
        )
        keys_all, values_all = (
            lax.all_gather(keys_own, "narrow", axis=0, tiled=True),
            lax.all_gather(values_own, "narrow", axis=0, tiled=True),
        )
        grad_query, grad_keys_all, grad_values_all = when(
            active, attend_backward, query, keys_all, values_all, allowed, log_totals, grad_mixture
        )
        grad_keys, grad_values = (
            lax.psum_scatter(grad_keys_all, "narrow", scatter_dimension=0, tiled=True),
            lax.psum_scatter(grad_values_all, "narrow", scatter_dimension=0, tiled=True),
        )
        grad_resid, grad_qkv, gain_zero, shift_zero = when(
            active,
            head_back,
            resid,
            grad_middle,
            grad_query,
            grad_keys,
            grad_values,
            full_qkv,
            gains,
            shifts,
            offsets,
        )
        sent = grad_resid.astype(jnp.bfloat16)
        arrived = from_behind(sent, "wide", -halfway)
        results = put(results, sent, micro_at, active & (section == 0))
        gain_grads = jnp.stack([gain_zero, gain_parts[0], gain_parts[1], gain_parts[2]])
        shift_grads = jnp.stack([shift_zero, shift_parts[0], shift_parts[1], shift_parts[2]])
        pieces = (
            grad_qkv,
            matrices[0],
            matrices[1],
            matrices[2],
            matrices[3],
            gain_grads,
            shift_grads,
        )
        summed = (
            pieces
            if summed is None
            else tuple((older + newer for older, newer in zip(summed, pieces)))
        )
    summed = (
        lax.psum_scatter(
            summed[0].astype(jnp.bfloat16), "narrow", scatter_dimension=1, tiled=True
        ).astype(jnp.float32),
        lax.psum_scatter(
            summed[1].astype(jnp.bfloat16), "narrow", scatter_dimension=1, tiled=True
        ).astype(jnp.float32),
        lax.psum_scatter(
            summed[2].astype(jnp.bfloat16), "narrow", scatter_dimension=1, tiled=True
        ).astype(jnp.float32),
        lax.psum_scatter(
            summed[3].astype(jnp.bfloat16), "narrow", scatter_dimension=0, tiled=True
        ).astype(jnp.float32),
        lax.psum_scatter(
            summed[4].astype(jnp.bfloat16), "narrow", scatter_dimension=1, tiled=True
        ).astype(jnp.float32),
        lax.psum_scatter(
            summed[5].astype(jnp.bfloat16), "narrow", scatter_dimension=1, tiled=True
        ).astype(jnp.float32),
        lax.psum_scatter(
            summed[6].astype(jnp.bfloat16), "narrow", scatter_dimension=1, tiled=True
        ).astype(jnp.float32),
    )
    select = (jnp.arange(2) == section).astype(jnp.float32)
    padded = tuple((select.reshape((2,) + (1,) * piece.ndim) * piece[None] for piece in summed))
    totals = jax.tree.map(lambda part: part.astype(jnp.float32), lax.psum(as_sent(padded), "wide"))
    return (results.reshape(MICRO * row_count, width),) + tuple(totals)


def solution(mesh):
    placed = (
        P(("wide", "narrow"), None),
        P(),
        P(None, None, "narrow"),
        P(None, None, "narrow"),
        P(None, None, "narrow"),
        P(None, "narrow"),
        P(None, None, "narrow"),
        P(None, None, "narrow"),
        P(None, None, "narrow"),
    )
    return jax.shard_map(
        on_device,
        mesh=mesh,
        in_specs=placed,
        out_specs=(
            P(("wide", "narrow"), None),
            P(None, None, "narrow"),
            P(None, None, "narrow"),
            P(None, None, "narrow"),
            P(None, "narrow"),
            P(None, None, "narrow"),
            P(None, None, "narrow"),
            P(None, None, "narrow"),
        ),
        check_vma=False,
    )
```

profile of v0, /device:TPU:0, one launch (start us, length us, event | category | flops | bytes accessed | tf_op | source)
XLA Modules:
  0.0 2566.2 jit_solution(3797250634259683610)
XLA Ops:
  27.4 32.2 %all-gather.42.cloned.1.call-done = bf16[1,1024,3072]{2,1,0:T(8,128)(2,1)} async-done(((bf16[1,1024,768]{2,1,0:T(8,128)(2,1)}), bf16[1,1024,3072]{2,1,0:T(8,128)(2,1)}) %all-gather.42.cloned.1.call-update) | async-done | bytes 6291472 | tf_op jit(solution)/shard_map/all_gather | solution.py:231
  88.2 21.5 all-gather.30.cloned.1.call-done
  109.7 24.9 all-gather.32.cloned.1.call-done
  134.6 60.3 %all-gather.46.cloned.1.call-done = bf16[1,1024,4096]{2,1,0:T(8,128)(2,1)} async-done(((bf16[1,1024,1024]{2,1,0:T(8,128)(2,1)}), bf16[1,1024,4096]{2,1,0:T(8,128)(2,1)}) %all-gather.46.cloned.1.call-update) | async-done | bytes 8388624 | tf_op jit(solution)/shard_map/all_gather | solution.py:233
  194.9 61.4 %all-gather.48.cloned.1.call-done = bf16[1,4096,1024]{2,1,0:T(8,128)(2,1)} async-done(((bf16[1,4096,256]{2,1,0:T(8,128)(2,1)}), bf16[1,4096,1024]{2,1,0:T(8,128)(2,1)}) %all-gather.48.cloned.1.call-update) | async-done | bytes 8388624 | tf_op jit(solution)/shard_map/all_gather | solution.py:235
  256.3 113.4 %conditional.16 = (f32[16,256]{1,0:T(8,128)S(1)}, f32[256,1024]{1,0:T(8,128)S(1)}, f32[256,1024]{1,0:T(8,128)}, f32[256,4096]{1,0:T(8,128)}, f32[256,1024]{1,0:T...) conditional(s32[]{:T(128)} %convert_element_type.503, () %tuple.242, ...), branch_computations={%region_6.7_spmd, %region_7.20_spmd} | conditional | flops 4978122240 | bytes 99959296 | solution.py:70
  258.0 80.3 %while.99 = (s32[]{:T(128)}, bf16[16,256,64]{1,2,0:T(8,128)(2,1)}, f32[16,256]{1,0:T(8,128)}, bf16[16,256,64]{1,2,0:T(8,128)(2,1)}, bf16[16,1024,64]{1,2,0:T(8,1...) while((s32[]{:T(128)}, bf16[16,256,64]{1,2,0:T(8,128)(2,1)}, ...), condition=%wide.region_13.13_spmd, body=%wide.region_10.12_spmd.sunk | while | flops 69205760 | bytes 3780705 | solution.py:103
  383.6 22.8 conditional.17
  442.6 25.0 all-gather.36.cloned.1.call-done
  467.6 116.8 %conditional.18 = (f32[16,256]{1,0:T(8,128)S(1)}, f32[256,1024]{1,0:T(8,128)S(1)}, f32[256,1024]{1,0:T(8,128)}, f32[256,4096]{1,0:T(8,128)}, f32[256,1024]{1,0:T...) conditional(s32[]{:T(128)} %convert_element_type.511, ...), branch_computations={%region_26.27_spmd, %region_27.40_spmd} | conditional | flops 4978122240 | bytes 88424880 | solution.py:70
  468.6 79.8 %while.100 = (s32[]{:T(128)}, bf16[16,256,64]{1,2,0:T(8,128)(2,1)}, f32[16,256]{1,0:T(8,128)}, bf16[16,256,64]{1,2,0:T(8,128)(2,1)}, bf16[16,1024,64]{1,2,0:T(8,...) while((s32[]{:T(128)}, bf16[16,256,64]{1,2,0:T(8,128)(2,1)}, ...), condition=%wide.region_33.33_spmd, body=%wide.region_30.32_spmd.sunk | while | flops 69205760 | bytes 3780705 | solution.py:103
  769.4 350.2 %reduce-scatter.17.cloned.1.call-done = f32[256,1024]{0,1:T(8,128)} async-done(((f32[1024,1024]{0,1:T(8,128)}), f32[256,1024]{0,1:T(8,128)}) %reduce-scatter.17.cloned.1.call-update) | async-done | bytes 1048592 | tf_op jit(solution)/shard_map/reduce_scatter | solution.py:337
  1119.6 47.1 %reduce-scatter.19.cloned.1.call-done = f32[256,1024]{0,1:T(8,128)} async-done(((f32[1024,1024]{0,1:T(8,128)}), f32[256,1024]{0,1:T(8,128)}) %reduce-scatter.19.cloned.1.call-update) | async-done | bytes 1048592 | tf_op jit(solution)/shard_map/reduce_scatter | solution.py:338
  1176.0 37.9 %collective-permute-done.2 = bf16[256,1024]{1,0:T(8,128)(2,1)} collective-permute-done((bf16[256,1024]{1,0:T(8,128)(2,1)}, bf16[256,1024]{1,0:T(8,128)(2,1)}, u32[]{:S(2)}, u32[]{:S(2)}) %collective-permute-start.2) | collective-permute-done | bytes 524320 | tf_op jit(solution)/shard_map/ppermute | solution.py:20
  1215.2 67.0 %conditional.24 = (f32[256,1024]{1,0:T(8,128)}, bf16[256,1024]{1,0:T(8,128)(2,1)}, f32[1024,1024]{1,0:T(8,128)}, f32[1024,4096]{1,0:T(8,128)}, f32[4096]{0:T(102...) conditional(s32[]{:T(128)} %convert_element_type.528, ...), branch_computations={%region_102.103_spmd, %region_103.123_spmd} | conditional | flops 9767741440 | bytes 200450880 | solution.py:70
  1282.9 136.1 %conditional.25 = (f32[256,1024]{0,1:T(8,128)}, f32[1024,1024]{0,1:T(8,128)}, f32[1024,1024]{0,1:T(8,128)}) conditional(s32[]{:T(128)} %convert_element_type.528, () %tuple.261, (bf16[2,256,1024]{1,2,0:T(8,128)(2,1)}, s32[]{:T(128)}, bf16[1024,1024]{0,1:T(8,128)(2,1)}, bf16[1024,1024]{0,1:T(8,128)(2,1)}, f32[2,16,256]{2,1,0:T(8,128)S(1)}, ...), branch_computations={%region_123.124_spmd, %region_124.130_spmd} | conditional | flops 170739968 | bytes 11930873 | solution.py:70
  1287.9 131.1 %while.103 = (s32[]{:T(128)}, f32[16,256,64]{1,2,0:T(8,128)}, f32[16,1024,64]{1,2,0:T(8,128)}, f32[16,1024,64]{1,2,0:T(8,128)}, bf16[16,256,64]{1,2,0:T(8,128)(2...) while((s32[]{:T(128)}, f32[16,256,64]{1,2,0:T(8,128)}, ...), condition=%wide.region_129.129_spmd, body=%wide.region_127.128_spmd.sunk | while | flops 170213120 | bytes 9250929 | solution.py:177
  1421.0 39.9 %reduce-scatter.21.cloned.1.call-done = f32[256,1024]{0,1:T(8,128)} async-done(((f32[1024,1024]{0,1:T(8,128)}), f32[256,1024]{0,1:T(8,128)}) %reduce-scatter.21.cloned.1.call-update) | async-done | bytes 1048592 | tf_op jit(solution)/shard_map/reduce_scatter | solution.py:337
  1460.9 47.1 %reduce-scatter.23.cloned.1.call-done = f32[256,1024]{0,1:T(8,128)} async-done(((f32[1024,1024]{0,1:T(8,128)}), f32[256,1024]{0,1:T(8,128)}) %reduce-scatter.23.cloned.1.call-update) | async-done | bytes 1048592 | tf_op jit(solution)/shard_map/reduce_scatter | solution.py:338
  1508.0 21.0 conditional.26
  1530.4 26.7 %collective-permute-done.3 = bf16[256,1024]{1,0:T(8,128)(2,1)} collective-permute-done((bf16[256,1024]{1,0:T(8,128)(2,1)}, bf16[256,1024]{1,0:T(8,128)(2,1)}, u32[]{:S(2)}, u32[]{:S(2)}) %collective-permute-start.3) | collective-permute-done | bytes 524320 | tf_op jit(solution)/shard_map/ppermute | solution.py:20
  1558.4 66.8 %conditional.27 = (f32[256,1024]{1,0:T(8,128)}, bf16[256,1024]{1,0:T(8,128)(2,1)}, f32[1024,1024]{1,0:T(8,128)}, f32[1024,4096]{1,0:T(8,128)}, f32[4096]{0:T(102...) conditional(s32[]{:T(128)} %convert_element_type.533, ...), branch_computations={%region_142.143_spmd, %region_143.163_spmd} | conditional | flops 9767741440 | bytes 200450880 | solution.py:70
  1625.2 132.5 %conditional.28 = (f32[256,1024]{0,1:T(8,128)}, f32[1024,1024]{0,1:T(8,128)}, f32[1024,1024]{0,1:T(8,128)}) conditional(s32[]{:T(128)} %convert_element_type.533, () %tuple.267, (bf16[2,256,1024]{1,2,0:T(8,128)(2,1)}, s32[]{:T(128)}, bf16[1024,1024]{0,1:T(8,128)(2,1)}, bf16[1024,1024]{0,1:T(8,128)(2,1)}, f32[2,16,256]{2,1,0:T(8,128)S(1)}, ...), branch_computations={%region_163.164_spmd, %region_164.170_spmd} | conditional | flops 170739968 | bytes 11930873 | solution.py:70
  1629.5 128.3 %while.104 = (s32[]{:T(128)}, f32[16,256,64]{1,2,0:T(8,128)}, f32[16,1024,64]{1,2,0:T(8,128)}, f32[16,1024,64]{1,2,0:T(8,128)}, bf16[16,256,64]{1,2,0:T(8,128)(2...) while((s32[]{:T(128)}, f32[16,256,64]{1,2,0:T(8,128)}, ...), condition=%wide.region_169.169_spmd, body=%wide.region_167.168_spmd.sunk | while | flops 170213120 | bytes 9250929 | solution.py:177
  1767.4 20.8 add_convert_fusion.66
  1808.9 38.0 %reduce-scatter.27.cloned.1.call-done = f32[256,1024]{0,1:T(8,128)} async-done(((f32[1024,1024]{0,1:T(8,128)}), f32[256,1024]{0,1:T(8,128)}) %reduce-scatter.27.cloned.1.call-update) | async-done | bytes 1048592 | tf_op jit(solution)/shard_map/reduce_scatter | solution.py:338
  1885.6 70.2 %reduce-scatter.35.cloned.1.call-done = bf16[4096,256]{1,0:T(8,128)(2,1)} async-done(((bf16[4096,1024]{1,0:T(8,128)(2,1)}), bf16[4096,256]{1,0:T(8,128)(2,1)}) %reduce-scatter.35.cloned.1.call-update) | async-done | bytes 2097168 | tf_op jit(solution)/shard_map/reduce_scatter | solution.py:385
  1960.6 70.2 %reduce-scatter.33.cloned.1.call-done = bf16[1024,1024]{1,0:T(8,128)(2,1)} async-done(((bf16[1024,4096]{1,0:T(8,128)(2,1)}), bf16[1024,1024]{1,0:T(8,128)(2,1)}) %reduce-scatter.33.cloned.1.call-update) | async-done | bytes 2097168 | tf_op jit(solution)/shard_map/reduce_scatter | solution.py:379
  2035.8 56.4 %reduce-scatter.29.cloned.1.call-done = bf16[1024,768]{1,0:T(8,128)(2,1)} async-done(((bf16[1024,3072]{1,0:T(8,128)(2,1)}), bf16[1024,768]{1,0:T(8,128)(2,1)}) %reduce-scatter.29.cloned.1.call-update) | async-done | bytes 1572880 | tf_op jit(solution)/shard_map/reduce_scatter | solution.py:373
  2115.5 21.8 reduce-scatter.39.cloned.1.call-done
  2138.3 38.5 %all-reduce.1 = (bf16[2,1024]{1,0:T(2,128)(2,1)S(1)}, bf16[2,4,256]{2,1,0:T(4,128)(2,1)S(1)}, bf16[2,4,256]{2,1,0:T(4,128)(2,1)S(1)}) all-reduce(bf16[2,1024]{1,0:T(2,128)(2,1)S(1)} %multiply_convert_fusion.9, bf16[2,4,256]{2,1,0:T(4,128)(2,1)S(1)} %get-tuple-element.2234, ...), channel_id=1, replica_groups=mesh['wide'=8,'narrow'=4] {'wide'}, use_global_device_ids=true, to_apply=%region_187.188 | all-reduce | flops 6144 | bytes 24576 | tf_op jit(solution)/shard_map/psum | solution.py:397
  2178.6 365.0 %all-reduce.5.cloned.1.call-done = (bf16[2,1024,768]{2,1,0:T(8,128)(2,1)}, bf16[2,1024,256]{2,1,0:T(8,128)(2,1)}, bf16[2,1024,1024]{2,1,0:T(8,128)(2,1)}, bf16[2,4096,256]{2,1,0:T(8,128)(2,1)}) async-done(((bf16[2,1024,768]{2,1,0:T(8,128)(2,1)}, bf16[2,1024,256]{2,1,0:T(8,128)(2,1)}, bf16[2,1024,1024]{2,1,0:T(8,128)(2,1)}, bf16[2,4096,256]{2,1,0:T(8,128)(2,1)}), (bf16[2,1024,768]{2,1,0:T(8,128)(2,1)}, ...) | async-done | bytes 12582928 | tf_op jit(solution)/shard_map/psum | solution.py:397
  (1139 shorter events, 1166.5 us)
Async XLA Ops:
  7.2 52.4 %all-gather.42.cloned.1.call-start = ((), (), s32[]{:S(2)}) async-start(), calls=%async_computation.28 | async-start | bytes 7864320 | tf_op jit(solution)/shard_map/all_gather | solution.py:231
  10.3 77.8 %all-gather.44.cloned.1.call-start = ((), (), s32[]{:S(2)}) async-start(), calls=%async_computation.29 | async-start | bytes 2621440 | tf_op jit(solution)/shard_map/all_gather | solution.py:232
  12.3 97.4 %all-gather.30.cloned.1.call-start = ((), (), s32[]{:S(2)}) async-start(), calls=%async_computation.12 | async-start | bytes 2621440 | tf_op jit(solution)/shard_map/all_gather | solution.py:280
  74.8 59.8 %all-gather.32.cloned.1.call-start = ((), (), s32[]{:S(2)}) async-start(), calls=%async_computation.13 | async-start | bytes 2621440 | tf_op jit(solution)/shard_map/all_gather | solution.py:281
  75.6 119.3 %all-gather.46.cloned.1.call-start = ((), (), s32[]{:S(2)}) async-start(), calls=%async_computation.30 | async-start | bytes 10485760 | tf_op jit(solution)/shard_map/all_gather | solution.py:233
  78.7 177.6 %all-gather.48.cloned.1.call-start = ((), (), s32[]{:S(2)}) async-start(), calls=%async_computation.31 | async-start | bytes 10485760 | tf_op jit(solution)/shard_map/all_gather | solution.py:235
  81.9 360.7 %all-gather.34.cloned.1.call-start = ((), (), s32[]{:S(2)}) async-start(), calls=%async_computation.14 | async-start | bytes 2621440 | tf_op jit(solution)/shard_map/all_gather | solution.py:280
  406.4 61.2 %all-gather.36.cloned.1.call-start = ((), (), s32[]{:S(2)}) async-start(), calls=%async_computation.15 | async-start | bytes 2621440 | tf_op jit(solution)/shard_map/all_gather | solution.py:281
  407.2 311.5 %all-gather.38.cloned.1.call-start = ((), (), s32[]{:S(2)}) async-start(), calls=%async_computation.16 | async-start | bytes 2621440 | tf_op jit(solution)/shard_map/all_gather | solution.py:280
  584.4 16.3 collective-permute-start.1
  608.1 110.6 %all-gather.40.cloned.1.call-start = ((), (), s32[]{:S(2)}) async-start(), calls=%async_computation.17 | async-start | bytes 2621440 | tf_op jit(solution)/shard_map/all_gather | solution.py:281
  627.6 133.4 %all-gather.52.cloned.1.call-start = ((), (), s32[]{:S(2)}) async-start(), calls=%async_computation.33 | async-start | bytes 2621440 | tf_op jit(solution)/shard_map/all_gather | solution.py:331
  684.2 76.8 %all-gather.50.cloned.1.call-start = ((), (), s32[]{:S(2)}) async-start(), calls=%async_computation.32 | async-start | bytes 2621440 | tf_op jit(solution)/shard_map/all_gather | solution.py:330
  708.3 411.4 %reduce-scatter.17.cloned.1.call-start = ((), (), s32[]{:S(2)}) async-start(), calls=%async_computation.18 | async-start | bytes 5242880 | tf_op jit(solution)/shard_map/reduce_scatter | solution.py:337
  767.6 399.1 %reduce-scatter.19.cloned.1.call-start = ((), (), s32[]{:S(2)}) async-start(), calls=%async_computation.19 | async-start | bytes 5242880 | tf_op jit(solution)/shard_map/reduce_scatter | solution.py:338
  768.2 514.2 %all-gather.56.cloned.1.call-start = ((), (), s32[]{:S(2)}) async-start(), calls=%async_computation.35 | async-start | bytes 2621440 | tf_op jit(solution)/shard_map/all_gather | solution.py:331
  768.8 513.6 %all-gather.54.cloned.1.call-start = ((), (), s32[]{:S(2)}) async-start(), calls=%async_computation.34 | async-start | bytes 2621440 | tf_op jit(solution)/shard_map/all_gather | solution.py:330
  769.4 691.6 %reduce-scatter.21.cloned.1.call-start = ((), (), s32[]{:S(2)}) async-start(), calls=%async_computation.20 | async-start | bytes 5242880 | tf_op jit(solution)/shard_map/reduce_scatter | solution.py:337
  1174.6 39.3 %collective-permute-start.2 = (bf16[256,1024]{1,0:T(8,128)(2,1)}, bf16[256,1024]{1,0:T(8,128)(2,1)}, u32[]{:S(2)}, u32[]{:S(2)}) collective-permute-start(bf16[256,1024]{1,0:T(8,128)(2,1)} %get-tuple-element.1405), channel_id=1, source_target_pairs={{16,0},{20,4},{24,8},{28,12},{17,1},{21,5},{25,9},{29,13},{18,2},{... | collective-permute-start | bytes 1572872 | tf_op jit(solution)/shard_map/ppermute | solution.py:20
  1419.0 89.0 %reduce-scatter.23.cloned.1.call-start = ((), (), s32[]{:S(2)}) async-start(), calls=%async_computation.21 | async-start | bytes 5242880 | tf_op jit(solution)/shard_map/reduce_scatter | solution.py:338
  1419.6 205.6 %all-gather.60.cloned.1.call-start = ((), (), s32[]{:S(2)}) async-start(), calls=%async_computation.37 | async-start | bytes 2621440 | tf_op jit(solution)/shard_map/all_gather | solution.py:331
  1420.3 204.9 %all-gather.58.cloned.1.call-start = ((), (), s32[]{:S(2)}) async-start(), calls=%async_computation.36 | async-start | bytes 2621440 | tf_op jit(solution)/shard_map/all_gather | solution.py:330
  1420.9 388.0 %reduce-scatter.25.cloned.1.call-start = ((), (), s32[]{:S(2)}) async-start(), calls=%async_computation.22 | async-start | bytes 5242880 | tf_op jit(solution)/shard_map/reduce_scatter | solution.py:337
  1529.0 28.0 %collective-permute-start.3 = (bf16[256,1024]{1,0:T(8,128)(2,1)}, bf16[256,1024]{1,0:T(8,128)(2,1)}, u32[]{:S(2)}, u32[]{:S(2)}) collective-permute-start(bf16[256,1024]{1,0:T(8,128)(2,1)} %get-tuple-element.1411), channel_id=1, source_target_pairs={{16,0},{20,4},{24,8},{28,12},{17,1},{21,5},{25,9},{29,13},{18,2},{... | collective-permute-start | bytes 1572872 | tf_op jit(solution)/shard_map/ppermute | solution.py:20
  1757.8 89.1 %reduce-scatter.27.cloned.1.call-start = ((), (), s32[]{:S(2)}) async-start(), calls=%async_computation.23 | async-start | bytes 5242880 | tf_op jit(solution)/shard_map/reduce_scatter | solution.py:338
  1758.5 122.4 %reduce-scatter.31.cloned.1.call-start = ((), (), s32[]{:S(2)}) async-start(), calls=%async_computation.25 | async-start | bytes 2621440 | tf_op jit(solution)/shard_map/reduce_scatter | solution.py:376
  1767.3 188.5 %reduce-scatter.35.cloned.1.call-start = ((), (), s32[]{:S(2)}) async-start(), calls=%async_computation.27 | async-start | bytes 10485760 | tf_op jit(solution)/shard_map/reduce_scatter | solution.py:385
  1788.1 242.6 %reduce-scatter.33.cloned.1.call-start = ((), (), s32[]{:S(2)}) async-start(), calls=%async_computation.26 | async-start | bytes 10485760 | tf_op jit(solution)/shard_map/reduce_scatter | solution.py:379
  1808.3 284.0 %reduce-scatter.29.cloned.1.call-start = ((), (), s32[]{:S(2)}) async-start(), calls=%async_computation.24 | async-start | bytes 7864320 | tf_op jit(solution)/shard_map/reduce_scatter | solution.py:373
  1878.9 235.8 %reduce-scatter.37.cloned.1.call-start = ((), (), s32[]{:S(2)}) async-start(), calls=%async_computation.38 | async-start | bytes 327680
  1884.2 253.1 %reduce-scatter.39.cloned.1.call-start = ((), (), s32[]{:S(2)}) async-start(), calls=%async_computation.39 | async-start | bytes 327680
  1885.3 658.3 %all-reduce.5.cloned.1.call-start = ((), (), s32[]{:S(2)}) async-start(), calls=%async_computation.40 | async-start | bytes 25165824 | tf_op jit(solution)/shard_map/psum | solution.py:397
  (129 other events, 1318.6 us)
Sparse Core Ops, SparseCore 0:
  10.5 49.0 all-gather.41
  61.7 22.8 all-gather.43
  86.7 22.9 all-gather.29
  111.7 22.8 all-gather.31
  136.5 58.2 all-gather.45
  196.9 59.3 all-gather.47
  406.5 36.0 all-gather.33
  444.7 22.8 all-gather.35
  608.2 52.9 all-gather.37
  662.6 22.8 all-gather.39
  687.0 46.4 all-gather.51
  734.9 23.9 all-gather.49
  767.7 351.8 reduce-scatter.16
  1122.2 44.4 reduce-scatter.18
  1168.1 22.8 all-gather.55
  1192.4 22.8 all-gather.53
  1419.1 41.7 reduce-scatter.20
  1463.5 44.5 reduce-scatter.22
  1509.6 22.8 all-gather.59
  1533.9 22.8 all-gather.57
  1757.9 41.7 reduce-scatter.24
  1802.4 44.4 reduce-scatter.26
  1849.4 31.4 reduce-scatter.30
  1884.0 71.7 reduce-scatter.34
  1959.0 71.7 reduce-scatter.32
  2033.9 58.3 reduce-scatter.28
  2094.5 20.0 reduce-scatter.36
  2117.2 20.0 reduce-scatter.38
  2142.7 400.8 all-reduce.4
where the time goes:
time: 2580 us; the launch traced here: 2570 us
  waiting for transfers between devices  1440 us (56%)
  matrix products  524 us (20%)
  local copies, waits for them, and re-layouts  260 us (10%)
  other arithmetic  251 us (10%)
  blocking collectives  61.1 us (2%)
    reduce_scatter x3, waiting for transfers between devices, on_device(): lax.psum_scatter(grad_keys_all, 'narrow', scatter_dimension=0, tiled=True)  390 us
    psum x1, waiting for transfers between devices, on_device(): lax.psum(as_sent(padded), 'wide')  365 us
    reduce_scatter x3, waiting for transfers between devices, on_device(): lax.psum_scatter(grad_values_all, 'narrow', scatter_dimension=0, tiled=True)  132 us
    dot_general x64, matrix products, one_head(): jnp.dot(q_head, k_head.T, preferred_element_type=jnp.float32) * HD ** (-0.5)  91.8 us
    ppermute x4, waiting for transfers between devices, from_behind(): return lax.ppermute(block, axis, route)  77.8 us
    reduce_scatter x1, waiting for transfers between devices, on_device(): lax.psum_scatter(summed[4].astype(jnp.bfloat16), 'narrow', scatter_dimens...  70.2 us
    reduce_scatter x1, waiting for transfers between devices, on_device(): lax.psum_scatter(summed[2].astype(jnp.bfloat16), 'narrow', scatter_dimens...  70.2 us
    all_gather x1, waiting for transfers between devices, on_device(): lax.all_gather(mine(w_down), 'narrow', axis=1, tiled=True)  61.4 us
  transfers between devices with their start and end apart: 33, of which 23 were waited for; matrix products, arithmetic and copies ran while one was open for 18% of the time, Pallas kernels for 0%

commit v1 on v0

v1 whole, which is shorter than its diff:
```python
import functools
import math

import jax
import jax.numpy as jnp
from jax import lax
from jax.experimental import pallas as pl
from jax.experimental.pallas import tpu as pltpu
from jax.sharding import PartitionSpec as P

HD = 64
EPSILON = 1e-05
MASKED = -1e30
SCALE = HD ** (-0.5)
F32 = jnp.float32
BF16 = jnp.bfloat16


def layer_norm(values, gain_row, shift_row):
    center = jnp.mean(values, axis=-1, keepdims=True)
    centred = values - center
    spread = jnp.mean(centred * centred, axis=-1, keepdims=True)
    return centred * lax.rsqrt(spread + EPSILON) * gain_row + shift_row


def smooth(values):
    return jax.nn.gelu(values, approximate=False)


def rope_tables(offsets):
    halfway = HD // 2
    ladder = jnp.arange(halfway, dtype=F32) * (2.0 / HD)
    inverse = jnp.exp(-math.log(10000.0) * ladder)
    angles = offsets.astype(F32)[:, None] * inverse[None, :]
    return jnp.cos(angles), jnp.sin(angles)


def rotate(matrix, cosine, sine):
    rows, width = matrix.shape
    field = matrix.reshape(rows, width // HD, 2, HD // 2)
    first, second = field[:, :, 0], field[:, :, 1]
    cosine, sine = cosine[:, None], sine[:, None]
    turned = jnp.stack([first * cosine - second * sine, second * cosine + first * sine], axis=2)
    return turned.reshape(rows, width)


def dot(left, right):
    return jnp.dot(left, right, preferred_element_type=F32)


def dot_t(left, right):
    return lax.dot_general(left, right, (((1,), (1,)), ((), ())), preferred_element_type=F32)


def t_dot(left, right):
    return lax.dot_general(left, right, (((0,), (0,)), ((), ())), preferred_element_type=F32)


BLOCK = 256


def attend_kernel(q_ref, k_ref, v_ref, start_ref, o_ref, lse_ref):
    length = q_ref.shape[0]
    for at in range(length // BLOCK):
        rows = slice(at * BLOCK, (at + 1) * BLOCK)
        reach = (at + 1) * BLOCK
        key = lax.broadcasted_iota(jnp.int32, (BLOCK, reach), 1)
        query = lax.broadcasted_iota(jnp.int32, (BLOCK, reach), 0) + at * BLOCK
        allowed = (key >= start_ref[rows, :]) & (key <= query)
        mixed, logs = [], []
        for head in range(q_ref.shape[1] // HD):
            lanes = slice(head * HD, (head + 1) * HD)
            scores = dot_t(q_ref[rows, lanes] * SCALE, k_ref[:reach, lanes])
            scores = jnp.where(allowed, scores, MASKED)
            summit = jnp.max(scores, axis=1, keepdims=True)
            weights = jnp.exp(scores - summit)
            total = jnp.sum(weights, axis=1, keepdims=True)
            chances = (weights * (1.0 / total)).astype(BF16)
            mixed.append(dot(chances, v_ref[:reach, lanes]))
            logs.append(summit + jnp.log(total))
        o_ref[rows, :] = jnp.concatenate(mixed, axis=1).astype(BF16)
        lse_ref[0, rows, :] = jnp.concatenate(logs, axis=1)


def attend(query, keys, values, start):
    length, width = query.shape
    pairs = width // 128
    block = pl.BlockSpec((length, 128), lambda i: (0, i))
    return pl.pallas_call(
        attend_kernel,
        grid=(pairs,),
        in_specs=[block, block, block, pl.BlockSpec((length, 1), lambda i: (0, 0))],
        out_specs=[block, pl.BlockSpec((1, length, 2), lambda i: (i, 0, 0))],
        out_shape=[
            jax.ShapeDtypeStruct((length, width), BF16),
            jax.ShapeDtypeStruct((pairs, length, 2), F32),
        ],
        compiler_params=pltpu.CompilerParams(vmem_limit_bytes=48 * 2**20),
        cost_estimate=pl.CostEstimate(
            flops=4 * length * length * width, bytes_accessed=8 * length * width,
            transcendentals=length * length * width // HD,
        ),
        name="attend",
    )(query, keys, values, start)


def attend_back_kernel(
    q_ref, k_ref, v_ref, g_ref, start_ref, lse_ref, inner_ref, dq_ref, dk_ref, dv_ref
):
    length = q_ref.shape[0]
    dk_ref[...] = jnp.zeros_like(dk_ref)
    dv_ref[...] = jnp.zeros_like(dv_ref)
    for at in range(length // BLOCK):
        rows = slice(at * BLOCK, (at + 1) * BLOCK)
        reach = (at + 1) * BLOCK
        key = lax.broadcasted_iota(jnp.int32, (reach, BLOCK), 0)
        query = lax.broadcasted_iota(jnp.int32, (reach, BLOCK), 1) + at * BLOCK
        allowed = (key >= start_ref[:, rows]) & (key <= query)
        dqs, dks, dvs = [], [], []
        for head in range(q_ref.shape[1] // HD):
            lanes = slice(head * HD, (head + 1) * HD)
            k_head, g_head = k_ref[:reach, lanes], g_ref[rows, lanes]
            q_head = q_ref[rows, lanes] * SCALE
            scores = dot_t(k_head, q_head) - lse_ref[0, head : head + 1, rows]
            chances = jnp.exp(jnp.where(allowed, scores, MASKED))
            grad_prob = dot_t(v_ref[:reach, lanes], g_head)
            grad_score = chances * (grad_prob - inner_ref[0, head : head + 1, rows])
            grad_score = grad_score.astype(BF16)
            dvs.append(dot(chances.astype(BF16), g_head))
            dks.append(dot(grad_score, q_head))
            dqs.append(t_dot(grad_score, k_head) * SCALE)
        dq_ref[rows, :] = jnp.concatenate(dqs, axis=1)
        dk_ref[:reach, :] += jnp.concatenate(dks, axis=1)
        dv_ref[:reach, :] += jnp.concatenate(dvs, axis=1)


def attend_back(query, keys, values, grad, start, logs, inner):
    length, width = query.shape
    pairs = width // 128
    block = pl.BlockSpec((length, 128), lambda i: (0, i))
    line = pl.BlockSpec((1, 2, length), lambda i: (i, 0, 0))
    return pl.pallas_call(
        attend_back_kernel,
        grid=(pairs,),
        in_specs=[block] * 4 + [pl.BlockSpec((1, length), lambda i: (0, 0)), line, line],
        out_specs=[block] * 3,
        out_shape=[jax.ShapeDtypeStruct((length, width), F32)] * 3,
        compiler_params=pltpu.CompilerParams(vmem_limit_bytes=48 * 2**20),
        cost_estimate=pl.CostEstimate(
            flops=10 * length * length * width, bytes_accessed=20 * length * width,
            transcendentals=length * length * width // HD,
        ),
        name="attend_back",
    )(query, keys, values, grad, start, logs, inner)


def swap(block, distance):
    count = lax.axis_size("narrow")
    return lax.ppermute(block, "narrow", [(i, i ^ distance) for i in range(count)])


def pick(stack, table, at):
    return lax.dynamic_index_in_dim(stack, jnp.asarray(table)[at], 0, keepdims=False)


def by_heads(block, at):
    parts = jnp.stack(jnp.split(block, 3, axis=1))
    own = pick(parts, [0, 2, 0, 2], at)
    near = swap(parts[1], 1)
    far = swap(pick(parts, [2, 0, 2, 0], at), 2)
    parts = jnp.stack([own, near, far])
    order = jnp.asarray([[0, 1, 2], [1, 0, 2], [2, 0, 1], [2, 1, 0]])[at]
    return jnp.concatenate(
        [lax.dynamic_index_in_dim(parts, order[i], 0, keepdims=False) for i in range(3)], axis=1
    )


def from_heads(block, at):
    parts = jnp.stack(jnp.split(block, 3, axis=1))
    own = pick(parts, [0, 1, 1, 2], at)
    near = swap(pick(parts, [1, 0, 2, 1], at), 1)
    far = swap(pick(parts, [2, 2, 0, 0], at), 2)
    parts = jnp.stack([own, near, far])
    order = jnp.asarray([[0, 1, 2], [2, 1, 0], [0, 1, 2], [2, 1, 0]])[at]
    return jnp.concatenate(
        [lax.dynamic_index_in_dim(parts, order[i], 0, keepdims=False) for i in range(3)], axis=1
    )


def to_rows(block):
    return lax.all_to_all(block, "narrow", split_axis=0, concat_axis=1, tiled=True)


def to_columns(block):
    return lax.all_to_all(block, "narrow", split_axis=1, concat_axis=0, tiled=True)


def gather(block):
    return lax.all_gather(block, "narrow", axis=0, tiled=True)


def scatter(block):
    return lax.psum_scatter(
        block.astype(BF16), "narrow", scatter_dimension=0, tiled=True
    ).astype(F32)


def layer_forward(resid, weights, start, tables):
    w_qkv, w_out, w_up, b_up, w_down, gains, shifts = weights
    normed = gather(layer_norm(resid, gains[0], shifts[0]).astype(BF16))
    query, keys, values = jnp.split(dot(normed, w_qkv), 3, axis=1)
    query = rotate(query, *tables).astype(BF16)
    keys = rotate(keys, *tables).astype(BF16)
    values = values.astype(BF16)
    mixture, logs = attend(query, keys, values, start[:, None])
    branch = scatter(dot(mixture, w_out))
    middle = resid + layer_norm(branch, gains[1], shifts[1])
    inner = gather(layer_norm(middle, gains[2], shifts[2]).astype(BF16))
    hidden = dot(inner, w_up) + b_up
    second = scatter(dot(smooth(hidden).astype(BF16), w_down))
    result = middle + layer_norm(second, gains[3], shifts[3])
    return result, (resid, normed, query, keys, values, mixture, logs, branch, middle, inner, hidden, second)


def layer_backward(grad, saved, weights, start, tables):
    w_qkv, w_out, w_up, b_up, w_down, gains, shifts = weights
    resid, normed, query, keys, values, mixture, logs, branch, middle, inner, hidden, second = saved
    grad_second, gain_3, shift_3 = jax.vjp(layer_norm, second, gains[3], shifts[3])[1](grad)
    grad_second = gather(grad_second.astype(BF16))
    grad_down = t_dot(smooth(hidden).astype(BF16), grad_second)
    grad_hidden = jax.vjp(smooth, hidden)[1](dot_t(grad_second, w_down))[0].astype(BF16)
    grad_b_up = jnp.sum(grad_hidden.astype(F32), axis=0)
    grad_up = t_dot(inner, grad_hidden)
    grad_inner = scatter(dot_t(grad_hidden, w_up))
    grad_middle, gain_2, shift_2 = jax.vjp(layer_norm, middle, gains[2], shifts[2])[1](grad_inner)
    grad_middle = grad + grad_middle
    grad_branch, gain_1, shift_1 = jax.vjp(layer_norm, branch, gains[1], shifts[1])[1](grad_middle)
    grad_branch = gather(grad_branch.astype(BF16))
    grad_out = t_dot(mixture, grad_branch)
    grad_mixture = dot_t(grad_branch, w_out).astype(BF16)
    length = grad_mixture.shape[0]
    inner_sums = jnp.sum(
        (grad_mixture.astype(F32) * mixture.astype(F32)).reshape(length, -1, 2, HD), axis=-1
    ).transpose(1, 2, 0)
    dq, dk, dv = attend_back(
        query, keys, values, grad_mixture, start[None], logs.transpose(0, 2, 1), inner_sums
    )
    cosine, sine = tables
    grad_projected = jnp.concatenate(
        [rotate(dq, cosine, -sine), rotate(dk, cosine, -sine), dv], axis=1
    ).astype(BF16)
    grad_qkv = t_dot(normed, grad_projected)
    grad_normed = scatter(dot_t(grad_projected, w_qkv))
    grad_resid, gain_0, shift_0 = jax.vjp(layer_norm, resid, gains[0], shifts[0])[1](grad_normed)
    grads = (
        grad_qkv,
        grad_out,
        grad_up,
        grad_b_up,
        grad_down,
        jnp.stack([gain_0, gain_1, gain_2, gain_3]),
        jnp.stack([shift_0, shift_1, shift_2, shift_3]),
    )
    return grad_middle + grad_resid, grads


def reduce_grads(grads, at):
    def fold(block):
        return lax.psum_scatter(block.astype(BF16), "wide", scatter_dimension=0, tiled=True)

    def spread(block):
        return lax.all_gather(block, "wide", axis=0, tiled=True)

    def spread_rows(block):
        wide, narrow = lax.axis_size("wide"), lax.axis_size("narrow")
        rows, width = block.shape
        full = spread(block).reshape(wide, narrow, rows // narrow, width)
        return full.transpose(1, 0, 2, 3).reshape(wide * rows, width)

    qkv, out, up, b_up, down, gains, shifts = grads
    qkv = spread(from_heads(fold(qkv), at))
    out = spread_rows(to_columns(fold(out)))
    up = spread(fold(up))
    down = spread_rows(to_columns(fold(down)))
    b_up = lax.psum(b_up, "wide")
    norms = lax.psum(jnp.concatenate([gains, shifts]), ("wide", "narrow"))
    part = norms.shape[1] // lax.axis_size("narrow")
    norms = lax.dynamic_slice_in_dim(norms, at * part, part, 1)
    return qkv, out, up, b_up, down, norms[:4], norms[4:]


def on_device(ends, lengths, w_qkv, w_out, w_up, b_up, w_down, norm_gain, norm_bias):
    wide = lax.axis_size("wide")
    narrow = lax.axis_size("narrow")
    halfway = wide // 2
    flip = wide - 2
    wide_at = lax.axis_index("wide")
    at = lax.axis_index("narrow")
    first = wide_at < halfway
    row_count = ends.shape[0] // 2
    width = ends.shape[1]
    length = row_count * narrow
    blocks = ends.reshape(2, row_count, width)

    def route(block, pairs):
        return lax.ppermute(block, "wide", pairs)

    groups = range(halfway)
    x_came = route(blocks[1], [(g, g ^ flip) for g in groups])
    dy_first = route(blocks[0], [(g + halfway, g) for g in groups])
    dy_second = route(blocks[1], [(g + halfway, g ^ flip) for g in groups])
    resid = jnp.where(first, blocks[0], x_came).astype(F32)
    upstream = jnp.where(first, dy_first, dy_second).astype(F32)
    group_at = jnp.where(first, wide_at, wide_at ^ flip)
    micro_at = jnp.where(first, 0, 1)

    own_lengths = lengths[group_at, micro_at]
    places = jnp.arange(length, dtype=jnp.int32)
    passed = (places[:, None] >= jnp.cumsum(own_lengths)[None, :]).astype(jnp.int32)
    start = jnp.sum(passed * own_lengths[None, :], axis=1)
    tables = rope_tables(places - start)

    def weights_of(layer):
        return (
            by_heads(w_qkv[layer], at),
            to_rows(w_out[layer]),
            w_up[layer],
            b_up[layer].astype(F32),
            to_rows(w_down[layer]),
            lax.all_gather(norm_gain[layer], "narrow", axis=1, tiled=True).astype(F32),
            lax.all_gather(norm_bias[layer], "narrow", axis=1, tiled=True).astype(F32),
        )

    weights = [weights_of(layer) for layer in range(2)]
    middle, saved_first = layer_forward(resid, weights[0], start, tables)
    middle = middle.astype(BF16).astype(F32)
    result, saved_second = layer_forward(middle, weights[1], start, tables)
    result = result.astype(BF16)
    grad, grads_second = layer_backward(upstream, saved_second, weights[1], start, tables)
    totals_second = reduce_grads(grads_second, at)
    grad = grad.astype(BF16).astype(F32)
    grad, grads_first = layer_backward(grad, saved_first, weights[0], start, tables)
    totals_first = reduce_grads(grads_first, at)
    grad = grad.astype(BF16)

    grad_came = route(grad, [(g ^ flip, g) for g in groups])
    result_first = route(result, [(g, g + halfway) for g in groups])
    result_second = route(result, [(g ^ flip, g + halfway) for g in groups])
    ends_out = jnp.where(
        first,
        jnp.concatenate([grad, grad_came]),
        jnp.concatenate([result_first, result_second]),
    )
    totals = [jnp.stack([a.astype(F32), b.astype(F32)]) for a, b in zip(totals_first, totals_second)]
    return (ends_out,) + tuple(totals)


def solution(mesh):
    placed = (
        P(("wide", "narrow"), None),
        P(),
        P(None, None, "narrow"),
        P(None, None, "narrow"),
        P(None, None, "narrow"),
        P(None, "narrow"),
        P(None, None, "narrow"),
        P(None, None, "narrow"),
        P(None, None, "narrow"),
    )
    return jax.shard_map(
        on_device,
        mesh=mesh,
        in_specs=placed,
        out_specs=(P(("wide", "narrow"), None),) + placed[2:],
        check_vma=False,
    )
```

time: 2580 us -> 1760 us (0.68)
  matrix products: 524 us -> 127 us
  waiting for transfers between devices: 1440 us -> 1120 us
  local copies, waits for them, and re-layouts: 260 us -> 92.1 us
  other arithmetic: 251 us -> 93.9 us
  blocking collectives: 61.1 us -> 196 us
  Pallas kernels: 0 us -> 37.7 us
  starting transfers between devices: 11.4 us -> 43.5 us
    dot_general x248 -> x24, matrix products: 524 us -> 127 us  [the longest x8 48.9 us: dot(): return jnp.dot(left, right, preferred_element_type=F32)]
    psum x1, waiting for transfers between devices: 365 us -> 80.5 us  [reduce_grads(): norms = lax.psum(jnp.concatenate([gains, shifts]), ('wide', 'narrow'))]
    convert_element_type x84 -> x10, other arithmetic: 121 us -> 9.98 us  [the longest x2 3.2 us: layer_forward(): inner = gather(layer_norm(middle, gains[2], shifts[2]).astype(BF16))]
    all_to_all x0 -> x4, blocking collectives: none -> 90.6 us  [the longest x2 72.3 us: to_rows(): lax.all_to_all(block, 'narrow', split_axis=0, concat_axis=1, tiled=True)]
    all_gather x3 -> x6, blocking collectives: 16.7 us -> 84.6 us  [the longest x2 63.8 us: spread(): return lax.all_gather(block, 'wide', axis=0, tiled=True)]
    ppermute x4 -> x14, waiting for transfers between devices: 77.8 us -> 10.9 us  [the longest x8 10.9 us: swap(): lax.ppermute(block, 'narrow', [(i, i ^ distance) for i in range(count)])]
    dynamic_update_slice x47 -> x0, local copies, waits for them, and re-layouts: 61.6 us -> none  [the longest x32 42 us: attend_forward(): lax.map(one_head, (by_heads(query), by_heads(keys_all), by_heads(values_a...]
    dynamic_slice x76 -> x11, local copies, waits for them, and re-layouts: 62.3 us -> 5.47 us  [the longest x5 2.94 us: pick(): jnp.asarray(table)[at]]
  transfers between devices with their start and end apart: 33 -> 49, of which waited for: 23 -> 29; matrix products, arithmetic and copies ran while one was open for 18% -> 8% of each run, Pallas kernels for 0% -> 1%
where the time goes in v1:
time: 1760 us; the launch traced here: 1750 us
  waiting for transfers between devices  1120 us (64%)
  blocking collectives  196 us (11%)
  matrix products  127 us (7%)
  other arithmetic  93.9 us (5%)
  local copies, waits for them, and re-layouts  92.1 us (5%)
  starting transfers between devices  43.5 us (2%)
  between operations  37.8 us (2%)
  Pallas kernels  37.7 us (2%)
    reduce_scatter x8, waiting for transfers between devices, fold(): lax.psum_scatter(block.astype(BF16), 'wide', scatter_dimension=0, tiled=T...  464 us
    reduce_scatter x8, waiting for transfers between devices, scatter(): lax.psum_scatter(block.astype(BF16), 'narrow', scatter_dimension=0, tiled...  233 us
    all_gather x6, waiting for transfers between devices, spread(): return lax.all_gather(block, 'wide', axis=0, tiled=True)  226 us
    psum x1, waiting for transfers between devices, reduce_grads(): norms = lax.psum(jnp.concatenate([gains, shifts]), ('wide', 'narrow'))  80.5 us
    all_to_all x2, blocking collectives, to_rows(): lax.all_to_all(block, 'narrow', split_axis=0, concat_axis=1, tiled=True)  72.3 us
    all_gather x8, waiting for transfers between devices, gather(): return lax.all_gather(block, 'narrow', axis=0, tiled=True)  69.2 us
    all_gather x2, blocking collectives, spread(): return lax.all_gather(block, 'wide', axis=0, tiled=True)  63.8 us
    dot_general x8, matrix products, dot(): return jnp.dot(left, right, preferred_element_type=F32)  48.9 us
  transfers between devices with their start and end apart: 49, of which 29 were waited for; matrix products, arithmetic and copies ran while one was open for 8% of the time, Pallas kernels for 1%

profile of v1, /device:TPU:0, one launch (start us, length us, event | category | flops | bytes accessed | tf_op | source)
XLA Modules:
  0.0 1749.7 jit_solution(7247461619152233390)
XLA Ops:
  94.8 37.3 %reduce-scatter.17.cloned.1.call-done = bf16[256,1024]{1,0:T(8,128)(2,1)} async-done(((bf16[1024,1024]{1,0:T(8,128)(2,1)}), bf16[256,1024]{1,0:T(8,128)(2,1)}) %reduce-scatter.17.cloned.1.call-update) | async-done | bytes 524304 | tf_op jit(solution)/shard_map/reduce_scatter | solution.py:203
  149.0 34.7 %all-to-all-done.1 = bf16[4,1024,256]{2,1,0:T(8,128)(2,1)} async-done(((bf16[4,1024,256]{2,1,0:T(8,128)(2,1)}), bf16[4,1024,256]{2,1,0:T(8,128)(2,1)}, u32[]{:S(2)}, u32[]{:S(2)}) %all-to-all-start.1) | async-done | bytes 2097184 | tf_op jit(solution)/shard_map/all_to_all | solution.py:191
  187.7 15.0 multiply_convert_fusion.1
  218.5 21.0 %reduce-scatter.19.cloned.1.call-done = bf16[256,1024]{1,0:T(8,128)(2,1)} async-done(((bf16[1024,1024]{1,0:T(8,128)(2,1)}), bf16[256,1024]{1,0:T(8,128)(2,1)}) %reduce-scatter.19.cloned.1.call-update) | async-done | bytes 524304 | tf_op jit(solution)/shard_map/reduce_scatter | solution.py:203
  248.9 30.9 %all_to_all.152 = bf16[4,256,256]{2,1,0:T(8,128)(2,1)S(1)} all-to-all(bf16[4,256,256]{2,1,0:T(8,128)(2,1)S(1)} %bitcast.310), channel_id=1, replica_groups=mesh['wide'=8,'narrow'=4] {'narrow'}, dimensions={0} | all-to-all | bytes 1048576 | tf_op jit(solution)/shard_map/all_to_all | solution.py:191
  309.6 31.1 %reduce-scatter.21.cloned.1.call-done = bf16[256,1024]{1,0:T(8,128)(2,1)} async-done(((bf16[1024,1024]{1,0:T(8,128)(2,1)}), bf16[256,1024]{1,0:T(8,128)(2,1)}) %reduce-scatter.21.cloned.1.call-update) | async-done | bytes 524304 | tf_op jit(solution)/shard_map/reduce_scatter | solution.py:203
  348.1 41.4 %all_to_all.153 = bf16[4,1024,256]{2,1,0:T(8,128)(2,1)} all-to-all(bf16[4,1024,256]{2,1,0:T(8,128)(2,1)} %bitcast.277), channel_id=1, replica_groups=mesh['wide'=8,'narrow'=4] {'narrow'}, dimensions={0} | all-to-all | bytes 4194304 | tf_op jit(solution)/shard_map/all_to_all | solution.py:191
  416.4 28.8 %reduce-scatter.23.cloned.1.call-done = bf16[256,1024]{1,0:T(8,128)(2,1)} async-done(((bf16[1024,1024]{1,0:T(8,128)(2,1)}), bf16[256,1024]{1,0:T(8,128)(2,1)}) %reduce-scatter.23.cloned.1.call-update) | async-done | bytes 524304 | tf_op jit(solution)/shard_map/reduce_scatter | solution.py:203
  451.5 22.5 %all-gather.27.cloned.1.call-done = bf16[1024,1024]{1,0:T(8,128)(2,1)} async-done(((bf16[256,1024]{1,0:T(8,128)(2,1)}), bf16[1024,1024]{1,0:T(8,128)(2,1)}) %all-gather.27.cloned.1.call-update) | async-done | bytes 2097168 | tf_op jit(solution)/shard_map/all_gather | solution.py:199
  487.5 31.6 %reduce-scatter.25.cloned.1.call-done = bf16[256,1024]{1,0:T(8,128)(2,1)} async-done(((bf16[1024,1024]{1,0:T(8,128)(2,1)}), bf16[256,1024]{1,0:T(8,128)(2,1)}) %reduce-scatter.25.cloned.1.call-update) | async-done | bytes 524304 | tf_op jit(solution)/shard_map/reduce_scatter | solution.py:203
  528.1 22.2 %all-gather.29.cloned.1.call-done = bf16[1024,1024]{1,0:T(8,128)(2,1)} async-done(((bf16[256,1024]{1,0:T(8,128)(2,1)}), bf16[1024,1024]{1,0:T(8,128)(2,1)}) %all-gather.29.cloned.1.call-update) | async-done | bytes 2097168 | tf_op jit(solution)/shard_map/all_gather | solution.py:199
  582.5 31.5 %reduce-scatter.27.cloned.1.call-done = bf16[256,1024]{1,0:T(8,128)(2,1)} async-done(((bf16[1024,1024]{1,0:T(8,128)(2,1)}), bf16[256,1024]{1,0:T(8,128)(2,1)}) %reduce-scatter.27.cloned.1.call-update) | async-done | bytes 524304 | tf_op jit(solution)/shard_map/reduce_scatter | solution.py:203
  621.5 22.3 %all-gather.31.cloned.1.call-done = bf16[1024,1024]{1,0:T(8,128)(2,1)} async-done(((bf16[256,1024]{1,0:T(8,128)(2,1)}), bf16[1024,1024]{1,0:T(8,128)(2,1)}) %all-gather.31.cloned.1.call-update) | async-done | bytes 2097168 | tf_op jit(solution)/shard_map/all_gather | solution.py:199
  657.4 31.5 %reduce-scatter.29.cloned.1.call-done = bf16[256,1024]{1,0:T(8,128)(2,1)} async-done(((bf16[1024,1024]{1,0:T(8,128)(2,1)}), bf16[256,1024]{1,0:T(8,128)(2,1)}) %reduce-scatter.29.cloned.1.call-update) | async-done | bytes 524304 | tf_op jit(solution)/shard_map/reduce_scatter | solution.py:203
  761.9 28.1 %reduce-scatter.47.cloned.1.call-done = bf16[128,1024]{1,0:T(8,128)(2,1)} async-done(((bf16[1024,1024]{1,0:T(8,128)(2,1)}), bf16[128,1024]{1,0:T(8,128)(2,1)}) %reduce-scatter.47.cloned.1.call-update) | async-done | bytes 262160 | tf_op jit(solution)/shard_map/reduce_scatter | solution.py:269
  803.6 57.5 %reduce-scatter.43.cloned.1.call-done = bf16[128,1024]{1,0:T(8,128)(2,1)} async-done(((bf16[1024,1024]{1,0:T(8,128)(2,1)}), bf16[128,1024]{1,0:T(8,128)(2,1)}) %reduce-scatter.43.cloned.1.call-update) | async-done | bytes 262160 | tf_op jit(solution)/shard_map/reduce_scatter | solution.py:269
  861.2 71.2 %reduce-scatter.41.cloned.1.call-done = bf16[128,1024]{1,0:T(8,128)(2,1)} async-done(((bf16[1024,1024]{1,0:T(8,128)(2,1)}), bf16[128,1024]{1,0:T(8,128)(2,1)}) %reduce-scatter.41.cloned.1.call-update) | async-done | bytes 262160 | tf_op jit(solution)/shard_map/reduce_scatter | solution.py:269
  932.4 71.4 %reduce-scatter.45.cloned.1.call-done = bf16[128,1024]{1,0:T(8,128)(2,1)} async-done(((bf16[1024,1024]{1,0:T(8,128)(2,1)}), bf16[128,1024]{1,0:T(8,128)(2,1)}) %reduce-scatter.45.cloned.1.call-update) | async-done | bytes 262160 | tf_op jit(solution)/shard_map/reduce_scatter | solution.py:269
  1021.9 49.5 %reduce-scatter.35.cloned.1.call-done = bf16[128,768]{1,0:T(8,128)(2,1)} async-done(((bf16[1024,768]{1,0:T(8,128)(2,1)}), bf16[128,768]{1,0:T(8,128)(2,1)}) %reduce-scatter.35.cloned.1.call-update) | async-done | bytes 196624 | tf_op jit(solution)/shard_map/reduce_scatter | solution.py:269
  1084.3 20.5 %reduce-scatter.31.cloned.1.call-done = bf16[256,1024]{1,0:T(8,128)(2,1)} async-done(((bf16[1024,1024]{1,0:T(8,128)(2,1)}), bf16[256,1024]{1,0:T(8,128)(2,1)}) %reduce-scatter.31.cloned.1.call-update) | async-done | bytes 524304 | tf_op jit(solution)/shard_map/reduce_scatter | solution.py:203
  1109.4 64.0 %reduce-scatter.33.cloned.1.call-done = bf16[128,768]{1,0:T(8,128)(2,1)} async-done(((bf16[1024,768]{1,0:T(8,128)(2,1)}), bf16[128,768]{1,0:T(8,128)(2,1)}) %reduce-scatter.33.cloned.1.call-update) | async-done | bytes 196624 | tf_op jit(solution)/shard_map/reduce_scatter | solution.py:269
  1183.3 52.2 %all-gather.45.cloned.1.call-done = bf16[4096,256]{1,0:T(8,128)(2,1)} async-done(((bf16[512,256]{1,0:T(8,128)(2,1)}), bf16[4096,256]{1,0:T(8,128)(2,1)}) %all-gather.45.cloned.1.call-update) | async-done | bytes 2097168 | tf_op jit(solution)/shard_map/all_gather | solution.py:272
  1238.7 60.4 %reduce-scatter.39.cloned.1.call-done = bf16[32,1024]{1,0:T(8,128)(2,1)} async-done(((bf16[256,1024]{1,0:T(8,128)(2,1)}), bf16[32,1024]{1,0:T(8,128)(2,1)}) %reduce-scatter.39.cloned.1.call-update) | async-done | bytes 65552 | tf_op jit(solution)/shard_map/reduce_scatter | solution.py:269
  1308.0 32.2 %all_gather.75 = bf16[1024,256]{1,0:T(8,128)(2,1)S(1)} all-gather(bf16[128,256]{1,0:T(8,128)(2,1)S(1)} %bitcast.347), channel_id=1, replica_groups=mesh['wide'=8,'narrow'=4] {'wide'}, dimensions={0}, use_global_device_ids=true | all-gather | bytes 589824 | tf_op jit(solution)/shard_map/all_gather | solution.py:272
  1340.2 20.4 %all-reduce.1 = (f32[1,1024]{1,0:T(1,128)S(1)}, f32[1,1024]{1,0:T(1,128)S(1)}) all-reduce(f32[1,1024]{1,0:T(1,128)S(1)} %bitcast.409, f32[1,1024]{1,0:T(1,128)S(1)} %bitcast.410), channel_id=1, replica_groups=mesh['wide'=8,'narrow'=4] {'wide'}, use_global_device_ids=true, to_apply=%region_53.54 | all-reduce | flops 2048 | bytes 16384 | tf_op jit(solution)/shard_map/psum | solution.py:285
  1361.2 42.4 %all-gather.39.cloned.1.call-done = bf16[1024,1024]{1,0:T(8,128)(2,1)} async-done(((bf16[128,1024]{1,0:T(8,128)(2,1)}), bf16[1024,1024]{1,0:T(8,128)(2,1)}) %all-gather.39.cloned.1.call-update) | async-done | bytes 2097168 | tf_op jit(solution)/shard_map/all_gather | solution.py:272
  1409.8 43.8 %all-gather.43.cloned.1.call-done = bf16[4096,256]{1,0:T(8,128)(2,1)} async-done(((bf16[512,256]{1,0:T(8,128)(2,1)}), bf16[4096,256]{1,0:T(8,128)(2,1)}) %all-gather.43.cloned.1.call-update) | async-done | bytes 2097168 | tf_op jit(solution)/shard_map/all_gather | solution.py:272
  1456.7 61.5 %reduce-scatter.37.cloned.1.call-done = bf16[32,1024]{1,0:T(8,128)(2,1)} async-done(((bf16[256,1024]{1,0:T(8,128)(2,1)}), bf16[32,1024]{1,0:T(8,128)(2,1)}) %reduce-scatter.37.cloned.1.call-update) | async-done | bytes 65552 | tf_op jit(solution)/shard_map/reduce_scatter | solution.py:269
  1529.3 31.6 %all_gather.74 = bf16[1024,256]{1,0:T(8,128)(2,1)S(1)} all-gather(bf16[128,256]{1,0:T(8,128)(2,1)S(1)} %bitcast.348), channel_id=1, replica_groups=mesh['wide'=8,'narrow'=4] {'wide'}, dimensions={0}, use_global_device_ids=true | all-gather | bytes 589824 | tf_op jit(solution)/shard_map/all_gather | solution.py:272
  1564.2 80.5 %all-reduce.4.cloned.1.call-done = (f32[8,1024]{1,0:T(8,128)}, f32[8,1024]{1,0:T(8,128)}) async-done(((f32[8,1024]{1,0:T(8,128)}, f32[8,1024]{1,0:T(8,128)}), (f32[8,1024]{1,0:T(8,128)}, f32[8,1024]{1,0:T(8,128)})) %all-reduce.4.cloned.1.call-update) | async-done | bytes 65552 | tf_op jit(solution)/shard_map/psum | solution.py:286
  1650.3 41.9 %all-gather.37.cloned.1.call-done = bf16[1024,768]{1,0:T(8,128)(2,1)} async-done(((bf16[128,768]{1,0:T(8,128)(2,1)}), bf16[1024,768]{1,0:T(8,128)(2,1)}) %all-gather.37.cloned.1.call-update) | async-done | bytes 1572880 | tf_op jit(solution)/shard_map/all_gather | solution.py:272
  1692.2 45.2 %all-gather.35.cloned.1.call-done = bf16[1024,768]{1,0:T(8,128)(2,1)} async-done(((bf16[128,768]{1,0:T(8,128)(2,1)}), bf16[1024,768]{1,0:T(8,128)(2,1)}) %all-gather.35.cloned.1.call-update) | async-done | bytes 1572880 | tf_op jit(solution)/shard_map/all_gather | solution.py:272
  (503 shorter events, 435.5 us)
Async XLA Ops:
  38.7 93.4 %reduce-scatter.17.cloned.1.call-start = ((), (), s32[]{:S(2)}) async-start(), calls=%async_computation.25 | async-start | bytes 2621440 | tf_op jit(solution)/shard_map/reduce_scatter | solution.py:203
  94.6 93.1 %all-gather.21.cloned.1.call-start = ((), (), s32[]{:S(2)}) async-start(), calls=%async_computation.26 | async-start | bytes 2621440 | tf_op jit(solution)/shard_map/all_gather | solution.py:199
  149.0 90.5 %reduce-scatter.19.cloned.1.call-start = ((), (), s32[]{:S(2)}) async-start(), calls=%async_computation.27 | async-start | bytes 2621440 | tf_op jit(solution)/shard_map/reduce_scatter | solution.py:203
  207.8 76.5 %all-gather.23.cloned.1.call-start = ((), (), s32[]{:S(2)}) async-start(), calls=%async_computation.28 | async-start | bytes 2621440 | tf_op jit(solution)/shard_map/all_gather | solution.py:199
  245.1 95.6 %reduce-scatter.21.cloned.1.call-start = ((), (), s32[]{:S(2)}) async-start(), calls=%async_computation.29 | async-start | bytes 2621440 | tf_op jit(solution)/shard_map/reduce_scatter | solution.py:203
  309.1 84.3 %all-gather.25.cloned.1.call-start = ((), (), s32[]{:S(2)}) async-start(), calls=%async_computation.30 | async-start | bytes 2621440 | tf_op jit(solution)/shard_map/all_gather | solution.py:199
  348.0 97.1 %reduce-scatter.23.cloned.1.call-start = ((), (), s32[]{:S(2)}) async-start(), calls=%async_computation.31 | async-start | bytes 2621440 | tf_op jit(solution)/shard_map/reduce_scatter | solution.py:203
  451.2 67.8 %reduce-scatter.25.cloned.1.call-start = ((), (), s32[]{:S(2)}) async-start(), calls=%async_computation.33 | async-start | bytes 2621440 | tf_op jit(solution)/shard_map/reduce_scatter | solution.py:203
  527.5 86.5 %reduce-scatter.27.cloned.1.call-start = ((), (), s32[]{:S(2)}) async-start(), calls=%async_computation.35 | async-start | bytes 2621440 | tf_op jit(solution)/shard_map/reduce_scatter | solution.py:203
  621.1 67.9 %reduce-scatter.29.cloned.1.call-start = ((), (), s32[]{:S(2)}) async-start(), calls=%async_computation.37 | async-start | bytes 2621440 | tf_op jit(solution)/shard_map/reduce_scatter | solution.py:203
  657.3 68.6 %all-gather.33.cloned.1.call-start = ((), (), s32[]{:S(2)}) async-start(), calls=%async_computation.38 | async-start | bytes 2621440 | tf_op jit(solution)/shard_map/all_gather | solution.py:199
  695.8 94.2 %reduce-scatter.47.cloned.1.call-start = ((), (), s32[]{:S(2)}) async-start(), calls=%async_computation.52 | async-start | bytes 2359296 | tf_op jit(solution)/shard_map/reduce_scatter | solution.py:269
  701.8 159.3 %reduce-scatter.43.cloned.1.call-start = ((), (), s32[]{:S(2)}) async-start(), calls=%async_computation.48 | async-start | bytes 2359296 | tf_op jit(solution)/shard_map/reduce_scatter | solution.py:269
  708.4 223.9 %reduce-scatter.41.cloned.1.call-start = ((), (), s32[]{:S(2)}) async-start(), calls=%async_computation.46 | async-start | bytes 2359296 | tf_op jit(solution)/shard_map/reduce_scatter | solution.py:269
  714.5 289.3 %reduce-scatter.45.cloned.1.call-start = ((), (), s32[]{:S(2)}) async-start(), calls=%async_computation.50 | async-start | bytes 2359296 | tf_op jit(solution)/shard_map/reduce_scatter | solution.py:269
  720.6 350.7 %reduce-scatter.35.cloned.1.call-start = ((), (), s32[]{:S(2)}) async-start(), calls=%async_computation.42 | async-start | bytes 1769472 | tf_op jit(solution)/shard_map/reduce_scatter | solution.py:269
  725.4 379.4 %reduce-scatter.31.cloned.1.call-start = ((), (), s32[]{:S(2)}) async-start(), calls=%async_computation.39 | async-start | bytes 2621440 | tf_op jit(solution)/shard_map/reduce_scatter | solution.py:203
  757.1 416.3 %reduce-scatter.33.cloned.1.call-start = ((), (), s32[]{:S(2)}) async-start(), calls=%async_computation.40 | async-start | bytes 1769472 | tf_op jit(solution)/shard_map/reduce_scatter | solution.py:269
  761.9 473.6 %all-gather.45.cloned.1.call-start = ((), (), s32[]{:S(2)}) async-start(), calls=%async_computation.53 | async-start | bytes 2359296 | tf_op jit(solution)/shard_map/all_gather | solution.py:272
  800.3 498.8 %reduce-scatter.39.cloned.1.call-start = ((), (), s32[]{:S(2)}) async-start(), calls=%async_computation.45 | async-start | bytes 589824 | tf_op jit(solution)/shard_map/reduce_scatter | solution.py:269
  803.5 557.7 %all-gather.41.cloned.1.call-start = ((), (), s32[]{:S(2)}) async-start(), calls=%async_computation.49 | async-start | bytes 2359296 | tf_op jit(solution)/shard_map/all_gather | solution.py:272
  861.1 542.5 %all-gather.39.cloned.1.call-start = ((), (), s32[]{:S(2)}) async-start(), calls=%async_computation.47 | async-start | bytes 2359296 | tf_op jit(solution)/shard_map/all_gather | solution.py:272
  932.4 521.2 %all-gather.43.cloned.1.call-start = ((), (), s32[]{:S(2)}) async-start(), calls=%async_computation.51 | async-start | bytes 2359296 | tf_op jit(solution)/shard_map/all_gather | solution.py:272
  1013.9 504.4 %reduce-scatter.37.cloned.1.call-start = ((), (), s32[]{:S(2)}) async-start(), calls=%async_computation.44 | async-start | bytes 589824 | tf_op jit(solution)/shard_map/reduce_scatter | solution.py:269
  1075.5 569.3 %all-reduce.4.cloned.1.call-start = ((), (), s32[]{:S(2)}) async-start(), calls=%async_computation.54 | async-start | bytes 131072 | tf_op jit(solution)/shard_map/psum | solution.py:286
  1108.6 583.5 %all-gather.37.cloned.1.call-start = ((), (), s32[]{:S(2)}) async-start(), calls=%async_computation.43 | async-start | bytes 1769472 | tf_op jit(solution)/shard_map/all_gather | solution.py:272
  1174.4 129.5 %collective-permute-start.11 = (bf16[128,256]{1,0:T(8,128)(2,1)S(1)}, bf16[128,256]{1,0:T(8,128)(2,1)S(1)}, u32[]{:S(2)}, u32[]{:S(2)}) collective-permute-start(bf16[128,256]{1,0:T(8,128)(2,1)S(1)} %get-tuple-element.142), channel_id=1, source_target_pairs={{0,2},{1,3},{2,0},{3,1},{4,6},{5,7},{6,4},{7,5},{8,10},{9,11},{10,... | collective-permute-start | bytes 196616 | tf_op jit(solution)/shard_map/ppermute | solution.py:159
  1175.9 128.0 %collective-permute-start.10 = (bf16[128,256]{1,0:T(8,128)(2,1)S(1)}, bf16[128,256]{1,0:T(8,128)(2,1)S(1)}, u32[]{:S(2)}, u32[]{:S(2)}) collective-permute-start(bf16[128,256]{1,0:T(8,128)(2,1)S(1)} %get-tuple-element.143), channel_id=1, source_target_pairs={{0,1},{1,0},{2,3},{3,2},{4,5},{5,4},{6,7},{7,6},{8,9},{9,8},{10,11... | collective-permute-start | bytes 196616 | tf_op jit(solution)/shard_map/ppermute | solution.py:159
  1175.9 471.7 %collective-permute-start.9 = (bf16[256,1024]{1,0:T(8,128)(2,1)}, bf16[256,1024]{1,0:T(8,128)(2,1)}, u32[]{:S(2)}, u32[]{:S(2)}) collective-permute-start(bf16[256,1024]{1,0:T(8,128)(2,1)} %get-tuple-element.125), channel_id=1, source_target_pairs={{24,16},{28,20},{16,24},{20,28},{25,17},{29,21},{17,25},{21,29},{2... | collective-permute-start | bytes 1572872 | tf_op jit(solution)/shard_map/ppermute | solution.py:306
  1177.4 470.2 %collective-permute-start.8 = (bf16[256,1024]{1,0:T(8,128)(2,1)}, bf16[256,1024]{1,0:T(8,128)(2,1)}, u32[]{:S(2)}, u32[]{:S(2)}) collective-permute-start(bf16[256,1024]{1,0:T(8,128)(2,1)} %get-tuple-element.125), channel_id=1, source_target_pairs={{0,16},{4,20},{8,24},{12,28},{1,17},{5,21},{9,25},{13,29},{2,18},{... | collective-permute-start | bytes 1572872 | tf_op jit(solution)/shard_map/ppermute | solution.py:306
  1303.9 433.5 %all-gather.35.cloned.1.call-start = ((), (), s32[]{:S(2)}) async-start(), calls=%async_computation.41 | async-start | bytes 1769472 | tf_op jit(solution)/shard_map/all_gather | solution.py:272
  1561.4 86.2 %collective-permute-start.7 = (bf16[256,1024]{1,0:T(8,128)(2,1)S(1)}, bf16[256,1024]{1,0:T(8,128)(2,1)S(1)}, u32[]{:S(2)}, u32[]{:S(2)}) collective-permute-start(bf16[256,1024]{1,0:T(8,128)(2,1)S(1)} %add_convert_fusion.2), channel_id=1, source_target_pairs={{24,0},{28,4},{16,8},{20,12},{25,1},{29,5},{17,9},{21,13},{26,2},{... | collective-permute-start | bytes 1572872 | tf_op jit(solution)/shard_map/ppermute | solution.py:306
  (110 other events, 2628.3 us)
Sparse Core Ops, SparseCore 0:
  32.5 40.7 all-gather.18
  94.7 37.3 reduce-scatter.16
  140.1 31.6 all-gather.20
  208.0 31.4 reduce-scatter.18
  245.2 33.9 all-gather.22
  309.2 31.4 reduce-scatter.20
  348.1 33.9 all-gather.24
  413.7 31.4 reduce-scatter.22
  451.4 22.5 all-gather.26
  487.6 31.4 reduce-scatter.24
  527.7 22.5 all-gather.28
  582.5 31.4 reduce-scatter.26
  621.2 22.5 all-gather.30
  657.5 31.4 reduce-scatter.28
  696.0 22.5 all-gather.32
  722.4 67.6 reduce-scatter.46
  794.4 66.5 reduce-scatter.42
  865.5 66.8 reduce-scatter.40
  936.9 66.9 reduce-scatter.44
  1007.5 63.8 reduce-scatter.34
  1074.5 30.2 reduce-scatter.30
  1108.6 64.7 reduce-scatter.32
  1175.6 59.9 all-gather.44
  1238.7 60.3 reduce-scatter.38
  1301.4 51.3 all-gather.40
  1355.0 48.5 all-gather.38
  1405.8 47.7 all-gather.42
  1457.9 60.3 reduce-scatter.36
  1524.0 120.7 all-reduce.3
  1646.8 45.3 all-gather.36
  1694.3 42.9 all-gather.34

commit v2 on v1

v2 whole, which is shorter than its diff:
```python
import functools
import math

import jax
import jax.numpy as jnp
from jax import lax
from jax.experimental import pallas as pl
from jax.experimental.pallas import tpu as pltpu
from jax.sharding import PartitionSpec as P

HD = 64
EPSILON = 1e-05
MASKED = -1e30
SCALE = HD ** (-0.5)
F32 = jnp.float32
BF16 = jnp.bfloat16


def layer_norm(values, gain_row, shift_row):
    center = jnp.mean(values, axis=-1, keepdims=True)
    centred = values - center
    spread = jnp.mean(centred * centred, axis=-1, keepdims=True)
    return centred * lax.rsqrt(spread + EPSILON) * gain_row + shift_row


def rope_tables(offsets):
    halfway = HD // 2
    ladder = jnp.arange(halfway, dtype=F32) * (2.0 / HD)
    inverse = jnp.exp(-math.log(10000.0) * ladder)
    angles = offsets.astype(F32)[:, None] * inverse[None, :]
    cosine, sine = jnp.cos(angles), jnp.sin(angles)
    return (
        jnp.concatenate([cosine, cosine] * 2, axis=1),
        jnp.concatenate([-sine, sine] * 2, axis=1),
    )


def dot(left, right):
    return jnp.dot(left, right, preferred_element_type=F32)


def dot_t(left, right):
    return lax.dot_general(left, right, (((1,), (1,)), ((), ())), preferred_element_type=F32)


def t_dot(left, right):
    return lax.dot_general(left, right, (((0,), (0,)), ((), ())), preferred_element_type=F32)


MESH = pl.DeviceIdType.MESH
SEMAPHORES = 160


def layer_norm_back(values, grad, gain_row):
    center = jnp.mean(values, axis=-1, keepdims=True)
    centred = values - center
    scale = lax.rsqrt(jnp.mean(centred * centred, axis=-1, keepdims=True) + EPSILON)
    unit = centred * scale
    inner = grad * gain_row
    mean = jnp.mean(inner, axis=-1, keepdims=True)
    slope = jnp.mean(inner * unit, axis=-1, keepdims=True)
    grad_values = scale * (inner - mean - unit * slope)
    return (
        grad_values,
        jnp.sum(grad * unit, axis=0, keepdims=True),
        jnp.sum(grad, axis=0, keepdims=True),
    )


class Wire:
    def __init__(self, sems):
        self.sems, self.used, self.made = sems, 0, []
        self.at = lax.axis_index("narrow")
        self.near = self.at + 1 - 2 * lax.rem(self.at, 2)
        self.far = lax.rem(self.at + 2, 4)
        self.diagonal = lax.rem(self.near + 2, 4)

    def barrier(self):
        barrier = pltpu.get_barrier_semaphore()
        for peer in (self.near, self.far):
            pl.semaphore_signal(barrier, inc=1, device_id={"narrow": peer}, device_id_type=MESH)
        pl.semaphore_wait(barrier, 2)

    def copy(self, source, target, peer):
        made = pltpu.make_async_remote_copy(
            src_ref=source,
            dst_ref=target,
            send_sem=self.sems.at[self.used],
            recv_sem=self.sems.at[self.used + 1],
            device_id=peer if isinstance(peer, dict) else {"narrow": peer},
            device_id_type=MESH,
        )
        self.used += 2
        self.made.append(made)
        return made

    def send(self, source, target, peer):
        made = self.copy(source, target, peer)
        made.start()
        return made

    def finish(self):
        for made in self.made:
            made.wait_send()


def block_rows(block, size, part=0, parts=1):
    step = size // parts
    return pl.ds(pl.multiple_of(block * size + part * step, step), step)


class Gather:
    def __init__(self, wire, full, size):
        self.wire, self.full, self.size = wire, full, size
        self.to_near, self.to_far, self.relayed = [], [], []

    def rows(self, block, part):
        return self.full.at[block_rows(block, self.size, part, 2)]

    def push(self, part):
        own = self.rows(self.wire.at, part)
        self.to_near.append(self.wire.send(own, own, self.wire.near))
        self.to_far.append(self.wire.send(own, own, self.wire.far))

    def wait_near(self):
        for made in self.to_near:
            made.wait_recv()

    def relay(self, part):
        self.to_far[part].wait_recv()
        held = self.rows(self.wire.far, part)
        self.relayed.append(self.wire.send(held, held, self.wire.near))

    def wait_diagonal(self, part):
        self.relayed[part].wait_recv()


class Scatter:
    def __init__(self, wire, held, own, parts):
        self.held, self.own = held, own
        self.size = own.shape[0]
        step = self.size // parts
        self.cuts = [pl.ds(i * step, step) for i in range(parts)]

        def copies(out, into, peer, cuts):
            return [wire.copy(held.at[out, cut], held.at[into, cut], peer) for cut in cuts]

        self.side = copies(0, 1, wire.near, self.cuts)
        self.cross = copies(2, 3, wire.far, self.cuts)
        self.home = copies(4, 5, wire.near, [pl.ds(0, self.size)])[0]

    def put_diagonal(self, partial, part):
        self.held[0, self.cuts[part]] = partial.astype(BF16)
        self.side[part].start()

    def put_far(self, partial, part):
        cut = self.cuts[part]
        self.side[part].wait_recv()
        self.held[2, cut] = (partial + self.held[1, cut].astype(F32)).astype(BF16)
        self.cross[part].start()

    def put_near(self, partial):
        self.held[4] = partial.astype(BF16)
        self.home.start()

    def total(self):
        self.home.wait_recv()
        for made in self.cross:
            made.wait_recv()
        return self.own[...] + self.held[5].astype(F32) + self.held[3].astype(F32)


def turn(field, cosine, sine):
    lane = lax.broadcasted_iota(jnp.int32, cosine.shape, 1)
    first = lax.rem(lane, HD) < HD // 2
    turned = []
    for at in range(0, field.shape[1], 128):
        part = field[:, at : at + 128]
        swapped = jnp.where(
            first, pltpu.roll(part, 128 - HD // 2, 1), pltpu.roll(part, HD // 2, 1)
        )
        turned.append(part * cosine + swapped * sine)
    return jnp.concatenate(turned, axis=1)


def vmem(count):
    return [pl.BlockSpec(memory_space=pltpu.VMEM)] * count


def shaped(*entries):
    return [jax.ShapeDtypeStruct(shape, kind) for shape, kind in entries]


def call(kernel, number, outs, scratch, flops, *operands):
    return pl.pallas_call(
        kernel,
        in_specs=vmem(len(operands)),
        out_specs=vmem(len(outs)),
        out_shape=shaped(*outs),
        scratch_shapes=scratch + [pltpu.SemaphoreType.DMA((SEMAPHORES,))],
        compiler_params=pltpu.CompilerParams(
            collective_id=number, has_side_effects=True, vmem_limit_bytes=52 * 2**20
        ),
        cost_estimate=pl.CostEstimate(flops=flops, bytes_accessed=2**24, transcendentals=0),
        name=kernel.__name__,
    )(*operands)


def attend_half_kernel(
    x_ref, gain_ref, shift_ref, cos_ref, sin_ref, start_ref, w_qkv_ref, w_out_ref,
    a_ref, q_ref, k_ref, v_ref, o_ref, lse_ref, z_ref, h_ref, c_ref,
    held, own, sems,
):
    size = x_ref.shape[0]
    wire = Wire(sems)
    wire.barrier()
    gather = Gather(wire, a_ref, size)
    for part in range(2):
        rows = pl.ds(part * (size // 2), size // 2)
        normed = layer_norm(x_ref[rows], gain_ref[0:1], shift_ref[0:1])
        a_ref[block_rows(wire.at, size, part, 2)] = normed.astype(BF16)
        gather.push(part)
    width = q_ref.shape[1]

    def project(block):
        rows = block_rows(block, size)
        projected = dot(a_ref[rows], w_qkv_ref[...])
        cosine, sine = cos_ref[rows], sin_ref[rows]
        q_ref[rows] = turn(projected[:, :width], cosine, sine).astype(BF16)
        k_ref[rows] = turn(projected[:, width : 2 * width], cosine, sine).astype(BF16)
        v_ref[rows] = projected[:, 2 * width :].astype(BF16)

    project(wire.at)
    gather.wait_near()
    project(wire.near)
    gather.relay(0)
    gather.relay(1)
    project(wire.far)
    gather.wait_diagonal(0)
    gather.wait_diagonal(1)
    project(wire.diagonal)

    scatter = Scatter(wire, held, own, 1)
    for block in (3, 1, 2, 0):
        rows = slice(block * size, (block + 1) * size)
        reach = (block + 1) * size
        key = lax.broadcasted_iota(jnp.int32, (size, reach), 1)
        query = lax.broadcasted_iota(jnp.int32, (size, reach), 0) + block * size
        allowed = (key >= start_ref[rows, :]) & (key <= query)
        mixed, logs = [], jnp.zeros((size, 128), F32)
        lane = lax.broadcasted_iota(jnp.int32, (size, 128), 1)
        for head in range(width // HD):
            lanes = slice(head * HD, (head + 1) * HD)
            scores = dot_t(q_ref[rows, lanes] * SCALE, k_ref[:reach, lanes])
            scores = jnp.where(allowed, scores, MASKED)
            summit = jnp.max(scores, axis=1, keepdims=True)
            weights = jnp.exp(scores - summit)
            total = jnp.sum(weights, axis=1, keepdims=True)
            chances = (weights * (1.0 / total)).astype(BF16)
            mixed.append(dot(chances, v_ref[:reach, lanes]))
            logs = jnp.where(lane == head, summit + jnp.log(total), logs)
        o_ref[rows, :] = jnp.concatenate(mixed, axis=1).astype(BF16)
        lse_ref[:, rows] = logs.T[: lse_ref.shape[0]]
        partial = dot(o_ref[rows, :], w_out_ref[...])

        @pl.when(wire.diagonal == block)
        def _():
            scatter.put_diagonal(partial, 0)

        @pl.when(wire.far == block)
        def _():
            scatter.put_far(partial, 0)

        @pl.when(wire.near == block)
        def _():
            scatter.put_near(partial)

        @pl.when(wire.at == block)
        def _():
            own[...] = partial

    branch = scatter.total()
    z_ref[...] = branch
    middle = x_ref[...] + layer_norm(branch, gain_ref[1:2], shift_ref[1:2])
    h_ref[...] = middle
    c_ref[...] = layer_norm(middle, gain_ref[2:3], shift_ref[2:3]).astype(BF16)
    wire.finish()


def attend_half(resid, gains, shifts, cosine, sine, start, w_qkv, w_out):
    size, width = resid.shape
    length, part = cosine.shape[0], w_out.shape[0]
    return call(
        attend_half_kernel,
        1,
        [((length, width), BF16)]
        + [((length, part), BF16)] * 4
        + [((8, length), F32), ((size, width), F32), ((size, width), F32), ((size, width), BF16)],
        [pltpu.VMEM((6, size, width), BF16), pltpu.VMEM((size, width), F32)],
        8 * length * width * part + 4 * length * length * part,
        resid, gains, shifts, cosine, sine, start, w_qkv, w_out,
    )


def feed_half_kernel(
    c_ref, h_ref, gain_ref, shift_ref, w_up_ref, b_up_ref, w_down_ref,
    inner_ref, e_ref, d_ref, w_ref, y_ref,
    held, own, sems,
):
    size = c_ref.shape[0]
    half = size // 2
    wire = Wire(sems)
    wire.barrier()
    gather = Gather(wire, inner_ref, size)
    for part in range(2):
        inner_ref[block_rows(wire.at, size, part, 2)] = c_ref[pl.ds(part * half, half)]
        gather.push(part)
    scatter = Scatter(wire, held, own, 2)

    def feed(cuts):
        inner = jnp.concatenate([inner_ref[cut] for cut in cuts])
        hidden = dot(inner, w_up_ref[...]) + b_up_ref[...]
        below = 0.5 + 0.5 * lax.erf(hidden * (0.5**0.5))
        density = jnp.exp(-0.5 * hidden * hidden) * ((2.0 * math.pi) ** -0.5)
        active = (hidden * below).astype(BF16)
        slope = (below + hidden * density).astype(BF16)
        for at, cut in enumerate(cuts):
            step = inner.shape[0] // len(cuts)
            e_ref[cut] = active[at * step : (at + 1) * step]
            d_ref[cut] = slope[at * step : (at + 1) * step]
        return dot(active, w_down_ref[...])

    own[...] = feed([block_rows(wire.at, size)])
    gather.wait_near()
    scatter.put_near(feed([block_rows(wire.near, size)]))
    for part in range(2):
        gather.relay(part)
        gather.wait_diagonal(part)
        partial = feed(
            [block_rows(wire.diagonal, size, part, 2), block_rows(wire.far, size, part, 2)]
        )
        scatter.put_diagonal(partial[:half], part)
        scatter.put_far(partial[half:], part)
    second = scatter.total()
    w_ref[...] = second
    y_ref[...] = h_ref[...] + layer_norm(second, gain_ref[3:4], shift_ref[3:4])
    wire.finish()


def feed_half(inner, middle, gains, shifts, w_up, b_up, w_down):
    size, width = inner.shape
    length, hidden = 4 * size, w_up.shape[1]
    return call(
        feed_half_kernel,
        2,
        [((length, width), BF16)]
        + [((length, hidden), BF16)] * 2
        + [((size, width), F32)] * 2,
        [pltpu.VMEM((6, size, width), BF16), pltpu.VMEM((size, width), F32)],
        4 * length * width * hidden,
        inner, middle, gains, shifts, w_up, b_up, w_down,
    )


def feed_back_kernel(
    g_ref, w_ref, h_ref, z_ref, gain_ref, inner_ref, e_ref, d_ref, w_up_ref, w_down_ref,
    grad_down_ref, grad_up_ref, grad_b_ref, norms_ref, dh_ref, dz_ref,
    second, hidden, held, own, sems,
):
    size = g_ref.shape[0]
    half = size // 2
    wire = Wire(sems)
    wire.barrier()
    gather = Gather(wire, second, size)
    norms = [jnp.zeros((1, g_ref.shape[1]), F32)] * 2
    for part in range(2):
        rows = pl.ds(part * half, half)
        grad, gain, shift = layer_norm_back(w_ref[rows], g_ref[rows], gain_ref[3:4])
        second[block_rows(wire.at, size, part, 2)] = grad.astype(BF16)
        gather.push(part)
        norms = [norms[0] + gain, norms[1] + shift]
    norms_ref[3:4] = norms[0]
    norms_ref[7:8] = norms[1]
    norms_ref[0:1] = jnp.zeros_like(norms[0])
    norms_ref[4:5] = jnp.zeros_like(norms[0])
    scatter = Scatter(wire, held, own, 2)

    def feed(cuts, first=False):
        grad = jnp.concatenate([second[cut] for cut in cuts])
        slope = jnp.concatenate([d_ref[cut] for cut in cuts]).astype(F32)
        grad = (slope * dot_t(grad, w_down_ref[...])).astype(BF16)
        for at, cut in enumerate(cuts):
            step = grad.shape[0] // len(cuts)
            hidden[cut] = grad[at * step : (at + 1) * step]
        bias = jnp.sum(grad.astype(F32), axis=0, keepdims=True)
        grad_b_ref[...] = bias if first else grad_b_ref[...] + bias
        return dot_t(grad, w_up_ref[...])

    own[...] = feed([block_rows(wire.at, size)], True)
    gather.wait_near()
    scatter.put_near(feed([block_rows(wire.near, size)]))
    for part in range(2):
        gather.relay(part)
        gather.wait_diagonal(part)
        partial = feed(
            [block_rows(wire.diagonal, size, part, 2), block_rows(wire.far, size, part, 2)]
        )
        scatter.put_diagonal(partial[:half], part)
        scatter.put_far(partial[half:], part)
    for at in range(0, e_ref.shape[1], 256):
        cut = slice(at, at + 256)
        grad_down_ref[cut, :] = t_dot(e_ref[:, cut], second[...]).astype(BF16)
    for at in range(0, inner_ref.shape[1], 256):
        cut = slice(at, at + 256)
        grad_up_ref[cut, :] = t_dot(inner_ref[:, cut], hidden[...]).astype(BF16)
    grad, gain, shift = layer_norm_back(h_ref[...], scatter.total(), gain_ref[2:3])
    norms_ref[2:3] = gain
    norms_ref[6:7] = shift
    grad = g_ref[...] + grad
    dh_ref[...] = grad
    grad, gain, shift = layer_norm_back(z_ref[...], grad, gain_ref[1:2])
    norms_ref[1:2] = gain
    norms_ref[5:6] = shift
    dz_ref[...] = grad.astype(BF16)
    wire.finish()


def feed_back(grad, second, middle, branch, gains, inner, active, slope, w_up, w_down):
    size, width = grad.shape
    length, hidden = 4 * size, w_up.shape[1]
    return call(
        feed_back_kernel,
        3,
        [
            ((hidden, width), BF16),
            ((width, hidden), BF16),
            ((1, hidden), F32),
            ((8, width), F32),
            ((size, width), F32),
            ((size, width), BF16),
        ],
        [
            pltpu.VMEM((length, width), BF16),
            pltpu.VMEM((length, hidden), BF16),
            pltpu.VMEM((6, size, width), BF16),
            pltpu.VMEM((size, width), F32),
        ],
        8 * length * width * hidden,
        grad, second, middle, branch, gains, inner, active, slope, w_up, w_down,
    )


def attend_back_kernel(
    dz_ref, dh_ref, x_ref, gain_ref, a_ref, q_ref, k_ref, v_ref, o_ref, lse_ref, start_ref,
    cos_ref, sin_ref, w_qkv_ref, w_out_ref,
    grad_qkv_ref, grad_out_ref, norms_ref, dx_ref,
    branch, mixture, projected, dk, dv, held, own, sems,
):
    size = dz_ref.shape[0]
    length, width = q_ref.shape
    half = size // 2
    wire = Wire(sems)
    wire.barrier()
    gather = Gather(wire, branch, size)
    for part in range(2):
        branch[block_rows(wire.at, size, part, 2)] = dz_ref[pl.ds(part * half, half)]
        gather.push(part)

    def unmix(block):
        rows = block_rows(block, size)
        mixture[rows] = dot_t(branch[rows], w_out_ref[...]).astype(BF16)

    dk[...] = jnp.zeros_like(dk)
    dv[...] = jnp.zeros_like(dv)
    unmix(wire.at)
    gather.wait_near()
    unmix(wire.near)
    gather.relay(0)
    gather.relay(1)
    unmix(wire.far)
    gather.wait_diagonal(0)
    gather.wait_diagonal(1)
    unmix(wire.diagonal)
    grad_out_ref[...] = t_dot(o_ref[...], branch[...]).astype(BF16)

    pick_head = (
        lax.broadcasted_iota(jnp.int32, (8, width), 1) // HD
        == lax.broadcasted_iota(jnp.int32, (8, width), 0)
    ).astype(F32)
    for block in range(length // size):
        rows = slice(block * size, (block + 1) * size)
        reach = (block + 1) * size
        key = lax.broadcasted_iota(jnp.int32, (reach, size), 0)
        query = lax.broadcasted_iota(jnp.int32, (reach, size), 1) + block * size
        allowed = (key >= start_ref[:, rows]) & (key <= query)
        inner = lax.dot_general(
            pick_head,
            mixture[rows].astype(F32) * o_ref[rows].astype(F32),
            (((1,), (1,)), ((), ())),
            precision=lax.Precision.HIGHEST,
            preferred_element_type=F32,
        )
        dqs, dks, dvs = [], [], []
        for head in range(width // HD):
            lanes = slice(head * HD, (head + 1) * HD)
            k_head, g_head = k_ref[:reach, lanes], mixture[rows, lanes]
            q_head = q_ref[rows, lanes] * SCALE
            scores = dot_t(k_head, q_head) - lse_ref[head : head + 1, rows]
            chances = jnp.exp(jnp.where(allowed, scores, MASKED))
            grad_prob = dot_t(v_ref[:reach, lanes], g_head)
            grad_score = (chances * (grad_prob - inner[head : head + 1])).astype(BF16)
            dvs.append(dot(chances.astype(BF16), g_head))
            dks.append(dot(grad_score, q_head))
            dqs.append(t_dot(grad_score, k_head) * SCALE)
        dq = jnp.concatenate(dqs, axis=1)
        projected[rows, :width] = turn(dq, cos_ref[rows], -sin_ref[rows]).astype(BF16)
        dk[:reach, :] += jnp.concatenate(dks, axis=1)
        dv[:reach, :] += jnp.concatenate(dvs, axis=1)
    for block in range(length // size):
        rows = slice(block * size, (block + 1) * size)
        turned = turn(dk[rows], cos_ref[rows], -sin_ref[rows])
        projected[rows, width : 2 * width] = turned.astype(BF16)
        projected[rows, 2 * width :] = dv[rows].astype(BF16)

    scatter = Scatter(wire, held, own, 2)

    def unproject(cut):
        return dot_t(projected[cut], w_qkv_ref[...])

    partial = unproject(block_rows(wire.diagonal, size))
    scatter.put_diagonal(partial[:half], 0)
    scatter.put_diagonal(partial[half:], 1)
    partial = unproject(block_rows(wire.far, size))
    scatter.put_far(partial[:half], 0)
    scatter.put_far(partial[half:], 1)
    scatter.put_near(unproject(block_rows(wire.near, size)))
    own[...] = unproject(block_rows(wire.at, size))
    for at in range(0, a_ref.shape[1], 256):
        cut = slice(at, at + 256)
        grad_qkv_ref[cut, :] = t_dot(a_ref[:, cut], projected[...]).astype(BF16)
    grad, gain, shift = layer_norm_back(x_ref[...], scatter.total(), gain_ref[0:1])
    norms_ref[...] = jnp.zeros_like(norms_ref)
    norms_ref[0:1] = gain
    norms_ref[4:5] = shift
    dx_ref[...] = (dh_ref[...] + grad).astype(BF16)
    wire.finish()


def attend_back(
    grad_branch, grad_middle, resid, gains, normed, query, keys, values, mixture, logs, start,
    cosine, sine, w_qkv, w_out,
):
    size, width = resid.shape
    length, part = query.shape
    return call(
        attend_back_kernel,
        4,
        [
            ((width, 3 * part), BF16),
            ((part, width), BF16),
            ((8, width), F32),
            ((size, width), BF16),
        ],
        [
            pltpu.VMEM((length, width), BF16),
            pltpu.VMEM((length, part), BF16),
            pltpu.VMEM((length, 3 * part), BF16),
            pltpu.VMEM((length, part), F32),
            pltpu.VMEM((length, part), F32),
            pltpu.VMEM((6, size, width), BF16),
            pltpu.VMEM((size, width), F32),
        ],
        16 * length * width * part + 10 * length * length * part,
        grad_branch, grad_middle, resid, gains, normed, query, keys, values, mixture, logs,
        start, cosine, sine, w_qkv, w_out,
    )


class Ring:
    def __init__(self):
        at = lax.axis_index("wide")
        self.pair = lax.rem(at, 2)
        self.turn = at // 2
        self.up = {"wide": lax.rem(self.turn + 1, 4) * 2 + self.pair}
        self.down = {"wide": lax.rem(self.turn + 3, 4) * 2 + self.pair}
        self.side = {"wide": at + 1 - 2 * self.pair}


def span(start, size):
    return pl.ds(pl.multiple_of(start, 16), size)


class Piece:
    def __init__(self, view, rows, by_side, ring):
        self.view, self.rows, self.by_side = view, rows, by_side
        self.eighth = rows // 8
        pair, turn = ring.pair, ring.turn
        if by_side:
            self.mine = pair * (rows // 2) + turn * self.eighth
            self.joined, self.joined_size = pair * (rows // 2), rows // 2
        else:
            self.mine = turn * (rows // 4) + pair * self.eighth
            self.joined, self.joined_size = turn * (rows // 4), rows // 4

    def own(self):
        return self.view(span(self.mine, self.eighth))

    def whole(self):
        return self.view(span(self.joined, self.joined_size))

    def around(self, ring, step, half):
        size = self.eighth if self.by_side else self.joined_size
        start = self.joined if self.by_side else 0
        other = lax.rem(ring.turn + step, 4) * size + start
        return self.view(span(other + half * (size // 2), size // 2))


def spread_steps(wire, ring, pieces):
    def both_ways(piece, part):
        return (
            wire.send(part, part, ring.up),
            wire.send(part, part, ring.down),
        )

    def onwards(piece, sent):
        sent[0].wait_recv()
        first = piece.around(ring, 3, 0)
        up = wire.send(first, first, ring.up)
        sent[1].wait_recv()
        second = piece.around(ring, 1, 1)
        return up, wire.send(second, second, ring.down)

    by_side = [piece for piece in pieces if piece.by_side]
    others = [piece for piece in pieces if not piece.by_side]
    sent = [both_ways(piece, piece.own()) for piece in by_side]
    across = [wire.send(piece.own(), piece.own(), ring.side) for piece in others]
    yield
    relayed = [onwards(piece, pair) for piece, pair in zip(by_side, sent)]
    for made in across:
        made.wait_recv()
    sent = [both_ways(piece, piece.whole()) for piece in others]
    yield
    for pair in relayed:
        for made in pair:
            made.wait_recv()
    across = [wire.send(piece.whole(), piece.whole(), ring.side) for piece in by_side]
    relayed = [onwards(piece, pair) for piece, pair in zip(others, sent)]
    yield
    for made in across:
        made.wait_recv()
    for pair in relayed:
        for made in pair:
            made.wait_recv()


def add_rows(target, rows, *sources):
    step = min(rows, 128)
    for at in range(0, rows, step):
        cut = pl.ds(at, step)
        total = sources[0](at, step).astype(F32)
        for source in sources[1:]:
            total = total + source(at, step).astype(F32)
        target[cut] = total.astype(BF16)


def part_of(ref, start=0):
    return lambda at, step: ref[span(start + at, step)]


def slot_of(ref, slot, start=0):
    return lambda at, step: ref[slot, span(start + at, step)]


class Fold:
    def __init__(self, wire, ring, ref, by_side, scratch):
        self.wire, self.ring, self.ref, self.by_side = wire, ring, ref, by_side
        self.joined, self.across, self.early, self.out, self.into, self.final = scratch
        self.rows = ref.shape[0]
        self.size = self.rows // 8 if by_side else self.rows // 4

    @staticmethod
    def scratch(rows, columns, by_side):
        size = rows // 8 if by_side else rows // 4
        joined = rows // 2 if by_side else rows // 4
        across = rows // 2 if by_side else rows // 8
        return [
            pltpu.VMEM((joined, columns), BF16),
            pltpu.VMEM((across, columns), BF16),
            pltpu.VMEM((2, size // 2, columns), BF16),
            pltpu.VMEM((2, size, columns), BF16),
            pltpu.VMEM((2, size, columns), BF16),
            pltpu.VMEM((rows // 8, columns), BF16),
        ]

    def source(self):
        return self.joined if self.by_side else self.ref

    def part(self, step):
        return lax.rem(self.ring.turn + step, 4) * self.size

    def start_side(self):
        pair = self.ring.pair
        if self.by_side:
            half = self.rows // 2
            source = self.ref.at[span((1 - pair) * half, half)]
        else:
            half = self.rows // 8
            source = self.joined.at[span((1 - pair) * half, half)]
        self.side = self.wire.send(source, self.across, self.ring.side)

    def end_side(self):
        self.side.wait_recv()
        pair = self.ring.pair
        if self.by_side:
            half = self.rows // 2
            add_rows(self.joined, half, part_of(self.ref, pair * half), part_of(self.across))
        else:
            half = self.rows // 8
            add_rows(self.final, half, part_of(self.joined, pair * half), part_of(self.across))

    def start_early(self):
        half = self.size // 2
        opposite = self.part(2)
        source = self.source()
        self.first = [
            self.wire.send(source.at[span(opposite, half)], self.early.at[0], self.ring.up),
            self.wire.send(source.at[span(opposite + half, half)], self.early.at[1], self.ring.down),
        ]

    def start_late(self):
        half = self.size // 2
        source = self.source()
        self.second = []
        for way, (step, peer) in enumerate([(1, self.ring.up), (3, self.ring.down)]):
            self.first[way].wait_recv()
            start = self.part(step)
            out = self.out.at[way]
            for at in (0, 1):
                cut = out.at[pl.ds(at * half, half)]
                if at == way:
                    add_rows(
                        cut, half, part_of(source, start + at * half), slot_of(self.early, way)
                    )
                else:
                    cut[...] = source[span(start + at * half, half)]
            self.second.append(self.wire.send(out, self.into.at[way], peer))

    def end_late(self):
        for made in self.second:
            made.wait_recv()
        target = self.final if self.by_side else self.joined
        start = self.part(0)
        add_rows(
            target,
            self.size,
            part_of(self.source(), start),
            slot_of(self.into, 0),
            slot_of(self.into, 1),
        )


def fold_steps(folds):
    by_side = [fold for fold in folds if fold.by_side]
    others = [fold for fold in folds if not fold.by_side]
    for fold in others:
        fold.start_early()
    for fold in by_side:
        fold.start_side()
    yield
    for fold in others:
        fold.start_late()
    yield
    for fold in by_side:
        fold.end_side()
        fold.start_early()
    yield
    for fold in others:
        fold.end_late()
        fold.start_side()
    for fold in by_side:
        fold.start_late()
    yield
    for fold in others:
        fold.end_side()
    for fold in by_side:
        fold.end_late()


def small_steps(wire, ring, norms_ref, bias_ref, narrow_in, sums, side_in, turn_in, total_ref):
    part = total_ref.shape[1]
    made = []

    def columns(device):
        return pl.ds(pl.multiple_of(device * part, part), part)

    for peer in (wire.near, wire.far, wire.diagonal):
        made.append(
            wire.send(norms_ref.at[:, columns(peer)], narrow_in.at[wire.at], {"narrow": peer})
        )
    narrow_in[wire.at] = norms_ref[:, columns(wire.at)]
    yield
    for copy in made:
        copy.wait_recv()
    total = narrow_in[0] + narrow_in[1] + narrow_in[2] + narrow_in[3]
    lines = [bias_ref[:, at * part : (at + 1) * part] for at in range(4)]
    sums[...] = jnp.concatenate([total] + lines + [jnp.zeros((4, part), F32)], axis=0)
    side = wire.send(sums, side_in, ring.side)
    yield
    side.wait_recv()
    turn_in[ring.turn] = sums[...] + side_in[...]
    own = turn_in.at[ring.turn]
    up, down = wire.send(own, own, ring.up), wire.send(own, own, ring.down)
    yield
    up.wait_recv()
    down.wait_recv()
    below = turn_in.at[lax.rem(ring.turn + 3, 4)]
    last = wire.send(below, below, ring.up)
    yield
    last.wait_recv()
    total_ref[...] = turn_in[0] + turn_in[1] + turn_in[2] + turn_in[3]


def wide_barrier(wire, ring):
    barrier = pltpu.get_barrier_semaphore()
    peers = [ring.up, ring.down, ring.side]
    peers += [{"narrow": peer} for peer in (wire.near, wire.far, wire.diagonal)]
    for peer in peers:
        pl.semaphore_signal(barrier, inc=1, device_id=peer, device_id_type=MESH)
    pl.semaphore_wait(barrier, len(peers))


def run(*steps):
    steps = list(steps)
    while steps:
        for at in list(steps):
            if next(at, "end") == "end":
                steps.remove(at)


def sum_gradients_kernel(
    qkv_ref, out_ref, up_ref, down_ref, norms_ref, bias_ref,
    full_qkv, full_out, full_up, full_down, total_ref,
    *scratch,
):
    narrow_in, sums, side_in, turn_in, sems = scratch[24:]
    wire, ring = Wire(sems), Ring()
    wide_barrier(wire, ring)
    down = Fold(wire, ring, down_ref, True, scratch[0:6])
    out = Fold(wire, ring, out_ref, True, scratch[6:12])
    up = Fold(wire, ring, up_ref, False, scratch[12:18])
    qkv = Fold(wire, ring, qkv_ref, False, scratch[18:24])
    run(
        fold_steps([down, out, up, qkv]),
        small_steps(
            wire, ring, norms_ref, bias_ref, narrow_in, sums, side_in, turn_in, total_ref
        ),
    )
    part = total_ref.shape[1]

    def columns(device):
        return pl.ds(pl.multiple_of(device * part, part), part)

    pieces = [
        Piece(lambda rows: full_down.at[:, rows], down_ref.shape[0], True, ring),
        Piece(lambda rows: full_out.at[:, rows], out_ref.shape[0], True, ring),
        Piece(lambda rows: full_up.at[rows], up_ref.shape[0], False, ring),
        Piece(lambda rows: full_qkv.at[rows], qkv_ref.shape[0], False, ring),
    ]
    made = []
    at = wire.at
    for fold, piece, full in ((down, pieces[0], full_down), (out, pieces[1], full_out)):
        slot = full.at[at, span(piece.mine, piece.eighth)]
        for peer in (wire.diagonal, wire.far, wire.near):
            made.append(wire.send(fold.final.at[:, columns(peer)], slot, {"narrow": peer}))
        slot[...] = fold.final[:, columns(at)]
    pieces[2].own()[...] = up.final[...]
    rows = span(pieces[3].mine, pieces[3].eighth)
    odd, upper = lax.rem(at, 2), at // 2
    made.append(
        wire.send(
            qkv.final.at[:, columns(2 - 2 * upper)],
            full_qkv.at[rows, columns(2 - 2 * odd)],
            {"narrow": wire.far},
        )
    )
    made.append(
        wire.send(
            qkv.final.at[:, columns(1 - odd + upper)],
            full_qkv.at[rows, columns(1)],
            {"narrow": wire.near},
        )
    )
    full_qkv[rows, columns(2 * odd)] = qkv.final[:, columns((at + 1) // 2)]
    for copy in made:
        copy.wait_recv()
    run(spread_steps(wire, ring, pieces))
    wire.finish()


def sum_gradients(qkv, out, up, down, norms, bias):
    narrow = lax.axis_size("narrow")
    part = norms.shape[1] // narrow
    items = ((down, True), (out, True), (up, False), (qkv, False))
    scratch = [entry for item, kind in items for entry in Fold.scratch(*item.shape, kind)]
    scratch += [
        pltpu.VMEM((narrow, 8, part), F32),
        pltpu.VMEM((16, part), F32),
        pltpu.VMEM((16, part), F32),
        pltpu.VMEM((4, 16, part), F32),
    ]
    return call(
        sum_gradients_kernel,
        5,
        [
            (qkv.shape, BF16),
            ((narrow, out.shape[0], part), BF16),
            (up.shape, BF16),
            ((narrow, down.shape[0], part), BF16),
            ((16, part), F32),
        ],
        scratch,
        0,
        qkv, out, up, down, norms, bias,
    )


def swap(block, distance):
    count = lax.axis_size("narrow")
    return lax.ppermute(block, "narrow", [(i, i ^ distance) for i in range(count)])


def pick(stack, table, at):
    return lax.dynamic_index_in_dim(stack, jnp.asarray(table)[at], 0, keepdims=False)


def by_heads(block, at):
    parts = jnp.stack(jnp.split(block, 3, axis=1))
    own = pick(parts, [0, 2, 0, 2], at)
    near = swap(parts[1], 1)
    far = swap(pick(parts, [2, 0, 2, 0], at), 2)
    parts = jnp.stack([own, near, far])
    order = jnp.asarray([[0, 1, 2], [1, 0, 2], [2, 0, 1], [2, 1, 0]])[at]
    return jnp.concatenate(
        [lax.dynamic_index_in_dim(parts, order[i], 0, keepdims=False) for i in range(3)], axis=1
    )


def from_heads(block, at):
    parts = jnp.stack(jnp.split(block, 3, axis=1))
    own = pick(parts, [0, 1, 1, 2], at)
    near = swap(pick(parts, [1, 0, 2, 1], at), 1)
    far = swap(pick(parts, [2, 2, 0, 0], at), 2)
    parts = jnp.stack([own, near, far])
    order = jnp.asarray([[0, 1, 2], [2, 1, 0], [0, 1, 2], [2, 1, 0]])[at]
    return jnp.concatenate(
        [lax.dynamic_index_in_dim(parts, order[i], 0, keepdims=False) for i in range(3)], axis=1
    )


def to_rows(block):
    return lax.all_to_all(block, "narrow", split_axis=0, concat_axis=1, tiled=True)


def to_columns(block):
    return lax.all_to_all(block, "narrow", split_axis=1, concat_axis=0, tiled=True)


def layer_forward(resid, weights, start, tables):
    w_qkv, w_out, w_up, b_up, w_down, gains, shifts = weights
    normed, query, keys, values, mixture, logs, branch, middle, inner = attend_half(
        resid, gains, shifts, *tables, start[:, None], w_qkv, w_out
    )
    inner, active, slope, second, result = feed_half(
        inner, middle, gains, shifts, w_up, b_up, w_down
    )
    return result, (
        resid, normed, query, keys, values, mixture, logs, branch, middle, inner, active, slope, second
    )


def layer_backward(grad, saved, weights, start, tables):
    w_qkv, w_out, w_up, b_up, w_down, gains, shifts = weights
    resid, normed, query, keys, values, mixture, logs, branch, middle, inner, active, slope, second = saved
    grad_down, grad_up, grad_b_up, norms, grad_middle, grad_branch = feed_back(
        grad, second, middle, branch, gains, inner, active, slope, w_up, w_down
    )
    grad_qkv, grad_out, norms_too, grad = attend_back(
        grad_branch, grad_middle, resid, gains, normed, query, keys, values, mixture, logs,
        start[None], *tables, w_qkv, w_out,
    )
    return grad, (grad_qkv, grad_out, grad_up, grad_b_up, grad_down, norms + norms_too)


def reduce_grads(grads, at):
    def fold(block):
        return lax.psum_scatter(block, "wide", scatter_dimension=0, tiled=True)

    def spread(block):
        return lax.all_gather(block, "wide", axis=0, tiled=True)

    def spread_rows(block):
        wide, narrow = lax.axis_size("wide"), lax.axis_size("narrow")
        rows, width = block.shape
        full = spread(block).reshape(wide, narrow, rows // narrow, width)
        return full.transpose(1, 0, 2, 3).reshape(wide * rows, width)

    qkv, out, up, b_up, down, norms = grads
    if lax.axis_size("wide") == 8:
        qkv, out, up, down, total = sum_gradients(qkv, out, up, down, norms, b_up)
        out, down = (block.reshape(-1, block.shape[2]) for block in (out, down))
        return qkv, out, up, total[8:12].reshape(-1), down, total[:4], total[4:8]
    qkv = spread(from_heads(fold(qkv), at))
    out = spread_rows(to_columns(fold(out)))
    up = spread(fold(up))
    down = spread_rows(to_columns(fold(down)))
    b_up = lax.psum(b_up[0], "wide")
    norms = lax.psum(norms, ("wide", "narrow"))
    part = norms.shape[1] // lax.axis_size("narrow")
    norms = lax.dynamic_slice_in_dim(norms, at * part, part, 1)
    return qkv, out, up, b_up, down, norms[:4], norms[4:]


def on_device(ends, lengths, w_qkv, w_out, w_up, b_up, w_down, norm_gain, norm_bias):
    wide = lax.axis_size("wide")
    narrow = lax.axis_size("narrow")
    halfway = wide // 2
    flip = wide - 2
    wide_at = lax.axis_index("wide")
    at = lax.axis_index("narrow")
    first = wide_at < halfway
    row_count = ends.shape[0] // 2
    width = ends.shape[1]
    length = row_count * narrow
    blocks = ends.reshape(2, row_count, width)

    def route(block, pairs):
        return lax.ppermute(block, "wide", pairs)

    groups = range(halfway)
    x_came = route(blocks[1], [(g, g ^ flip) for g in groups])
    dy_first = route(blocks[0], [(g + halfway, g) for g in groups])
    dy_second = route(blocks[1], [(g + halfway, g ^ flip) for g in groups])
    resid = jnp.where(first, blocks[0], x_came).astype(F32)
    upstream = jnp.where(first, dy_first, dy_second).astype(F32)
    group_at = jnp.where(first, wide_at, wide_at ^ flip)
    micro_at = jnp.where(first, 0, 1)

    own_lengths = lengths[group_at, micro_at]
    places = jnp.arange(length, dtype=jnp.int32)
    passed = (places[:, None] >= jnp.cumsum(own_lengths)[None, :]).astype(jnp.int32)
    start = jnp.sum(passed * own_lengths[None, :], axis=1)
    tables = rope_tables(places - start)

    def weights_of(layer):
        return (
            by_heads(w_qkv[layer], at),
            to_rows(w_out[layer]),
            w_up[layer],
            b_up[layer].astype(F32)[None],
            to_rows(w_down[layer]),
            lax.all_gather(norm_gain[layer], "narrow", axis=1, tiled=True).astype(F32),
            lax.all_gather(norm_bias[layer], "narrow", axis=1, tiled=True).astype(F32),
        )

    weights = [weights_of(layer) for layer in range(2)]
    middle, saved_first = layer_forward(resid, weights[0], start, tables)
    middle = middle.astype(BF16).astype(F32)
    result, saved_second = layer_forward(middle, weights[1], start, tables)
    result = result.astype(BF16)
    grad, grads_second = layer_backward(upstream, saved_second, weights[1], start, tables)
    totals_second = reduce_grads(grads_second, at)
    grad, grads_first = layer_backward(grad.astype(F32), saved_first, weights[0], start, tables)
    totals_first = reduce_grads(grads_first, at)

    grad_came = route(grad, [(g ^ flip, g) for g in groups])
    result_first = route(result, [(g, g + halfway) for g in groups])
    result_second = route(result, [(g ^ flip, g + halfway) for g in groups])
    ends_out = jnp.where(
        first,
        jnp.concatenate([grad, grad_came]),
        jnp.concatenate([result_first, result_second]),
    )
    totals = [jnp.stack([a.astype(F32), b.astype(F32)]) for a, b in zip(totals_first, totals_second)]
    return (ends_out,) + tuple(totals)


def solution(mesh):
    placed = (
        P(("wide", "narrow"), None),
        P(),
        P(None, None, "narrow"),
        P(None, None, "narrow"),
        P(None, None, "narrow"),
        P(None, "narrow"),
        P(None, None, "narrow"),
        P(None, None, "narrow"),
        P(None, None, "narrow"),
    )
    return jax.shard_map(
        on_device,
        mesh=mesh,
        in_specs=placed,
        out_specs=(P(("wide", "narrow"), None),) + placed[2:],
        check_vma=False,
    )
```

time: 1760 us -> 880 us (0.50)
  waiting for transfers between devices: 1120 us -> 11.9 us
  Pallas kernels: 37.7 us -> 703 us
  blocking collectives: 196 us -> 34 us
  matrix products: 127 us -> 0 us
  other arithmetic: 93.9 us -> 37.1 us
  local copies, waits for them, and re-layouts: 92.1 us -> 39.3 us
  between operations: 37.8 us -> 11.1 us
    reduce_scatter x16 -> x0, waiting for transfers between devices: 697 us -> none  [the longest x8 464 us: fold(): lax.psum_scatter(block.astype(BF16), 'wide', scatter_dimension=0, tiled=T...]
    pallas_call x4 -> x10, Pallas kernels: 37.7 us -> 703 us  [call(): pl.pallas_call(kernel, in_specs=vmem(len(operands)), out_specs=vmem(len(o...]
    all_gather x14 -> x0, waiting for transfers between devices: 295 us -> none  [the longest x6 226 us: spread(): return lax.all_gather(block, 'wide', axis=0, tiled=True)]
    dot_general x24 -> x0, matrix products: 127 us -> none  [the longest x8 48.9 us: dot(): return jnp.dot(left, right, preferred_element_type=F32)]
    all_to_all x4 -> x0, blocking collectives: 90.6 us -> none  [the longest x2 72.3 us: to_rows(): lax.all_to_all(block, 'narrow', split_axis=0, concat_axis=1, tiled=True)]
    psum x1 -> x0, waiting for transfers between devices: 80.5 us -> none  [reduce_grads(): norms = lax.psum(jnp.concatenate([gains, shifts]), ('wide', 'narrow'))]
    all_gather x2 -> x0, blocking collectives: 63.8 us -> none  [spread(): return lax.all_gather(block, 'wide', axis=0, tiled=True)]
    reduce_sum x33 -> x0, other arithmetic: 46.1 us -> none  [the longest x13 22.2 us: layer_norm(): return centred * lax.rsqrt(spread + EPSILON) * gain_row + shift_row]
  transfers between devices with their start and end apart: 49 -> 14, of which waited for: 29 -> 2; matrix products, arithmetic and copies ran while one was open for 8% -> 6% of each run, Pallas kernels for 1% -> 68%
where the time goes in v2:
time: 880 us; the launch traced here: 871 us
  Pallas kernels  703 us (80%)
  local copies, waits for them, and re-layouts  39.3 us (4%)
  other arithmetic  37.1 us (4%)
  starting transfers between devices  34.2 us (4%)
  blocking collectives  34 us (4%)
  waiting for transfers between devices  11.9 us (1%)
  between operations  11.1 us (1%)
    pallas_call x10, Pallas kernels, call(): pl.pallas_call(kernel, in_specs=vmem(len(operands)), out_specs=vmem(len(o...  703 us
    all_gather x2, blocking collectives, weights_of(): lax.all_gather(norm_bias[layer], 'narrow', axis=1, tiled=True).astype(F32)  23.7 us
  transfers between devices with their start and end apart: 14, of which 2 were waited for; matrix products, arithmetic and copies ran while one was open for 6% of the time, Pallas kernels for 68%

profile of v2, /device:TPU:0, one launch (start us, length us, event | category | flops | bytes accessed | tf_op | source)
XLA Modules:
  0.0 871.1 jit_solution(8266764193246892322)
XLA Ops:
  2.5 7.8 collective-permute-start.2
  10.3 2.2 fusion.5
  12.5 3.5 all-to-all-start
  32.3 2.3 fusion.2
  35.1 18.5 %all-gather.3 = bf16[1,4,1024]{2,1,0:T(4,128)(2,1)S(1)} all-gather(bf16[1,4,256]{2,1,0:T(4,128)(2,1)S(1)} %get-tuple-element.163), channel_id=5, replica_groups=mesh['wide'=8,'narrow'=4] {'narrow'}, dimensions={2}, use_global_device_ids=true | all-gather | bytes 10240 | tf_op jit(solution)/shard_map/all_gather | solution.py:1062
  53.6 5.1 all-gather.2
  58.7 5.1 all-gather.1
  63.9 5.1 all-gather
  69.2 3.5 all-to-all-start.2
  72.7 8.8 %all-to-all-done.2 = bf16[4,256,256]{2,1,0:T(8,128)(2,1)S(1)} async-done(((bf16[4,256,256]{2,1,0:T(8,128)(2,1)}), bf16[4,256,256]{2,1,0:T(8,128)(2,1)S(1)}, u32[]{:S(2)}, u32[]{:S(2)}) %all-to-all-start.2) | async-done | bytes 524320 | tf_op jit(solution)/shard_map/all_to_all | solution.py:961
  82.3 3.6 all-to-all-start.1
  85.9 4.7 slice_bitcast_fusion
  91.3 2.9 fusion
  101.7 3.5 pad_maximum_fusion.6
  108.5 3.1 all-to-all-done.1
  111.6 4.6 all-to-all-start.3
  124.5 55.9 %attend_half_kernel.2 = (bf16[1024,1024]{1,0:T(8,128)(2,1)}, bf16[1024,256]{1,0:T(8,128)(2,1)S(1)}, bf16[1024,256]{1,0:T(8,128)(2,1)S(1)}, bf16[1024,256]{1,0:T(...) custom-call(f32[256,1024]{1,0:T(8,128)} %get-tuple-element.150.x_ref, ...), custom_call_target="tpu_custom_call" | custom-call | flops 3221225472 | bytes 16777216 | tf_op jit(solution)/shard_map/attend_half_kernel/pallas_call | solution.py:195
  185.5 3.3 copy.55
  188.8 32.5 %feed_half_kernel.2 = (bf16[1024,1024]{1,0:T(8,128)(2,1)}, bf16[1024,1024]{1,0:T(8,128)(2,1)}, bf16[1024,1024]{1,0:T(8,128)(2,1)}, f32[256,1024]{1,0:T(8,128)S(1)}, f32[256,1024]{1,0:T(8,128)}) custom-call(bf16[256,1024]{1,0:T(8,128)(2,1)S(1)} %copy-done.10, f32[256,1024]{1,0:T(8,128)} %get-tuple-element.67.h_ref, ...), custom_call_target="tpu_custom_call" | custom-call | flops 4294967296 | bytes 16777216 | tf_op jit(solution)/shard_map/feed_half_kernel/pallas_call | solution.py:195
  222.3 2.3 convert_convert_fusion.x_ref
  224.6 44.1 %attend_half_kernel.3 = (bf16[1024,1024]{1,0:T(8,128)(2,1)}, bf16[1024,256]{1,0:T(8,128)(2,1)S(1)}, bf16[1024,256]{1,0:T(8,128)(2,1)S(1)}, bf16[1024,256]{1,0:T(...) custom-call(f32[256,1024]{1,0:T(8,128)} %convert_convert_fusion.x_re, ...), custom_call_target="tpu_custom_call" | custom-call | flops 3221225472 | bytes 16777216 | tf_op jit(solution)/shard_map/attend_half_kernel/pallas_call | solution.py:195
  272.2 32.6 %feed_half_kernel.3 = (bf16[1024,1024]{1,0:T(8,128)(2,1)}, bf16[1024,1024]{1,0:T(8,128)(2,1)}, bf16[1024,1024]{1,0:T(8,128)(2,1)}, f32[256,1024]{1,0:T(8,128)S(1)}, f32[256,1024]{1,0:T(8,128)}) custom-call(bf16[256,1024]{1,0:T(8,128)(2,1)S(1)} %copy-done.11, f32[256,1024]{1,0:T(8,128)} %get-tuple-element.70.h_ref, ...), custom_call_target="tpu_custom_call" | custom-call | flops 4294967296 | bytes 16777216 | tf_op jit(solution)/shard_map/feed_half_kernel/pallas_call | solution.py:195
  307.1 3.7 collective-permute-start.8
  310.9 36.3 %feed_back_kernel.2 = (bf16[1024,1024]{1,0:T(8,128)(2,1)}, bf16[1024,1024]{1,0:T(8,128)(2,1)}, f32[1,1024]{1,0:T(1,128)S(1)}, f32[8,1024]{1,0:T(8,128)S(1)}, f32...) custom-call(f32[256,1024]{1,0:T(8,128)} %select_convert_fusion.1.g_ref, f32[256,1024]{1,0:T(8,128)} %copy-done.3, ...), custom_call_target="tpu_custom_call" | custom-call | flops 8589934592 | bytes 16777216 | tf_op jit(solution)/shard_map/feed_back_kernel/pallas_call | solution.py:195
  348.2 47.2 %attend_back_kernel.2 = (bf16[1024,768]{1,0:T(8,128)(2,1)}, bf16[256,1024]{1,0:T(8,128)(2,1)S(1)}, f32[8,1024]{1,0:T(8,128)S(1)}, bf16[256,1024]{1,0:T(8,128)(2,1)S(1)}) custom-call(bf16[256,1024]{1,0:T(8,128)(2,1)S(1)} %get-tuple-element.76.dz_ref, f32[256,1024]{1,0:T(8,128)} %copy-done.13, f32[256,1024]{1,0:T(8,128)} %convert_convert_fusion.x_ref, ...), custom_call_target="tpu_custom_call" | custom-call | flops 6979321856 | bytes 16777216 | tf_op jit(solution)/shard_map/attend_back_kernel/pallas_call | solution.py:195
  396.5 35.8 %feed_back_kernel.3 = (bf16[1024,1024]{1,0:T(8,128)(2,1)}, bf16[1024,1024]{1,0:T(8,128)(2,1)}, f32[1,1024]{1,0:T(1,128)S(1)}, f32[8,1024]{1,0:T(8,128)S(1)}, f32...) custom-call(f32[256,1024]{1,0:T(8,128)} %convert_element_type.105.g_ref, f32[256,1024]{1,0:T(8,128)} %copy-done.2, ...), custom_call_target="tpu_custom_call" | custom-call | flops 8589934592 | bytes 16777216 | tf_op jit(solution)/shard_map/feed_back_kernel/pallas_call | solution.py:195
  433.2 47.2 %attend_back_kernel.3 = (bf16[1024,768]{1,0:T(8,128)(2,1)}, bf16[256,1024]{1,0:T(8,128)(2,1)S(1)}, f32[8,1024]{1,0:T(8,128)S(1)}, bf16[256,1024]{1,0:T(8,128)(2,1)S(1)}) custom-call(bf16[256,1024]{1,0:T(8,128)(2,1)S(1)} %get-tuple-element.90.dz_ref, f32[256,1024]{1,0:T(8,128)} %copy-done.12, f32[256,1024]{1,0:T(8,128)} %get-tuple-element.150.x_ref, ...), custom_call_target="tpu_custom_call" | custom-call | flops 6979321856 | bytes 16777216 | tf_op jit(solution)/shard_map/attend_back_kernel/pallas_call | solution.py:195
  480.4 177.1 %sum_gradients_kernel.2 = (bf16[1024,768]{1,0:T(8,128)(2,1)}, bf16[4,256,256]{2,1,0:T(8,128)(2,1)S(1)}, bf16[1024,1024]{1,0:T(8,128)(2,1)}, bf16[4,1024,256]{2,1,0:T(8,128)(2,1)}, f32[16,256]{1,0:T(8,128)S(1)}) custom-call(bf16[1024,768]{1,0:T(8,128)(2,1)} %get-tuple-element.100.qkv_ref, bf16[256,1024]{1,0:T(8,128)(2,1)S(1)} %get-tuple-element.101.out_ref, ...), custom_call_target="tpu_custom_call" | custom-call | bytes 16777216 | tf_op jit(solution)/shard_map/sum_gradients_kernel/pallas_call | solution.py:195
  658.9 194.8 %sum_gradients_kernel.3 = (bf16[1024,768]{1,0:T(8,128)(2,1)}, bf16[4,256,256]{2,1,0:T(8,128)(2,1)S(1)}, bf16[1024,1024]{1,0:T(8,128)(2,1)}, bf16[4,1024,256]{2,1,0:T(8,128)(2,1)}, f32[16,256]{1,0:T(8,128)S(1)}) custom-call(bf16[1024,768]{1,0:T(8,128)(2,1)} %get-tuple-element.108.qkv_ref, bf16[256,1024]{1,0:T(8,128)(2,1)S(1)} %get-tuple-element.109.out_ref, ...), custom_call_target="tpu_custom_call" | custom-call | bytes 16777216 | tf_op jit(solution)/shard_map/sum_gradients_kernel/pallas_call | solution.py:195
  857.0 3.5 maximum_convert_fusion.2
  861.3 4.2 maximum_convert_fusion
  865.5 3.9 maximum_convert_fusion.1
  (134 shorter events, 51.2 us)
Async XLA Ops:
  0.6 34.0 %copy-start = (s32[4,2,3]{0,1,2:T(2,128)S(1)}, s32[4,2,3]{0,1,2:T(2,128)}, u32[]{:S(2)}) copy-start(s32[4,2,3]{0,1,2:T(2,128)} %param.16) | copy-start | bytes 292
  2.5 104.5 %collective-permute-start.2 = (bf16[256,1024]{1,0:T(8,128)(2,1)}, bf16[256,1024]{1,0:T(8,128)(2,1)}, u32[]{:S(2)}, u32[]{:S(2)}) collective-permute-start(bf16[256,1024]{1,0:T(8,128)(2,1)} %slice.95), channel_id=1, source_target_pairs={{0,24},{4,28},{8,16},{12,20},{1,25},{5,29},{9,17},{13,21},{2,26},{... | collective-permute-start | bytes 1572872 | tf_op jit(solution)/shard_map/ppermute | solution.py:1037
  12.5 56.6 %all-to-all-start = ((bf16[4,256,256]{2,1,0:T(8,128)(2,1)}), bf16[4,256,256]{2,1,0:T(8,128)(2,1)S(1)}, u32[]{:S(2)}, u32[]{:S(2)}) async-start(bf16[4,256,256]{2,1,0:T(8,128)(2,1)} %bitcast.19), calls=%async_computation | async-start | bytes 1048576 | tf_op jit(solution)/shard_map/all_to_all | solution.py:961
  18.1 3.5 copy-start.31
  19.2 98.0 %collective-permute-start.5 = (bf16[1024,256]{1,0:T(8,128)(2,1)}, bf16[1024,256]{1,0:T(8,128)(2,1)}, u32[]{:S(2)}, u32[]{:S(2)}) collective-permute-start(bf16[1024,256]{1,0:T(8,128)(2,1)} %get-tuple-element.135), channel_id=1, source_target_pairs={{0,1},{1,0},{2,3},{3,2},{4,5},{5,4},{6,7},{7,6},{8,9},{9,8},{10,11... | collective-permute-start | bytes 1572872 | tf_op jit(solution)/shard_map/ppermute | solution.py:929
  27.0 91.8 %collective-permute-start.6 = (bf16[1024,256]{1,0:T(8,128)(2,1)}, bf16[1024,256]{1,0:T(8,128)(2,1)}, u32[]{:S(2)}, u32[]{:S(2)}) collective-permute-start(bf16[1024,256]{1,0:T(8,128)(2,1)} %get-tuple-element.134), channel_id=1, source_target_pairs={{0,2},{1,3},{2,0},{3,1},{4,6},{5,7},{6,4},{7,5},{8,10},{9,11},{10,... | collective-permute-start | bytes 1572872 | tf_op jit(solution)/shard_map/ppermute | solution.py:929
  29.7 90.6 %collective-permute-start.3 = (bf16[1024,256]{1,0:T(8,128)(2,1)}, bf16[1024,256]{1,0:T(8,128)(2,1)}, u32[]{:S(2)}, u32[]{:S(2)}) collective-permute-start(bf16[1024,256]{1,0:T(8,128)(2,1)} %get-tuple-element.144), channel_id=1, source_target_pairs={{0,1},{1,0},{2,3},{3,2},{4,5},{5,4},{6,7},{7,6},{8,9},{9,8},{10,11... | collective-permute-start | bytes 1572872 | tf_op jit(solution)/shard_map/ppermute | solution.py:929
  29.7 2.6 copy-start.14
  31.0 89.3 %collective-permute-start.4 = (bf16[1024,256]{1,0:T(8,128)(2,1)}, bf16[1024,256]{1,0:T(8,128)(2,1)}, u32[]{:S(2)}, u32[]{:S(2)}) collective-permute-start(bf16[1024,256]{1,0:T(8,128)(2,1)} %get-tuple-element.143), channel_id=1, source_target_pairs={{0,2},{1,3},{2,0},{3,1},{4,6},{5,7},{6,4},{7,5},{8,10},{9,11},{10,... | collective-permute-start | bytes 1572872 | tf_op jit(solution)/shard_map/ppermute | solution.py:929
  69.1 12.3 %copy-start.15 = (bf16[4,256,256]{2,1,0:T(8,128)(2,1)}, bf16[4,256,256]{2,1,0:T(8,128)(2,1)S(1)}, u32[]{:S(2)}) copy-start(bf16[4,256,256]{2,1,0:T(8,128)(2,1)S(1)} %all-to-all-done) | copy-start | bytes 1572868
  69.2 12.3 %all-to-all-start.2 = ((bf16[4,256,256]{2,1,0:T(8,128)(2,1)}), bf16[4,256,256]{2,1,0:T(8,128)(2,1)S(1)}, u32[]{:S(2)}, u32[]{:S(2)}) async-start(bf16[4,256,256]{2,1,0:T(8,128)(2,1)} %bitcast.36), calls=%async_computation.2 | async-start | bytes 1048576 | tf_op jit(solution)/shard_map/all_to_all | solution.py:961
  82.3 29.3 %all-to-all-start.1 = ((bf16[4,1024,256]{2,1,0:T(8,128)(2,1)}), bf16[4,1024,256]{2,1,0:T(8,128)(2,1)S(1)}, u32[]{:S(2)}, u32[]{:S(2)}) async-start(bf16[4,1024,256]{2,1,0:T(8,128)(2,1)} %bitcast.108), calls=%async_computation.1 | async-start | bytes 4194304 | tf_op jit(solution)/shard_map/all_to_all | solution.py:961
  101.7 3.5 copy-start.16
  101.7 4.4 copy-start.18
  107.0 75.8 %collective-permute-start.1 = (bf16[256,1024]{1,0:T(8,128)(2,1)}, bf16[256,1024]{1,0:T(8,128)(2,1)}, u32[]{:S(2)}, u32[]{:S(2)}) collective-permute-start(bf16[256,1024]{1,0:T(8,128)(2,1)} %slice.95), channel_id=1, source_target_pairs={{16,24},{20,28},{24,16},{28,20},{17,25},{21,29},{25,17},{29,21},{1... | collective-permute-start | bytes 1572872 | tf_op jit(solution)/shard_map/ppermute | solution.py:1037
  111.6 4.6 copy-start.27
  111.6 74.0 %all-to-all-start.3 = ((bf16[4,1024,256]{2,1,0:T(8,128)(2,1)}), bf16[4,1024,256]{2,1,0:T(8,128)(2,1)}, u32[]{:S(2)}, u32[]{:S(2)}) async-start(bf16[4,1024,256]{2,1,0:T(8,128)(2,1)} %bitcast.107), calls=%async_computation.3 | async-start | bytes 4194304 | tf_op jit(solution)/shard_map/all_to_all | solution.py:961
  116.2 2.7 copy-start.23
  117.2 3.0 copy-start.24
  117.3 65.6 %collective-permute-start = (bf16[256,1024]{1,0:T(8,128)(2,1)S(1)}, bf16[256,1024]{1,0:T(8,128)(2,1)S(1)}, u32[]{:S(2)}, u32[]{:S(2)}) collective-permute-start(bf16[256,1024]{1,0:T(8,128)(2,1)S(1)} %get-tuple-element.151), channel_id=1, source_target_pairs={{16,0},{20,4},{24,8},{28,12},{17,1},{21,5},{25,9},{29,13},{18,2},{... | collective-permute-start | bytes 1572872 | tf_op jit(solution)/shard_map/ppermute | solution.py:1037
  185.5 3.3 copy-start.10
  304.8 6.1 copy-start.3
  306.4 563.0 %collective-permute-start.9 = (bf16[256,1024]{1,0:T(8,128)(2,1)S(1)}, bf16[256,1024]{1,0:T(8,128)(2,1)S(1)}, u32[]{:S(2)}, u32[]{:S(2)}) collective-permute-start(bf16[256,1024]{1,0:T(8,128)(2,1)S(1)} %convert_element_type.106), channel_id=1, source_target_pairs={{24,16},{28,20},{16,24},{20,28},{25,17},{29,21},{17,25},{21,29},{2... | collective-permute-start | bytes 1572872 | tf_op jit(solution)/shard_map/ppermute | solution.py:1037
  307.1 562.3 %collective-permute-start.8 = (bf16[256,1024]{1,0:T(8,128)(2,1)S(1)}, bf16[256,1024]{1,0:T(8,128)(2,1)S(1)}, u32[]{:S(2)}, u32[]{:S(2)}) collective-permute-start(bf16[256,1024]{1,0:T(8,128)(2,1)S(1)} %convert_element_type.106), channel_id=1, source_target_pairs={{0,16},{4,20},{8,24},{12,28},{1,17},{5,21},{9,25},{13,29},{2,18},{... | collective-permute-start | bytes 1572872 | tf_op jit(solution)/shard_map/ppermute | solution.py:1037
  657.6 211.9 %collective-permute-start.7 = (bf16[256,1024]{1,0:T(8,128)(2,1)S(1)}, bf16[256,1024]{1,0:T(8,128)(2,1)S(1)}, u32[]{:S(2)}, u32[]{:S(2)}) collective-permute-start(bf16[256,1024]{1,0:T(8,128)(2,1)S(1)} %get-tuple-element.98), channel_id=1, source_target_pairs={{24,0},{28,4},{16,8},{20,12},{25,1},{29,5},{17,9},{21,13},{26,2},{... | collective-permute-start | bytes 1572872 | tf_op jit(solution)/shard_map/ppermute | solution.py:1037
  853.7 3.3 copy-start.25
  853.7 3.3 copy-start.26
  857.0 3.5 copy-start.20
  857.0 4.3 copy-start.22
  861.3 4.2 copy-start.19
  861.3 4.2 copy-start.21
  865.5 5.4 copy-start.1
  (15 other events, 16.6 us)

commit v3 on v2

--- a/solution.py
+++ b/solution.py
@@ -48,7 +48,7 @@
 
 
 MESH = pl.DeviceIdType.MESH
-SEMAPHORES = 160
+SEMAPHORES = 400
 
 
 def layer_norm_back(values, grad, gain_row):
@@ -67,6 +67,47 @@
     )
 
 
+class Copy:
+    def __init__(self, wire, source, target, peer, when):
+        self.when = when
+        self.pieces = (source, target, wire.sems.at[wire.used], wire.sems.at[wire.used + 1], peer)
+        wire.used += 2
+        wire.made.append(self)
+
+    def remote(self, source=None):
+        own, target, send_sem, recv_sem, peer = self.pieces
+        return pltpu.make_async_remote_copy(
+            src_ref=own if source is None else source,
+            dst_ref=target,
+            send_sem=send_sem,
+            recv_sem=recv_sem,
+            device_id=peer if isinstance(peer, dict) else {"narrow": peer},
+            device_id_type=MESH,
+        )
+
+    def start(self):
+        self.remote().start()
+
+    def start_from(self, source):
+        self.remote(source).start()
+
+    def wait_recv(self):
+        self.remote().wait_recv()
+
+    def wait_send_early(self, others):
+        self.when = others
+        self.remote().wait_send()
+
+    def wait_send(self):
+        if self.when is None:
+            self.remote().wait_send()
+        else:
+
+            @pl.when(self.when)
+            def _():
+                self.remote().wait_send()
+
+
 class Wire:
     def __init__(self, sems):
         self.sems, self.used, self.made = sems, 0, []
@@ -81,18 +122,8 @@
             pl.semaphore_signal(barrier, inc=1, device_id={"narrow": peer}, device_id_type=MESH)
         pl.semaphore_wait(barrier, 2)
 
-    def copy(self, source, target, peer):
-        made = pltpu.make_async_remote_copy(
-            src_ref=source,
-            dst_ref=target,
-            send_sem=self.sems.at[self.used],
-            recv_sem=self.sems.at[self.used + 1],
-            device_id=peer if isinstance(peer, dict) else {"narrow": peer},
-            device_id_type=MESH,
-        )
-        self.used += 2
-        self.made.append(made)
-        return made
+    def copy(self, source, target, peer, when=None):
+        return Copy(self, source, target, peer, when)
 
     def send(self, source, target, peer):
         made = self.copy(source, target, peer)
@@ -206,14 +237,73 @@
     )(*operands)
 
 
-def attend_half_kernel(
+class Background:
+    def __init__(self, number=None, operands=(), outs=(), scratch=(), steps=None, quad=False, across=False):
+        self.number, self.operands, self.outs = number, list(operands), list(outs)
+        self.scratch, self.steps, self.quad, self.across = list(scratch), steps, quad, across
+
+
+def call_with(body, background, outs, scratch, flops, *operands):
+    counts = [
+        len(operands), len(background.operands), len(outs), len(background.outs),
+        len(scratch), len(background.scratch),
+    ]
+
+    def kernel(*refs):
+        refs, groups = list(refs), []
+        for count in counts:
+            groups.append(refs[:count])
+            refs = refs[count:]
+        wire = Wire(refs[0])
+        steps = []
+        if background.steps is None:
+            wire.barrier()
+        else:
+            if background.quad:
+                place = Quad()
+                quad_barrier(wire, place, *([place.across] if background.across else []))
+            else:
+                place = Line()
+                wide_barrier(wire, place)
+            steps = [background.steps(wire, place, groups[1], groups[3], groups[5])]
+
+        def poll(times=1):
+            for _ in range(times):
+                for step in list(steps):
+                    if next(step, "end") == "end":
+                        steps.remove(step)
+
+        body(wire, poll, *groups[0], *groups[2], *groups[4])
+        while steps:
+            poll()
+        wire.finish()
+
+    kernel.__name__ = body.__name__ if background.steps is None else body.__name__ + "_wide"
+    place = anywhere if background.quad else vmem
+    results = pl.pallas_call(
+        kernel,
+        in_specs=vmem(len(operands)) + place(len(background.operands)),
+        out_specs=vmem(len(outs)) + place(len(background.outs)),
+        out_shape=shaped(*outs, *background.outs),
+        scratch_shapes=list(scratch)
+        + background.scratch
+        + [pltpu.SemaphoreType.DMA((SEMAPHORES,))],
+        compiler_params=pltpu.CompilerParams(
+            collective_id=background.number, has_side_effects=True, vmem_limit_bytes=52 * 2**20
+        ),
+        cost_estimate=pl.CostEstimate(flops=flops, bytes_accessed=2**24, transcendentals=0),
+        name=kernel.__name__,
+    )(*operands, *background.operands)
+    return results[: len(outs)], results[len(outs) :]
+
+
+def attend_half_body(
+    wire, poll,
     x_ref, gain_ref, shift_ref, cos_ref, sin_ref, start_ref, w_qkv_ref, w_out_ref,
     a_ref, q_ref, k_ref, v_ref, o_ref, lse_ref, z_ref, h_ref, c_ref,
-    held, own, sems,
+    held, own,
 ):
     size = x_ref.shape[0]
-    wire = Wire(sems)
-    wire.barrier()
     gather = Gather(wire, a_ref, size)
     for part in range(2):
         rows = pl.ds(part * (size // 2), size // 2)
@@ -230,6 +320,7 @@
         k_ref[rows] = turn(projected[:, width : 2 * width], cosine, sine).astype(BF16)
         v_ref[rows] = projected[:, 2 * width :].astype(BF16)
 
+    poll()
     project(wire.at)
     gather.wait_near()
     project(wire.near)
@@ -240,6 +331,7 @@
     gather.wait_diagonal(1)
     project(wire.diagonal)
 
+    poll()
     scatter = Scatter(wire, held, own, 1)
     for block in (3, 1, 2, 0):
         rows = slice(block * size, (block + 1) * size)
@@ -263,6 +355,9 @@
         lse_ref[:, rows] = logs.T[: lse_ref.shape[0]]
         partial = dot(o_ref[rows, :], w_out_ref[...])
 
+        if block in (1, 2):
+            poll()
+
         @pl.when(wire.diagonal == block)
         def _():
             scatter.put_diagonal(partial, 0)
@@ -284,15 +379,14 @@
     middle = x_ref[...] + layer_norm(branch, gain_ref[1:2], shift_ref[1:2])
     h_ref[...] = middle
     c_ref[...] = layer_norm(middle, gain_ref[2:3], shift_ref[2:3]).astype(BF16)
-    wire.finish()
-
-
-def attend_half(resid, gains, shifts, cosine, sine, start, w_qkv, w_out):
+
+
+def attend_half(background, resid, gains, shifts, cosine, sine, start, w_qkv, w_out):
     size, width = resid.shape
     length, part = cosine.shape[0], w_out.shape[0]
-    return call(
-        attend_half_kernel,
-        1,
+    return call_with(
+        attend_half_body,
+        background,
         [((length, width), BF16)]
         + [((length, part), BF16)] * 4
         + [((8, length), F32), ((size, width), F32), ((size, width), F32), ((size, width), BF16)],
@@ -362,15 +456,14 @@
     )
 
 
-def feed_back_kernel(
+def feed_back_body(
+    wire, poll,
     g_ref, w_ref, h_ref, z_ref, gain_ref, inner_ref, e_ref, d_ref, w_up_ref, w_down_ref,
     grad_down_ref, grad_up_ref, grad_b_ref, norms_ref, dh_ref, dz_ref,
-    second, hidden, held, own, sems,
+    second, hidden, held, own,
 ):
     size = g_ref.shape[0]
     half = size // 2
-    wire = Wire(sems)
-    wire.barrier()
     gather = Gather(wire, second, size)
     norms = [jnp.zeros((1, g_ref.shape[1]), F32)] * 2
     for part in range(2):
@@ -384,6 +477,7 @@
     norms_ref[0:1] = jnp.zeros_like(norms[0])
     norms_ref[4:5] = jnp.zeros_like(norms[0])
     scatter = Scatter(wire, held, own, 2)
+    poll()
 
     def feed(cuts, first=False):
         grad = jnp.concatenate([second[cut] for cut in cuts])
@@ -397,9 +491,12 @@
         return dot_t(grad, w_up_ref[...])
 
     own[...] = feed([block_rows(wire.at, size)], True)
+    poll()
     gather.wait_near()
     scatter.put_near(feed([block_rows(wire.near, size)]))
+    poll()
     for part in range(2):
+        poll(2)
         gather.relay(part)
         gather.wait_diagonal(part)
         partial = feed(
@@ -407,12 +504,16 @@
         )
         scatter.put_diagonal(partial[:half], part)
         scatter.put_far(partial[half:], part)
+        poll()
     for at in range(0, e_ref.shape[1], 256):
         cut = slice(at, at + 256)
         grad_down_ref[cut, :] = t_dot(e_ref[:, cut], second[...]).astype(BF16)
+        poll()
     for at in range(0, inner_ref.shape[1], 256):
         cut = slice(at, at + 256)
         grad_up_ref[cut, :] = t_dot(inner_ref[:, cut], hidden[...]).astype(BF16)
+        poll()
+    poll(3)
     grad, gain, shift = layer_norm_back(h_ref[...], scatter.total(), gain_ref[2:3])
     norms_ref[2:3] = gain
     norms_ref[6:7] = shift
@@ -422,15 +523,14 @@
     norms_ref[1:2] = gain
     norms_ref[5:6] = shift
     dz_ref[...] = grad.astype(BF16)
-    wire.finish()
-
-
-def feed_back(grad, second, middle, branch, gains, inner, active, slope, w_up, w_down):
+
+
+def feed_back(background, grad, second, middle, branch, gains, inner, active, slope, w_up, w_down):
     size, width = grad.shape
     length, hidden = 4 * size, w_up.shape[1]
-    return call(
-        feed_back_kernel,
-        3,
+    return call_with(
+        feed_back_body,
+        background,
         [
             ((hidden, width), BF16),
             ((width, hidden), BF16),
@@ -450,17 +550,16 @@
     )
 
 
-def attend_back_kernel(
+def attend_back_body(
+    wire, poll,
     dz_ref, dh_ref, x_ref, gain_ref, a_ref, q_ref, k_ref, v_ref, o_ref, lse_ref, start_ref,
     cos_ref, sin_ref, w_qkv_ref, w_out_ref,
     grad_qkv_ref, grad_out_ref, norms_ref, dx_ref,
-    branch, mixture, projected, dk, dv, held, own, sems,
+    branch, mixture, projected, dk, dv, held, own,
 ):
     size = dz_ref.shape[0]
     length, width = q_ref.shape
     half = size // 2
-    wire = Wire(sems)
-    wire.barrier()
     gather = Gather(wire, branch, size)
     for part in range(2):
         branch[block_rows(wire.at, size, part, 2)] = dz_ref[pl.ds(part * half, half)]
@@ -472,16 +571,21 @@
 
     dk[...] = jnp.zeros_like(dk)
     dv[...] = jnp.zeros_like(dv)
+    poll()
     unmix(wire.at)
     gather.wait_near()
     unmix(wire.near)
+    poll()
+    poll(2)
     gather.relay(0)
+    poll(2)
     gather.relay(1)
     unmix(wire.far)
     gather.wait_diagonal(0)
     gather.wait_diagonal(1)
     unmix(wire.diagonal)
     grad_out_ref[...] = t_dot(o_ref[...], branch[...]).astype(BF16)
+    poll()
 
     pick_head = (
         lax.broadcasted_iota(jnp.int32, (8, width), 1) // HD
@@ -512,6 +616,8 @@
             dvs.append(dot(chances.astype(BF16), g_head))
             dks.append(dot(grad_score, q_head))
             dqs.append(t_dot(grad_score, k_head) * SCALE)
+            if block > 0 and head % 2 == 1:
+                poll()
         dq = jnp.concatenate(dqs, axis=1)
         projected[rows, :width] = turn(dq, cos_ref[rows], -sin_ref[rows]).astype(BF16)
         dk[:reach, :] += jnp.concatenate(dks, axis=1)
@@ -530,31 +636,35 @@
     partial = unproject(block_rows(wire.diagonal, size))
     scatter.put_diagonal(partial[:half], 0)
     scatter.put_diagonal(partial[half:], 1)
+    poll()
     partial = unproject(block_rows(wire.far, size))
     scatter.put_far(partial[:half], 0)
     scatter.put_far(partial[half:], 1)
+    poll()
     scatter.put_near(unproject(block_rows(wire.near, size)))
     own[...] = unproject(block_rows(wire.at, size))
     for at in range(0, a_ref.shape[1], 256):
         cut = slice(at, at + 256)
         grad_qkv_ref[cut, :] = t_dot(a_ref[:, cut], projected[...]).astype(BF16)
+        poll()
+    poll(3)
     grad, gain, shift = layer_norm_back(x_ref[...], scatter.total(), gain_ref[0:1])
     norms_ref[...] = jnp.zeros_like(norms_ref)
     norms_ref[0:1] = gain
     norms_ref[4:5] = shift
     dx_ref[...] = (dh_ref[...] + grad).astype(BF16)
-    wire.finish()
 
 
 def attend_back(
+    background,
     grad_branch, grad_middle, resid, gains, normed, query, keys, values, mixture, logs, start,
     cosine, sine, w_qkv, w_out,
 ):
     size, width = resid.shape
     length, part = query.shape
-    return call(
-        attend_back_kernel,
-        4,
+    return call_with(
+        attend_back_body,
+        background,
         [
             ((width, 3 * part), BF16),
             ((part, width), BF16),
@@ -576,217 +686,244 @@
     )
 
 
-class Ring:
+CHUNK = 64
+LATE = 2
+
+
+class Line:
     def __init__(self):
         at = lax.axis_index("wide")
         self.pair = lax.rem(at, 2)
         self.turn = at // 2
+        self.upper = self.turn // 3
         self.up = {"wide": lax.rem(self.turn + 1, 4) * 2 + self.pair}
         self.down = {"wide": lax.rem(self.turn + 3, 4) * 2 + self.pair}
         self.side = {"wide": at + 1 - 2 * self.pair}
+        self.bottom, self.top = self.turn == 0, self.turn == 3
+        self.at_end = self.upper * 3 == self.turn
+        self.inside = jnp.logical_not(self.at_end)
+        not_bottom, not_top = self.turn > 0, self.turn < 3
+        self.ways = (
+            (self.up, self.bottom, self.top, not_bottom, not_top),
+            (self.down, self.top, self.bottom, not_top, not_bottom),
+        )
+
+    def steps(self, chunks):
+        for at in range(len(chunks) + 3 * LATE):
+            for turn in range(4):
+
+                @pl.when(self.turn == turn)
+                def _():
+                    for way, hops in sorted(((0, turn), (1, 3 - turn)), key=lambda item: item[1]):
+                        chunk = at - hops * LATE
+                        if not 0 <= chunk < len(chunks):
+                            continue
+                        if hops == 0:
+                            if chunk >= 2:
+                                chunks[chunk - 2](way, "sent")
+                            chunks[chunk](way, "first")
+                        else:
+                            chunks[chunk](way, "last" if hops == 3 else "inner")
+
+            yield
 
 
 def span(start, size):
     return pl.ds(pl.multiple_of(start, 16), size)
 
 
-class Piece:
-    def __init__(self, view, rows, by_side, ring):
-        self.view, self.rows, self.by_side = view, rows, by_side
-        self.eighth = rows // 8
-        pair, turn = ring.pair, ring.turn
-        if by_side:
-            self.mine = pair * (rows // 2) + turn * self.eighth
-            self.joined, self.joined_size = pair * (rows // 2), rows // 2
-        else:
-            self.mine = turn * (rows // 4) + pair * self.eighth
-            self.joined, self.joined_size = turn * (rows // 4), rows // 4
-
-    def own(self):
-        return self.view(span(self.mine, self.eighth))
-
-    def whole(self):
-        return self.view(span(self.joined, self.joined_size))
-
-    def around(self, ring, step, half):
-        size = self.eighth if self.by_side else self.joined_size
-        start = self.joined if self.by_side else 0
-        other = lax.rem(ring.turn + step, 4) * size + start
-        return self.view(span(other + half * (size // 2), size // 2))
-
-
-def spread_steps(wire, ring, pieces):
-    def both_ways(piece, part):
-        return (
-            wire.send(part, part, ring.up),
-            wire.send(part, part, ring.down),
-        )
-
-    def onwards(piece, sent):
-        sent[0].wait_recv()
-        first = piece.around(ring, 3, 0)
-        up = wire.send(first, first, ring.up)
-        sent[1].wait_recv()
-        second = piece.around(ring, 1, 1)
-        return up, wire.send(second, second, ring.down)
-
-    by_side = [piece for piece in pieces if piece.by_side]
-    others = [piece for piece in pieces if not piece.by_side]
-    sent = [both_ways(piece, piece.own()) for piece in by_side]
-    across = [wire.send(piece.own(), piece.own(), ring.side) for piece in others]
-    yield
-    relayed = [onwards(piece, pair) for piece, pair in zip(by_side, sent)]
-    for made in across:
-        made.wait_recv()
-    sent = [both_ways(piece, piece.whole()) for piece in others]
-    yield
-    for pair in relayed:
-        for made in pair:
-            made.wait_recv()
-    across = [wire.send(piece.whole(), piece.whole(), ring.side) for piece in by_side]
-    relayed = [onwards(piece, pair) for piece, pair in zip(others, sent)]
-    yield
-    for made in across:
-        made.wait_recv()
-    for pair in relayed:
-        for made in pair:
-            made.wait_recv()
-
-
-def add_rows(target, rows, *sources):
-    step = min(rows, 128)
-    for at in range(0, rows, step):
-        cut = pl.ds(at, step)
-        total = sources[0](at, step).astype(F32)
-        for source in sources[1:]:
-            total = total + source(at, step).astype(F32)
-        target[cut] = total.astype(BF16)
-
-
-def part_of(ref, start=0):
-    return lambda at, step: ref[span(start + at, step)]
-
-
-def slot_of(ref, slot, start=0):
-    return lambda at, step: ref[slot, span(start + at, step)]
-
-
 class Fold:
-    def __init__(self, wire, ring, ref, by_side, scratch):
-        self.wire, self.ring, self.ref, self.by_side = wire, ring, ref, by_side
-        self.joined, self.across, self.early, self.out, self.into, self.final = scratch
-        self.rows = ref.shape[0]
-        self.size = self.rows // 8 if by_side else self.rows // 4
+    def __init__(self, wire, line, ref, by_side, into, across, final):
+        self.wire, self.line, self.ref, self.by_side = wire, line, ref, by_side
+        self.into, self.across, self.final = into, across, final
+        rows = ref.shape[0]
+        self.length = rows // 4 if by_side else rows // 2
+        self.base = line.pair * (rows // 2) if by_side else 0
+        self.count = self.length // CHUNK
+        self.copies, self.sides = [], []
+        for way, (peer, _, _, _, inner) in enumerate(line.ways):
+            cuts = [into.at[way, pl.ds(c * CHUNK, CHUNK)] for c in range(self.count)]
+            self.copies.append([wire.copy(cut, cut, peer, inner) for cut in cuts])
 
     @staticmethod
     def scratch(rows, columns, by_side):
-        size = rows // 8 if by_side else rows // 4
-        joined = rows // 2 if by_side else rows // 4
-        across = rows // 2 if by_side else rows // 8
         return [
-            pltpu.VMEM((joined, columns), BF16),
-            pltpu.VMEM((across, columns), BF16),
-            pltpu.VMEM((2, size // 2, columns), BF16),
-            pltpu.VMEM((2, size, columns), BF16),
-            pltpu.VMEM((2, size, columns), BF16),
-            pltpu.VMEM((rows // 8, columns), BF16),
+            pltpu.VMEM((2, rows // 4 if by_side else rows // 2, columns), BF16),
+            pltpu.VMEM((rows // 2 if by_side else rows // 4, columns), BF16),
         ]
 
-    def source(self):
-        return self.joined if self.by_side else self.ref
-
-    def part(self, step):
-        return lax.rem(self.ring.turn + step, 4) * self.size
+    def place(self, way, chunk):
+        return (self.length if way == 0 else 0) + chunk * CHUNK
+
+    def start(self):
+        line = self.line
+        if self.by_side:
+            away = (1 - line.pair) * (self.ref.shape[0] // 2)
+            for chunk in range(self.count):
+                pair = []
+                for way in (0, 1):
+                    place = self.place(way, chunk)
+                    pair.append(
+                        self.wire.send(
+                            self.ref.at[span(away + place, CHUNK)],
+                            self.across.at[pl.ds(place, CHUNK)],
+                            line.side,
+                        )
+                    )
+                self.sides.append(pair)
+
+    def step(self, chunk, way, role):
+        place = self.place(way, chunk)
+        cut = pl.ds(chunk * CHUNK, CHUNK)
+        made = self.copies[way][chunk]
+        if role == "sent":
+            made.wait_send_early(self.line.inside)
+            return
+        if self.by_side:
+            self.sides[chunk][way].wait_recv()
+
+        def own():
+            total = self.ref[span(self.base + place, CHUNK)].astype(F32)
+            if self.by_side:
+                total = total + self.across[pl.ds(place, CHUNK)].astype(F32)
+            return total
+
+        if role == "first":
+            if self.by_side:
+                self.into[way, cut] = own().astype(BF16)
+                made.start()
+            else:
+                made.start_from(self.ref.at[pl.ds(place, CHUNK)])
+            return
+        made.wait_recv()
+        self.into[way, cut] = (own() + self.into[way, cut].astype(F32)).astype(BF16)
+        if role == "inner":
+            made.start()
+
+    def chunks(self):
+        return [functools.partial(self.step, chunk) for chunk in range(self.count)]
 
     def start_side(self):
-        pair = self.ring.pair
+        line = self.line
+        half = self.length // 2
+        source = self.into.at[1 - line.upper, span((1 - line.pair) * half, half)]
+        self.side = self.wire.copy(source, self.across, line.side, line.at_end)
+
+        @pl.when(line.at_end)
+        def _():
+            self.side.start()
+
+    def end(self):
+        line = self.line
+        size = self.final.shape[0]
+
+        @pl.when(line.at_end)
+        def _():
+            if not self.by_side:
+                self.side.wait_recv()
+            for at in range(0, size, CHUNK):
+                if self.by_side:
+                    self.final[pl.ds(at, CHUNK)] = self.into[1 - line.upper, pl.ds(at, CHUNK)]
+                else:
+                    own = self.into[1 - line.upper, span(line.pair * size + at, CHUNK)]
+                    total = own.astype(F32) + self.across[pl.ds(at, CHUNK)].astype(F32)
+                    self.final[pl.ds(at, CHUNK)] = total.astype(BF16)
+
+
+class Spread:
+    def __init__(self, wire, line, view, rows, by_side):
+        self.wire, self.line, self.view, self.by_side = wire, line, view, by_side
+        pair, upper = line.pair, line.upper
+        self.quarter = rows // 4
+        if by_side:
+            self.length, self.base = rows // 4, pair * (rows // 2)
+            self.mine = self.base + upper * self.quarter
+        else:
+            self.length, self.base = rows // 2, 0
+            self.mine = upper * (rows // 2) + pair * self.quarter
+        self.count = self.length // CHUNK
+        self.copies = []
+        for way, (peer, _, _, _, inner) in enumerate(line.ways):
+            cuts = [self.chunk(way, c) for c in range(self.count)]
+            self.copies.append([wire.copy(cut, cut, peer, inner) for cut in cuts])
+        self.sides = []
+        if not by_side:
+            self.side = wire.copy(self.own(), self.own(), line.side, line.at_end)
+
+    def own(self):
+        return self.view(span(self.mine, self.quarter))
+
+    def chunk(self, way, chunk):
+        start = self.base + (0 if way == 0 else self.length) + chunk * CHUNK
+        return self.view(span(start, CHUNK))
+
+    def start(self):
+        if not self.by_side:
+
+            @pl.when(self.line.at_end)
+            def _():
+                self.side.start()
+
+    def step(self, chunk, way, role):
+        made = self.copies[way][chunk]
+        if role == "sent":
+            made.wait_send_early(self.line.inside)
+            return
+        if role == "first":
+            if not self.by_side and chunk == 0:
+                self.side.wait_recv()
+            made.start()
+        else:
+            made.wait_recv()
+            if role == "inner":
+                made.start()
         if self.by_side:
-            half = self.rows // 2
-            source = self.ref.at[span((1 - pair) * half, half)]
-        else:
-            half = self.rows // 8
-            source = self.joined.at[span((1 - pair) * half, half)]
-        self.side = self.wire.send(source, self.across, self.ring.side)
-
-    def end_side(self):
-        self.side.wait_recv()
-        pair = self.ring.pair
+            self.sides[chunk][way].start()
+
+    def chunks(self):
         if self.by_side:
-            half = self.rows // 2
-            add_rows(self.joined, half, part_of(self.ref, pair * half), part_of(self.across))
-        else:
-            half = self.rows // 8
-            add_rows(self.final, half, part_of(self.joined, pair * half), part_of(self.across))
-
-    def start_early(self):
-        half = self.size // 2
-        opposite = self.part(2)
-        source = self.source()
-        self.first = [
-            self.wire.send(source.at[span(opposite, half)], self.early.at[0], self.ring.up),
-            self.wire.send(source.at[span(opposite + half, half)], self.early.at[1], self.ring.down),
+            self.sides = []
+            for chunk in range(self.count):
+                cuts = [self.chunk(way, chunk) for way in (0, 1)]
+                self.sides.append([self.wire.copy(cut, cut, self.line.side) for cut in cuts])
+        return [functools.partial(self.step, chunk) for chunk in range(self.count)]
+
+    def end(self):
+        for pair in self.sides:
+            for made in pair:
+                made.wait_recv()
+
+
+class Sequence:
+    def __init__(self, line):
+        self.line, self.chunks, self.actions = line, [], {}
+
+    def add(self, *lists):
+        total = max(len(chunks) for chunks in lists)
+        placed = [
+            ((at + 0.5) * total / len(chunks), which, chunk)
+            for which, chunks in enumerate(lists)
+            for at, chunk in enumerate(chunks)
         ]
-
-    def start_late(self):
-        half = self.size // 2
-        source = self.source()
-        self.second = []
-        for way, (step, peer) in enumerate([(1, self.ring.up), (3, self.ring.down)]):
-            self.first[way].wait_recv()
-            start = self.part(step)
-            out = self.out.at[way]
-            for at in (0, 1):
-                cut = out.at[pl.ds(at * half, half)]
-                if at == way:
-                    add_rows(
-                        cut, half, part_of(source, start + at * half), slot_of(self.early, way)
-                    )
-                else:
-                    cut[...] = source[span(start + at * half, half)]
-            self.second.append(self.wire.send(out, self.into.at[way], peer))
-
-    def end_late(self):
-        for made in self.second:
-            made.wait_recv()
-        target = self.final if self.by_side else self.joined
-        start = self.part(0)
-        add_rows(
-            target,
-            self.size,
-            part_of(self.source(), start),
-            slot_of(self.into, 0),
-            slot_of(self.into, 1),
-        )
-
-
-def fold_steps(folds):
-    by_side = [fold for fold in folds if fold.by_side]
-    others = [fold for fold in folds if not fold.by_side]
-    for fold in others:
-        fold.start_early()
-    for fold in by_side:
-        fold.start_side()
-    yield
-    for fold in others:
-        fold.start_late()
-    yield
-    for fold in by_side:
-        fold.end_side()
-        fold.start_early()
-    yield
-    for fold in others:
-        fold.end_late()
-        fold.start_side()
-    for fold in by_side:
-        fold.start_late()
-    yield
-    for fold in others:
-        fold.end_side()
-    for fold in by_side:
-        fold.end_late()
-
-
-def small_steps(wire, ring, norms_ref, bias_ref, narrow_in, sums, side_in, turn_in, total_ref):
+        self.chunks += [chunk for _, _, chunk in sorted(placed, key=lambda item: item[:2])]
+        return self
+
+    def before_next(self, *actions):
+        self.actions.setdefault(len(self.chunks) - 1, []).extend(actions)
+
+    def after(self, chunk, *actions):
+        self.actions.setdefault(self.chunks.index(chunk) + 3 * LATE, []).extend(actions)
+
+    def steps(self):
+        for action in self.actions.get(-1, []):
+            action()
+        for at, _ in enumerate(self.line.steps(self.chunks)):
+            for action in self.actions.get(at, []):
+                action()
+            yield
+
+
+def small_steps(wire, line, norms_ref, bias_ref, narrow_in, sums, side_in, slots, total_ref):
     part = total_ref.shape[1]
     made = []
 
@@ -804,29 +941,122 @@
     total = narrow_in[0] + narrow_in[1] + narrow_in[2] + narrow_in[3]
     lines = [bias_ref[:, at * part : (at + 1) * part] for at in range(4)]
     sums[...] = jnp.concatenate([total] + lines + [jnp.zeros((4, part), F32)], axis=0)
-    side = wire.send(sums, side_in, ring.side)
+    side = wire.send(sums, side_in, line.side)
     yield
     side.wait_recv()
-    turn_in[ring.turn] = sums[...] + side_in[...]
-    own = turn_in.at[ring.turn]
-    up, down = wire.send(own, own, ring.up), wire.send(own, own, ring.down)
-    yield
-    up.wait_recv()
-    down.wait_recv()
-    below = turn_in.at[lax.rem(ring.turn + 3, 4)]
-    last = wire.send(below, below, ring.up)
-    yield
-    last.wait_recv()
-    total_ref[...] = turn_in[0] + turn_in[1] + turn_in[2] + turn_in[3]
-
-
-def wide_barrier(wire, ring):
+    slots[line.turn] = sums[...] + side_in[...]
+    for step in range(3):
+        sends = []
+        for way, peer in enumerate((line.up, line.down)):
+            place = line.turn if way == 0 else 3 - line.turn
+            goes = (place >= step) & (place < 3)
+            comes = place > step
+            slot = slots.at[lax.rem(line.turn + (4 - step if way == 0 else step), 4)]
+            copy = wire.copy(slot, slot, peer, goes)
+            sends.append((copy, goes, comes))
+
+            @pl.when(goes)
+            def _():
+                copy.start()
+
+        yield
+        for copy, goes, comes in sends:
+
+            @pl.when(comes)
+            def _():
+                copy.wait_recv()
+
+    total_ref[...] = slots[0] + slots[1] + slots[2] + slots[3]
+
+
+def home(wire, line, down, out, qkv, full_down, full_out, full_qkv):
+    part = (full_out if full_down is None else full_down).shape[2]
+    made = []
+    at = wire.at
+
+    def columns(device):
+        return pl.ds(pl.multiple_of(device * part, part), part)
+
+    for final, full, by_side in ((down, full_down, True), (out, full_out, False)):
+        if final is None:
+            continue
+        quarter = final.shape[0]
+        if by_side:
+            mine = line.pair * (2 * quarter) + line.upper * quarter
+        else:
+            mine = line.upper * (2 * quarter) + line.pair * quarter
+        slot = full.at[at, span(mine, quarter)]
+        for peer in (wire.diagonal, wire.far, wire.near):
+            made.append(
+                wire.copy(final.at[:, columns(peer)], slot, {"narrow": peer}, line.at_end)
+            )
+
+        @pl.when(line.at_end)
+        def _():
+            slot[...] = final[:, columns(at)]
+
+    if qkv is not None:
+        quarter = qkv.shape[0]
+        rows = span(line.pair * (2 * quarter) + line.upper * quarter, quarter)
+        odd, upper = lax.rem(at, 2), at // 2
+        far_slot = columns(2 - 2 * odd)
+        made.append(
+            wire.copy(
+                qkv.at[:, columns(2 - 2 * upper)], full_qkv.at[rows, far_slot],
+                {"narrow": wire.far}, line.at_end,
+            )
+        )
+        made.append(
+            wire.copy(
+                qkv.at[:, columns(1 - odd + upper)], full_qkv.at[rows, columns(1)],
+                {"narrow": wire.near}, line.at_end,
+            )
+        )
+
+        @pl.when(line.at_end)
+        def _():
+            full_qkv[rows, columns(2 * odd)] = qkv[:, columns((at + 1) // 2)]
+
+    @pl.when(line.at_end)
+    def _():
+        for copy in made:
+            copy.start()
+
+    def wait():
+        @pl.when(line.at_end)
+        def _():
+            for copy in made:
+                copy.wait_recv()
+
+    return wait
+
+
+def wide_barrier(wire, line, *others):
     barrier = pltpu.get_barrier_semaphore()
-    peers = [ring.up, ring.down, ring.side]
-    peers += [{"narrow": peer} for peer in (wire.near, wire.far, wire.diagonal)]
-    for peer in peers:
+
+    def greet(peer):
         pl.semaphore_signal(barrier, inc=1, device_id=peer, device_id_type=MESH)
-    pl.semaphore_wait(barrier, len(peers))
+
+    for peer in (line.side,) + others:
+        greet(peer)
+    for peer in (wire.near, wire.far, wire.diagonal):
+        greet({"narrow": peer})
+
+    @pl.when(line.turn < 3)
+    def _():
+        greet(line.up)
+
+    @pl.when(line.turn > 0)
+    def _():
+        greet(line.down)
+
+    @pl.when(line.at_end)
+    def _():
+        pl.semaphore_wait(barrier, 5 + len(others))
+
+    @pl.when(line.inside)
+    def _():
+        pl.semaphore_wait(barrier, 6 + len(others))
 
 
 def run(*steps):
@@ -837,91 +1067,417 @@
                 steps.remove(at)
 
 
-def sum_gradients_kernel(
-    qkv_ref, out_ref, up_ref, down_ref, norms_ref, bias_ref,
-    full_qkv, full_out, full_up, full_down, total_ref,
-    *scratch,
-):
-    narrow_in, sums, side_in, turn_in, sems = scratch[24:]
-    wire, ring = Wire(sems), Ring()
-    wide_barrier(wire, ring)
-    down = Fold(wire, ring, down_ref, True, scratch[0:6])
-    out = Fold(wire, ring, out_ref, True, scratch[6:12])
-    up = Fold(wire, ring, up_ref, False, scratch[12:18])
-    qkv = Fold(wire, ring, qkv_ref, False, scratch[18:24])
-    run(
-        fold_steps([down, out, up, qkv]),
-        small_steps(
-            wire, ring, norms_ref, bias_ref, narrow_in, sums, side_in, turn_in, total_ref
-        ),
-    )
-    part = total_ref.shape[1]
-
-    def columns(device):
-        return pl.ds(pl.multiple_of(device * part, part), part)
-
-    pieces = [
-        Piece(lambda rows: full_down.at[:, rows], down_ref.shape[0], True, ring),
-        Piece(lambda rows: full_out.at[:, rows], out_ref.shape[0], True, ring),
-        Piece(lambda rows: full_up.at[rows], up_ref.shape[0], False, ring),
-        Piece(lambda rows: full_qkv.at[rows], qkv_ref.shape[0], False, ring),
+def fold_pair(wire, line, refs, finals, scratch):
+    return (
+        Fold(wire, line, refs[0], False, *scratch[0:2], finals[0]),
+        Fold(wire, line, refs[1], True, *scratch[2:4], finals[1]),
+    )
+
+
+def spread_feed(wire, line, full_up, full_down):
+    return (
+        Spread(wire, line, lambda rows: full_up.at[rows], full_up.shape[0], False),
+        Spread(wire, line, lambda rows: full_down.at[:, rows], full_down.shape[1], True),
+    )
+
+
+def spread_attend(wire, line, full_out, full_qkv):
+    return (
+        Spread(wire, line, lambda rows: full_out.at[:, rows], full_out.shape[1], False),
+        Spread(wire, line, lambda rows: full_qkv.at[rows], full_qkv.shape[0], True),
+    )
+
+
+def place_own(line, spread, final):
+    @pl.when(line.at_end)
+    def _():
+        spread.own()[...] = final[...]
+
+
+def fold_feed_steps(wire, line, refs, outs, scratch):
+    up, down = fold_pair(wire, line, refs, outs, scratch)
+    down.start()
+    sequence = Sequence(line)
+    chunks = up.chunks()
+    sequence.add(chunks).add(down.chunks())
+    sequence.after(chunks[-1], up.start_side)
+    yield from sequence.steps()
+    up.end()
+    down.end()
+
+
+def fold_attend_spread_feed_steps(wire, line, refs, outs, scratch):
+    out, qkv = fold_pair(wire, line, refs[0:2], outs[0:2], scratch)
+    up, down = spread_feed(wire, line, *outs[2:4])
+    place_own(line, up, refs[2])
+    home_wait = home(wire, line, refs[3], None, None, outs[3], None, None)
+    qkv.start()
+    up.start()
+    sequence = Sequence(line)
+    chunks = out.chunks()
+    sequence.add(chunks).before_next(home_wait)
+    sequence.add(down.chunks()).add(up.chunks(), qkv.chunks())
+    sequence.after(chunks[-1], out.start_side)
+    yield from sequence.steps()
+    out.end()
+    qkv.end()
+    down.end()
+
+
+def spread_attend_fold_feed_steps(wire, line, refs, outs, scratch):
+    out, qkv = spread_attend(wire, line, *outs[0:2])
+    up, down = fold_pair(wire, line, refs[2:4], outs[2:4], scratch)
+    home_wait = home(wire, line, None, refs[0], refs[1], None, *outs[0:2])
+    down.start()
+    sequence = Sequence(line)
+    chunks = up.chunks()
+    sequence.add(chunks[:2]).before_next(home_wait, out.start)
+    sequence.add(chunks[2:6], qkv.chunks()).add(chunks[6:], out.chunks()).add(down.chunks())
+    sequence.after(chunks[-1], up.start_side)
+    yield from sequence.steps()
+    up.end()
+    down.end()
+    qkv.end()
+
+
+def tail_steps(wire, line, grads, finals, full_feed, full_attend, own, scratch):
+    out, qkv = fold_pair(wire, line, grads, own, scratch)
+    up, down = spread_feed(wire, line, *full_feed)
+    full_out, full_qkv = spread_attend(wire, line, *full_attend)
+    place_own(line, up, finals[0])
+    home_wait = home(wire, line, finals[1], None, None, full_feed[1], None, None)
+    qkv.start()
+    up.start()
+    waits = []
+
+    def go_home():
+        out.end()
+        qkv.end()
+        waits.append(home(wire, line, None, *own, None, *full_attend))
+
+    sequence = Sequence(line)
+    out_chunks, qkv_chunks = out.chunks(), qkv.chunks()
+    sequence.add(out_chunks).before_next(home_wait)
+    sequence.add(down.chunks()).add(qkv_chunks).add(up.chunks())
+    sequence.before_next(lambda: waits[0](), full_out.start)
+    sequence.add(full_qkv.chunks()).add(full_out.chunks())
+    sequence.after(out_chunks[-1], out.start_side)
+    sequence.after(qkv_chunks[-1], go_home)
+    yield from sequence.steps()
+    down.end()
+    full_qkv.end()
+
+
+def fold_outs(blocks):
+    return [((block.shape[0] // 4, block.shape[1]), BF16) for block in blocks]
+
+
+def fold_scratch(blocks):
+    kinds = zip(blocks, (False, True))
+    return [entry for block, kind in kinds for entry in Fold.scratch(*block.shape, kind)]
+
+
+def feed_full(grads):
+    up, down = grads
+    return [(up.shape, BF16), ((4, down.shape[0], down.shape[1] // 4), BF16)]
+
+
+def attend_full(grads):
+    out, qkv = grads
+    return [((4, out.shape[0], out.shape[1] // 4), BF16), (qkv.shape, BF16)]
+
+
+def swap_across(wire, source, target, first_sends):
+    quad = Quad()
+    second = jnp.logical_not(quad.first)
+    sends, takes = (quad.first, second) if first_sends else (second, quad.first)
+    made = wire.copy(source, target, quad.across, sends)
+
+    @pl.when(sends)
+    def _():
+        made.start()
+
+    yield
+
+    @pl.when(takes)
+    def _():
+        made.wait_recv()
+
+
+def tail_kernel(*refs):
+    sems, refs = refs[-1], refs[:-1]
+    grads, finals, small_refs, away, refs = refs[0:2], refs[2:4], refs[4:8], refs[8], refs[9:]
+    full_feed, full_attend, totals, came = refs[0:2], refs[2:4], refs[4:6], refs[6]
+    scratch = refs[7:]
+    wire, line = Wire(sems), Line()
+    wide_barrier(wire, line, Quad().across)
+    swap = swap_across(wire, away, came, False)
+    next(swap)
+    smalls = [
+        small_steps(wire, line, *small_refs[2 * at : 2 * at + 2], *scratch[4 * at : 4 * at + 4], totals[at])
+        for at in range(2)
     ]
-    made = []
-    at = wire.at
-    for fold, piece, full in ((down, pieces[0], full_down), (out, pieces[1], full_out)):
-        slot = full.at[at, span(piece.mine, piece.eighth)]
-        for peer in (wire.diagonal, wire.far, wire.near):
-            made.append(wire.send(fold.final.at[:, columns(peer)], slot, {"narrow": peer}))
-        slot[...] = fold.final[:, columns(at)]
-    pieces[2].own()[...] = up.final[...]
-    rows = span(pieces[3].mine, pieces[3].eighth)
-    odd, upper = lax.rem(at, 2), at // 2
-    made.append(
-        wire.send(
-            qkv.final.at[:, columns(2 - 2 * upper)],
-            full_qkv.at[rows, columns(2 - 2 * odd)],
-            {"narrow": wire.far},
-        )
-    )
-    made.append(
-        wire.send(
-            qkv.final.at[:, columns(1 - odd + upper)],
-            full_qkv.at[rows, columns(1)],
-            {"narrow": wire.near},
-        )
-    )
-    full_qkv[rows, columns(2 * odd)] = qkv.final[:, columns((at + 1) // 2)]
-    for copy in made:
-        copy.wait_recv()
-    run(spread_steps(wire, ring, pieces))
+    own = scratch[12:14]
+    steps = tail_steps(wire, line, grads, finals, full_feed, full_attend, own, scratch[8:12])
+    run(steps, *smalls)
+    next(swap, None)
     wire.finish()
 
 
-def sum_gradients(qkv, out, up, down, norms, bias):
-    narrow = lax.axis_size("narrow")
-    part = norms.shape[1] // narrow
-    items = ((down, True), (out, True), (up, False), (qkv, False))
-    scratch = [entry for item, kind in items for entry in Fold.scratch(*item.shape, kind)]
-    scratch += [
-        pltpu.VMEM((narrow, 8, part), F32),
+def tail(attend, feed_finals, feed, norms, biases, away):
+    part = norms[0].shape[1] // 4
+    small = [
+        pltpu.VMEM((4, 8, part), F32),
         pltpu.VMEM((16, part), F32),
         pltpu.VMEM((16, part), F32),
         pltpu.VMEM((4, 16, part), F32),
     ]
     return call(
-        sum_gradients_kernel,
-        5,
-        [
-            (qkv.shape, BF16),
-            ((narrow, out.shape[0], part), BF16),
-            (up.shape, BF16),
-            ((narrow, down.shape[0], part), BF16),
-            ((16, part), F32),
-        ],
-        scratch,
+        tail_kernel,
+        9,
+        feed_full(feed)
+        + attend_full(attend)
+        + [((16, part), F32)] * 2
+        + [(away.shape, away.dtype)],
+        small * 2
+        + fold_scratch(attend)
+        + [pltpu.VMEM(shape, kind) for shape, kind in fold_outs(attend)],
         0,
-        qkv, out, up, down, norms, bias,
-    )
+        *attend, *feed_finals, norms[0], biases[0], norms[1], biases[1], away,
+    )
+
+
+def backward_wide(grad, result, saved, weights, start, tables):
+    (grad_feed_1, norms_1, bias_1, grad_middle, grad_branch), (result_came,) = feed_backward(
+        Background(
+            3, [result], [(result.shape, result.dtype)], [],
+            lambda wire, quad, refs, outs, scratch: swap_across(wire, refs[0], outs[0], True),
+            quad=True, across=True,
+        ),
+        grad, saved[1], weights[1],
+    )
+    (grad_attend_1, norms, grad), finals_1 = attend_backward(
+        Background(
+            4, grad_feed_1, fold_outs(grad_feed_1), fold_scratch(grad_feed_1),
+            fold_feed_steps,
+        ),
+        grad_branch, grad_middle, saved[1], weights[1], start, tables,
+    )
+    norms_1 = norms_1 + norms
+
+    (grad_feed_0, norms_0, bias_0, grad_middle, grad_branch), results = feed_backward(
+        Background(
+            6, list(grad_attend_1) + list(finals_1),
+            fold_outs(grad_attend_1) + feed_full(grad_feed_1), fold_scratch(grad_attend_1),
+            fold_attend_spread_feed_steps,
+        ),
+        grad.astype(F32), saved[0], weights[0],
+    )
+    finals_1, full_feed_1 = results[:2], results[2:]
+
+    (grad_attend_0, norms, grad), results = attend_backward(
+        Background(
+            7, list(finals_1) + list(grad_feed_0),
+            attend_full(grad_attend_1) + fold_outs(grad_feed_0), fold_scratch(grad_feed_0),
+            spread_attend_fold_feed_steps,
+        ),
+        grad_branch, grad_middle, saved[0], weights[0], start, tables,
+    )
+    norms_0 = norms_0 + norms
+    full_attend_1, finals_0 = results[:2], results[2:]
+    results = tail(
+        grad_attend_0, finals_0, grad_feed_0, (norms_0, norms_1), (bias_0, bias_1), grad
+    )
+    full_feed_0, full_attend_0, totals = results[:2], results[2:4], results[4:6]
+    grad_came = results[6]
+
+    def shards(feed, attend, total):
+        up, down = feed
+        out, qkv = attend
+        out, down = (block.reshape(-1, block.shape[2]) for block in (out, down))
+        return qkv, out, up, total[8:12].reshape(-1), down, total[:4], total[4:8]
+
+    return grad, grad_came, result_came, (
+        shards(full_feed_0, full_attend_0, totals[0]),
+        shards(full_feed_1, full_attend_1, totals[1]),
+    )
+
+
+class Quad:
+    def __init__(self):
+        at = lax.axis_index("wide")
+        pair, turn = lax.rem(at, 2), at // 2
+        odd = lax.rem(turn, 2)
+        self.side = {"wide": at + 1 - 2 * pair}
+        self.mate = {"wide": (turn + 1 - 2 * odd) * 2 + pair}
+        self.mine = odd * 2 + pair
+        self.from_side = odd * 2 + 1 - pair
+        self.from_mate = (1 - odd) * 2 + pair
+        halfway = lax.axis_size("wide") // 2
+        self.first = at < halfway
+        self.across = {"wide": lax.rem(at + halfway, 2 * halfway)}
+
+
+class Fetch:
+    def __init__(self, wire, shard, full, by_heads):
+        self.wire, self.full, self.rows = wire, full, full.shape[0]
+        at, odd, upper = wire.at, lax.rem(wire.at, 2), wire.at // 2
+        part = shard.shape[1]
+
+        def columns(block, count=1):
+            return pl.ds(pl.multiple_of(block * 256, 256), 256 * count)
+
+        if by_heads:
+            self.far = [
+                (
+                    lambda rows: shard.at[rows, columns(2 - 2 * odd)],
+                    lambda rows: full.at[rows, columns(2 * upper)],
+                    wire.far,
+                )
+            ]
+            self.relay = lambda rows: full.at[rows, columns(2 - 2 * upper)]
+            self.near = (shard.at[:, columns(1)], full.at[:, columns(odd + upper)])
+            self.own = (shard.at[:, columns(2 * odd)], full.at[:, columns((at + 1) // 2)])
+        else:
+            block = self.rows
+
+            def away(peer):
+                return (
+                    lambda rows: shard.at[span(peer * block + rows.start, rows.size)],
+                    lambda rows: full.at[rows, columns(at)],
+                    peer,
+                )
+
+            self.far = [away(wire.far), away(wire.diagonal)]
+            self.relay = lambda rows: full.at[rows, columns(2 - 2 * upper, 2)]
+            self.near = (shard.at[span(wire.near * block, block)], full.at[:, columns(at)])
+            self.own = (shard.at[span(at * block, block)], full.at[:, columns(at)])
+
+    def quarter(self, which, half=0, halves=1):
+        size = self.rows // 4
+        return span(which * size + half * (size // halves), size // halves)
+
+
+def fetch_steps(wire, quad, fetches, local):
+    copies, sent, nears = [], [], []
+    for at, fetch in enumerate(fetches):
+        rows = fetch.quarter(quad.mine)
+        for source, target, peer in fetch.far:
+            sent.append(wire.send(source(rows), target(rows), {"narrow": peer}))
+        nears.append(wire.send(*fetch.near, {"narrow": wire.near}))
+        copies.append(pltpu.make_async_copy(*fetch.own, local.at[at]))
+        copies[-1].start()
+    yield
+    for made in sent:
+        made.wait_recv()
+    sides, mates = [], []
+    for fetch in fetches:
+        held = fetch.relay(fetch.quarter(quad.mine))
+        sides.append(wire.send(held, held, quad.side))
+        mates.append(wire.send(held, held, quad.mate))
+    yield
+    last = []
+    for fetch, side, mate in zip(fetches, sides, mates):
+        side.wait_recv()
+        held = fetch.relay(fetch.quarter(quad.from_side, 0, 2))
+        last.append(wire.send(held, held, quad.mate))
+        mate.wait_recv()
+        held = fetch.relay(fetch.quarter(quad.from_mate, 1, 2))
+        last.append(wire.send(held, held, quad.side))
+    yield
+    for made in last + nears:
+        made.wait_recv()
+    for copy in copies:
+        copy.wait()
+
+
+def greet(peers):
+    barrier = pltpu.get_barrier_semaphore()
+    for peer in peers:
+        pl.semaphore_signal(barrier, inc=1, device_id=peer, device_id_type=MESH)
+    pl.semaphore_wait(barrier, len(peers))
+
+
+def quad_barrier(wire, quad, *others):
+    narrow = [{"narrow": peer} for peer in (wire.near, wire.far, wire.diagonal)]
+    greet(narrow + [quad.side, quad.mate] + list(others))
+
+
+def begin_kernel(
+    blocks_ref, w_qkv_ref, w_out_ref, norms_ref,
+    qkv_ref, out_ref, full_norms_ref, came_ref,
+    local, sems,
+):
+    wire, quad = Wire(sems), Quad()
+    quad_barrier(wire, quad, quad.across)
+    size = came_ref.shape[0]
+    away = blocks_ref.at[span(quad.first.astype(jnp.int32) * size, size)]
+    swap = wire.send(away, came_ref, quad.across)
+    fetches = [
+        Fetch(wire, w_qkv_ref.at[0], qkv_ref, True),
+        Fetch(wire, w_out_ref.at[0], out_ref, False),
+    ]
+    part = norms_ref.shape[1]
+    slot = full_norms_ref.at[:, pl.ds(pl.multiple_of(wire.at * part, part), part)]
+    sent = [
+        wire.send(norms_ref, slot, {"narrow": peer})
+        for peer in (wire.diagonal, wire.far, wire.near)
+    ]
+    own = pltpu.make_async_copy(norms_ref, slot, local.at[len(fetches)])
+    own.start()
+    run(fetch_steps(wire, quad, fetches, local))
+    for made in sent:
+        made.wait_recv()
+    own.wait()
+    swap.wait_recv()
+    wire.finish()
+
+
+def anywhere(count):
+    return [pl.BlockSpec(memory_space=pl.ANY)] * count
+
+
+def begin(blocks, w_qkv, w_out, norms):
+    width = blocks.shape[1]
+    shapes = [
+        (w_qkv.shape[1:], BF16),
+        ((w_out.shape[2], width), BF16),
+        ((norms.shape[0], width), BF16),
+        ((blocks.shape[0] // 2, width), BF16),
+    ]
+    return pl.pallas_call(
+        begin_kernel,
+        in_specs=anywhere(4),
+        out_specs=anywhere(4),
+        out_shape=shaped(*shapes),
+        scratch_shapes=[pltpu.SemaphoreType.DMA((8,)), pltpu.SemaphoreType.DMA((SEMAPHORES,))],
+        compiler_params=pltpu.CompilerParams(collective_id=10, has_side_effects=True),
+        name="begin",
+    )(blocks, w_qkv, w_out, norms)
+
+
+def fetch_rest_steps(wire, quad, refs, outs, scratch):
+    w_qkv, w_out, w_down = refs
+    down_0, qkv_1, out_1, down_1 = outs
+    first = fetch_steps(wire, quad, [Fetch(wire, w_down.at[0], down_0, False)], scratch[0])
+    rest = [
+        Fetch(wire, w_qkv.at[1], qkv_1, True),
+        Fetch(wire, w_out.at[1], out_1, False),
+        Fetch(wire, w_down.at[1], down_1, False),
+    ]
+    second = fetch_steps(wire, quad, rest, scratch[1])
+    next(first)
+    yield
+    next(first)
+    next(second)
+    yield
+    next(first)
+    next(second)
+    yield
+    next(first, None)
+    next(second)
+    yield
+    next(second, None)
 
 
 def swap(block, distance):
@@ -965,28 +1521,46 @@
     return lax.all_to_all(block, "narrow", split_axis=1, concat_axis=0, tiled=True)
 
 
-def layer_forward(resid, weights, start, tables):
+def layer_forward(resid, weights, start, tables, background=None):
     w_qkv, w_out, w_up, b_up, w_down, gains, shifts = weights
-    normed, query, keys, values, mixture, logs, branch, middle, inner = attend_half(
-        resid, gains, shifts, *tables, start[:, None], w_qkv, w_out
-    )
+    (normed, query, keys, values, mixture, logs, branch, middle, inner), more = attend_half(
+        background or Background(1), resid, gains, shifts, *tables, start[:, None], w_qkv, w_out
+    )
+    if background is not None:
+        w_down = more[0]
     inner, active, slope, second, result = feed_half(
         inner, middle, gains, shifts, w_up, b_up, w_down
     )
-    return result, (
+    return result, more, (
         resid, normed, query, keys, values, mixture, logs, branch, middle, inner, active, slope, second
     )
 
 
+def feed_backward(background, grad, saved, weights):
+    w_qkv, w_out, w_up, b_up, w_down, gains, shifts = weights
+    _, _, _, _, _, _, _, branch, middle, inner, active, slope, second = saved
+    (grad_down, grad_up, grad_b_up, norms, grad_middle, grad_branch), results = feed_back(
+        background, grad, second, middle, branch, gains, inner, active, slope, w_up, w_down
+    )
+    return ((grad_up, grad_down), norms, grad_b_up, grad_middle, grad_branch), results
+
+
+def attend_backward(background, grad_branch, grad_middle, saved, weights, start, tables):
+    w_qkv, w_out, w_up, b_up, w_down, gains, shifts = weights
+    resid, normed, query, keys, values, mixture, logs, _, _, _, _, _, _ = saved
+    (grad_qkv, grad_out, norms, grad), results = attend_back(
+        background, grad_branch, grad_middle, resid, gains, normed, query, keys, values, mixture,
+        logs, start[None], *tables, w_qkv, w_out,
+    )
+    return ((grad_out, grad_qkv), norms, grad), results
+
+
 def layer_backward(grad, saved, weights, start, tables):
-    w_qkv, w_out, w_up, b_up, w_down, gains, shifts = weights
-    resid, normed, query, keys, values, mixture, logs, branch, middle, inner, active, slope, second = saved
-    grad_down, grad_up, grad_b_up, norms, grad_middle, grad_branch = feed_back(
-        grad, second, middle, branch, gains, inner, active, slope, w_up, w_down
-    )
-    grad_qkv, grad_out, norms_too, grad = attend_back(
-        grad_branch, grad_middle, resid, gains, normed, query, keys, values, mixture, logs,
-        start[None], *tables, w_qkv, w_out,
+    ((grad_up, grad_down), norms, grad_b_up, grad_middle, grad_branch), _ = feed_backward(
+        Background(3), grad, saved, weights
+    )
+    ((grad_out, grad_qkv), norms_too, grad), _ = attend_backward(
+        Background(4), grad_branch, grad_middle, saved, weights, start, tables
     )
     return grad, (grad_qkv, grad_out, grad_up, grad_b_up, grad_down, norms + norms_too)
 
@@ -1005,10 +1579,6 @@
         return full.transpose(1, 0, 2, 3).reshape(wide * rows, width)
 
     qkv, out, up, b_up, down, norms = grads
-    if lax.axis_size("wide") == 8:
-        qkv, out, up, down, total = sum_gradients(qkv, out, up, down, norms, b_up)
-        out, down = (block.reshape(-1, block.shape[2]) for block in (out, down))
-        return qkv, out, up, total[8:12].reshape(-1), down, total[:4], total[4:8]
     qkv = spread(from_heads(fold(qkv), at))
     out = spread_rows(to_columns(fold(out)))
     up = spread(fold(up))
@@ -1024,61 +1594,75 @@
     wide = lax.axis_size("wide")
     narrow = lax.axis_size("narrow")
     halfway = wide // 2
-    flip = wide - 2
     wide_at = lax.axis_index("wide")
     at = lax.axis_index("narrow")
     first = wide_at < halfway
     row_count = ends.shape[0] // 2
-    width = ends.shape[1]
     length = row_count * narrow
-    blocks = ends.reshape(2, row_count, width)
-
-    def route(block, pairs):
+
+    def route(block):
+        pairs = [(i, (i + halfway) % wide) for i in range(wide)]
         return lax.ppermute(block, "wide", pairs)
 
-    groups = range(halfway)
-    x_came = route(blocks[1], [(g, g ^ flip) for g in groups])
-    dy_first = route(blocks[0], [(g + halfway, g) for g in groups])
-    dy_second = route(blocks[1], [(g + halfway, g ^ flip) for g in groups])
-    resid = jnp.where(first, blocks[0], x_came).astype(F32)
-    upstream = jnp.where(first, dy_first, dy_second).astype(F32)
-    group_at = jnp.where(first, wide_at, wide_at ^ flip)
-    micro_at = jnp.where(first, 0, 1)
-
-    own_lengths = lengths[group_at, micro_at]
+    own_lengths = lengths[lax.rem(wide_at, halfway), wide_at // halfway]
     places = jnp.arange(length, dtype=jnp.int32)
     passed = (places[:, None] >= jnp.cumsum(own_lengths)[None, :]).astype(jnp.int32)
     start = jnp.sum(passed * own_lengths[None, :], axis=1)
     tables = rope_tables(places - start)
-
-    def weights_of(layer):
-        return (
-            by_heads(w_qkv[layer], at),
-            to_rows(w_out[layer]),
-            w_up[layer],
-            b_up[layer].astype(F32)[None],
-            to_rows(w_down[layer]),
-            lax.all_gather(norm_gain[layer], "narrow", axis=1, tiled=True).astype(F32),
-            lax.all_gather(norm_bias[layer], "narrow", axis=1, tiled=True).astype(F32),
+    b_up = b_up.astype(F32)[:, None]
+    norms = jnp.concatenate([norm_gain, norm_bias]).reshape(16, -1)
+
+    if wide == 8:
+        qkv_0, out_0, norms, came = begin(ends, w_qkv, w_out, norms)
+    else:
+        came = route(jnp.where(first, ends[row_count:], ends[:row_count]))
+        norms = lax.all_gather(norms, "narrow", axis=1, tiled=True)
+        qkv_0, out_0 = by_heads(w_qkv[0], at), to_rows(w_out[0])
+        down_0, down_1 = to_rows(w_down[0]), to_rows(w_down[1])
+        qkv_1, out_1 = by_heads(w_qkv[1], at), to_rows(w_out[1])
+    norms = norms.astype(F32)
+    resid = jnp.where(first, ends[:row_count], came).astype(F32)
+    upstream = jnp.where(first, came, ends[row_count:]).astype(F32)
+
+    if wide == 8:
+        width = ends.shape[1]
+        part = w_out.shape[2]
+        background = Background(
+            11, [w_qkv, w_out, w_down],
+            [
+                ((w_up.shape[2], width), BF16),
+                (w_qkv.shape[1:], BF16),
+                ((part, width), BF16),
+                ((w_up.shape[2], width), BF16),
+            ],
+            [pltpu.SemaphoreType.DMA((4,))] * 2, fetch_rest_steps, quad=True,
         )
-
-    weights = [weights_of(layer) for layer in range(2)]
-    middle, saved_first = layer_forward(resid, weights[0], start, tables)
+        weights_0 = (qkv_0, out_0, w_up[0], b_up[0], None, norms[0:4], norms[8:12])
+        middle, more, saved_first = layer_forward(resid, weights_0, start, tables, background)
+        down_0, qkv_1, out_1, down_1 = more
+        weights_0 = weights_0[:4] + (down_0,) + weights_0[5:]
+    else:
+        weights_0 = (qkv_0, out_0, w_up[0], b_up[0], down_0, norms[0:4], norms[8:12])
+        middle, _, saved_first = layer_forward(resid, weights_0, start, tables)
+    weights_1 = (qkv_1, out_1, w_up[1], b_up[1], down_1, norms[4:8], norms[12:16])
+    weights = (weights_0, weights_1)
     middle = middle.astype(BF16).astype(F32)
-    result, saved_second = layer_forward(middle, weights[1], start, tables)
+    result, _, saved_second = layer_forward(middle, weights_1, start, tables)
     result = result.astype(BF16)
-    grad, grads_second = layer_backward(upstream, saved_second, weights[1], start, tables)
-    totals_second = reduce_grads(grads_second, at)
-    grad, grads_first = layer_backward(grad.astype(F32), saved_first, weights[0], start, tables)
-    totals_first = reduce_grads(grads_first, at)
-
-    grad_came = route(grad, [(g ^ flip, g) for g in groups])
-    result_first = route(result, [(g, g + halfway) for g in groups])
-    result_second = route(result, [(g ^ flip, g + halfway) for g in groups])
+    if wide == 8:
+        grad, grad_came, result_came, (totals_first, totals_second) = backward_wide(
+            upstream, result, (saved_first, saved_second), weights, start, tables
+        )
+    else:
+        result_came = route(result)
+        grad, grads_second = layer_backward(upstream, saved_second, weights_1, start, tables)
+        totals_second = reduce_grads(grads_second, at)
+        grad, grads_first = layer_backward(grad.astype(F32), saved_first, weights_0, start, tables)
+        totals_first = reduce_grads(grads_first, at)
+        grad_came = route(grad)
+
     ends_out = jnp.where(
-        first,
-        jnp.concatenate([grad, grad_came]),
-        jnp.concatenate([result_first, result_second]),
+        first, jnp.concatenate([grad, grad_came]), jnp.concatenate([result_came, result])
     )
     totals = [jnp.stack([a.astype(F32), b.astype(F32)]) for a, b in zip(totals_first, totals_second)]
     return (ends_out,) + tuple(totals)

time: 880 us -> 679 us (0.77)
  Pallas kernels: 703 us -> 619 us
  starting transfers between devices: 34.2 us -> 0 us
  blocking collectives: 34 us -> 0 us
  local copies, waits for them, and re-layouts: 39.3 us -> 21.6 us
  waiting for transfers between devices: 11.9 us -> 0 us
  between operations: 11.1 us -> 1.35 us
  other arithmetic: 37.1 us -> 28.3 us
    pallas_call x10 -> x3, Pallas kernels: 703 us -> 177 us  [call(): pl.pallas_call(kernel, in_specs=vmem(len(operands)), out_specs=vmem(len(o...]
    pallas_call x0 -> x7, Pallas kernels: none -> 442 us  [the longest x6 408 us: call_with(): pl.pallas_call(kernel, in_specs=vmem(len(operands)) + place(len(backgroun...]
    all_gather x4 -> x0, blocking collectives: 34 us -> none  [the longest x2 23.7 us: weights_of(): lax.all_gather(norm_bias[layer], 'narrow', axis=1, tiled=True).astype(F32)]
    ppermute x10 -> x0, starting transfers between devices: 19 us -> none  [the longest x6 16.5 us: route(): return lax.ppermute(block, 'wide', pairs)]
    all_to_all x4 -> x0, starting transfers between devices: 15.1 us -> none  [to_rows(): lax.all_to_all(block, 'narrow', split_axis=0, concat_axis=1, tiled=True)]
    all_to_all x4 -> x0, waiting for transfers between devices: 11.9 us -> none  [to_rows(): lax.all_to_all(block, 'narrow', split_axis=0, concat_axis=1, tiled=True)]
  transfers between devices with their start and end apart: 14 -> 0, of which waited for: 2 -> 0; matrix products, arithmetic and copies ran while one was open for 6% -> 0% of each run, Pallas kernels for 68% -> 0%
where the time goes in v3:
time: 679 us; the launch traced here: 670 us
  Pallas kernels  619 us (91%)
  other arithmetic  28.3 us (4%)
  local copies, waits for them, and re-layouts  21.6 us (3%)
    pallas_call x6, Pallas kernels, call_with(): pl.pallas_call(kernel, in_specs=vmem(len(operands)) + place(len(backgroun...  408 us
    pallas_call x3, Pallas kernels, call(): pl.pallas_call(kernel, in_specs=vmem(len(operands)), out_specs=vmem(len(o...  177 us
    pallas_call x1, Pallas kernels, begin(): pl.pallas_call(begin_kernel, in_specs=anywhere(4), out_specs=anywhere(4),...  34.8 us
    another operation x7, other arithmetic, on_device(): jnp.stack([a.astype(F32), b.astype(F32)])  14.9 us

profile of v3, /device:TPU:0, one launch (start us, length us, event | category | flops | bytes accessed | tf_op | source)
XLA Modules:
  0.0 670.4 jit_solution(4201646700248760682)
XLA Ops:
  3.9 1.0 copy.22.refs_5_
  5.0 1.9 fusion
  6.9 1.8 pad_maximum_fusion
  8.7 34.8 %begin.1 = (bf16[1024,768]{1,0:T(8,128)(2,1)}, bf16[256,1024]{1,0:T(8,128)(2,1)}, bf16[16,1024]{1,0:T(8,128)(2,1)}, bf16[256,1024]{1,0:T(8,128)(2,1)}) custom-call(bf16[512,1024]{1,0:T(8,128)(2,1)} %blocks_ref.1, bf16[2,1024,768]{2,1,0:T(8,128)(2,1)} %refs_8_.1, bf16[2,1024,256]{2,1,0:T(8,128)(2,1)} %refs_9_.1, bf16[16,256]{1,0:T(8,128)(2,1)} %reshape.113.norms_ref), custom_call_target="tpu_custom_call" | custom-call | tf_op jit(solution)/shard_map/begin/pallas_call | solution.py:1448
  43.6 0.8 fusion.1
  44.4 2.5 select_convert_fusion
  46.9 4.7 slice_bitcast_fusion
  51.6 65.0 %attend_half_body_wide.1 = (bf16[1024,1024]{1,0:T(8,128)(2,1)}, bf16[1024,256]{1,0:T(8,128)(2,1)S(1)}, bf16[1024,256]{1,0:T(8,128)(2,1)S(1)}, bf16[1024,256]{1,0...) custom-call(f32[256,1024]{1,0:T(8,128)} %get-tuple-element.158.refs_, ...), custom_call_target="tpu_custom_call" | custom-call | flops 3221225472 | bytes 16777216 | tf_op jit(solution)/shard_map/attend_half_body_wide/pallas_call | solution.py:283
  116.6 0.8 copy-done.4
  117.4 0.8 copy-done.5
  118.2 0.8 copy-done.6
  119.0 1.0 copy-done.7
  120.1 34.9 %feed_half_kernel.2 = (bf16[1024,1024]{1,0:T(8,128)(2,1)}, bf16[1024,1024]{1,0:T(8,128)(2,1)}, bf16[1024,1024]{1,0:T(8,128)(2,1)}, f32[256,1024]{1,0:T(8,128)S(1)}, f32[256,1024]{1,0:T(8,128)}) custom-call(bf16[256,1024]{1,0:T(8,128)(2,1)S(1)} %copy-done.7, f32[256,1024]{1,0:T(8,128)} %get-tuple-element.87.h_ref.refs_2_, ...), custom_call_target="tpu_custom_call" | custom-call | flops 4294967296 | bytes 16777216 | tf_op jit(solution)/shard_map/feed_half_kernel/pallas_call | solution.py:226
  155.0 1.0 copy-done.8
  155.9 2.3 convert_convert_fusion.refs_0_.refs_2_
  158.2 46.1 %attend_half_body.1 = (bf16[1024,1024]{1,0:T(8,128)(2,1)}, bf16[1024,256]{1,0:T(8,128)(2,1)S(1)}, bf16[1024,256]{1,0:T(8,128)(2,1)S(1)}, bf16[1024,256]{1,0:T(8,...) custom-call(f32[256,1024]{1,0:T(8,128)} %convert_convert_fusion.refs, ...), custom_call_target="tpu_custom_call" | custom-call | flops 3221225472 | bytes 16777216 | tf_op jit(solution)/shard_map/attend_half_body/pallas_call | solution.py:283
  205.9 0.8 copy-done.12
  206.8 1.0 copy-done.13
  207.8 34.8 %feed_half_kernel.3 = (bf16[1024,1024]{1,0:T(8,128)(2,1)}, bf16[1024,1024]{1,0:T(8,128)(2,1)}, bf16[1024,1024]{1,0:T(8,128)(2,1)}, f32[256,1024]{1,0:T(8,128)S(1)}, f32[256,1024]{1,0:T(8,128)}) custom-call(bf16[256,1024]{1,0:T(8,128)(2,1)S(1)} %copy-done.13, f32[256,1024]{1,0:T(8,128)} %get-tuple-element.93.h_ref.refs_2_, ...), custom_call_target="tpu_custom_call" | custom-call | flops 4294967296 | bytes 16777216 | tf_op jit(solution)/shard_map/feed_half_kernel/pallas_call | solution.py:226
  242.6 1.0 copy-done.9
  243.5 1.3 convert_element_type.87.refs_10_
  244.8 39.0 %feed_back_body_wide.2 = (bf16[1024,1024]{1,0:T(8,128)(2,1)}, bf16[1024,1024]{1,0:T(8,128)(2,1)}, f32[1,1024]{1,0:T(1,128)S(1)}, f32[8,1024]{1,0:T(8,128)S(1)}, ...) custom-call(f32[256,1024]{1,0:T(8,128)} %get-tuple-element.159.refs_0_, ...), custom_call_target="tpu_custom_call" | custom-call | flops 8589934592 | bytes 16777216 | tf_op jit(solution)/shard_map/feed_back_body_wide/pallas_call | solution.py:283
  284.7 81.1 %attend_back_body_wide.2 = (bf16[1024,768]{1,0:T(8,128)(2,1)}, bf16[256,1024]{1,0:T(8,128)(2,1)S(1)}, f32[8,1024]{1,0:T(8,128)S(1)}, bf16[256,1024]{1,0:T(8,128)...) custom-call(bf16[256,1024]{1,0:T(8,128)(2,1)} %copy-done.16, ...), custom_call_target="tpu_custom_call" | custom-call | flops 6979321856 | bytes 16777216 | tf_op jit(solution)/shard_map/attend_back_body_wide/pallas_call | solution.py:283
  366.6 1.1 convert_element_type.88.refs_0_
  367.7 92.3 %feed_back_body_wide.3 = (bf16[1024,1024]{1,0:T(8,128)(2,1)}, bf16[1024,1024]{1,0:T(8,128)(2,1)}, f32[1,1024]{1,0:T(1,128)S(1)}, f32[8,1024]{1,0:T(8,128)S(1)}, ...) custom-call(f32[256,1024]{1,0:T(8,128)} %convert_element_type.88.ref, ...), custom_call_target="tpu_custom_call" | custom-call | flops 8589934592 | bytes 16777216 | tf_op jit(solution)/shard_map/feed_back_body_wide/pallas_call | solution.py:283
  460.8 84.1 %attend_back_body_wide.3 = (bf16[1024,768]{1,0:T(8,128)(2,1)}, bf16[256,1024]{1,0:T(8,128)(2,1)S(1)}, f32[8,1024]{1,0:T(8,128)S(1)}, bf16[256,1024]{1,0:T(8,128)...) custom-call(bf16[256,1024]{1,0:T(8,128)(2,1)} %copy-done.14, ...), custom_call_target="tpu_custom_call" | custom-call | flops 6979321856 | bytes 16777216 | tf_op jit(solution)/shard_map/attend_back_body_wide/pallas_call | solution.py:283
  545.6 107.1 %tail_kernel.1 = (bf16[1024,1024]{1,0:T(8,128)(2,1)}, bf16[4,1024,256]{2,1,0:T(8,128)(2,1)}, bf16[4,256,256]{2,1,0:T(8,128)(2,1)S(1)}, bf16[1024,768]{1,0:T(8,12...) custom-call(bf16[256,1024]{1,0:T(8,128)(2,1)S(1)} %get-tuple-element.134.refs_0_, ...), custom_call_target="tpu_custom_call" | custom-call | bytes 16777216 | tf_op jit(solution)/shard_map/tail_kernel/pallas_call | solution.py:226
  652.7 1.4 maximum_select_fusion
  656.0 1.5 maximum_convert_fusion.3
  657.5 3.5 maximum_convert_fusion.2
  661.8 4.2 maximum_convert_fusion
  666.0 3.9 maximum_convert_fusion.1
  (59 shorter events, 10.7 us)
Async XLA Ops:
  0.6 0.7 copy-start
  8.7 35.6 %copy-start.17 = (bf16[512,1024]{1,0:T(8,128)(2,1)S(1)}, bf16[512,1024]{1,0:T(8,128)(2,1)}, u32[]{:S(2)}) copy-start(bf16[512,1024]{1,0:T(8,128)(2,1)} %blocks_ref.1) | copy-start | bytes 3145732
  116.6 0.8 copy-start.4
  117.4 0.8 copy-start.5
  118.2 0.8 copy-start.6
  119.0 1.0 copy-start.7
  155.0 1.0 copy-start.8
  204.3 0.8 copy-start.10
  205.1 0.8 copy-start.11
  205.9 0.8 copy-start.12
  206.8 1.0 copy-start.13
  242.6 1.0 copy-start.9
  283.9 0.8 copy-start.16
  365.8 0.8 copy-start.15
  460.0 0.8 copy-start.14
  544.8 0.8 copy-start.2
  545.6 107.1 %copy-start.3 = (bf16[256,1024]{1,0:T(8,128)(2,1)S(1)}, bf16[256,1024]{1,0:T(8,128)(2,1)}, u32[]{:S(2)}) copy-start(bf16[256,1024]{1,0:T(8,128)(2,1)} %copy-done.2) | copy-start | bytes 1572868
  652.7 3.3 copy-start.24
  654.2 3.3 copy-start.22
  654.2 3.3 copy-start.23
  657.5 3.5 copy-start.19
  657.5 4.3 copy-start.21
  661.8 4.2 copy-start.18
  661.8 4.2 copy-start.20
  666.0 3.9 copy-start.1

commit v4 on v3

--- a/solution.py
+++ b/solution.py
@@ -48,7 +48,6 @@
 
 
 MESH = pl.DeviceIdType.MESH
-SEMAPHORES = 400
 
 
 def layer_norm_back(values, grad, gain_row):
@@ -69,7 +68,8 @@
 
 class Copy:
     def __init__(self, wire, source, target, peer, when):
-        self.when = when
+        self.when, self.settled = when, False
+        source, target = (item.ref if isinstance(item, Staged) else item for item in (source, target))
         self.pieces = (source, target, wire.sems.at[wire.used], wire.sems.at[wire.used + 1], peer)
         wire.used += 2
         wire.made.append(self)
@@ -98,6 +98,11 @@
         self.when = others
         self.remote().wait_send()
 
+    def settle(self):
+        if not self.settled:
+            self.settled = True
+            self.wait_send()
+
     def wait_send(self):
         if self.when is None:
             self.remote().wait_send()
@@ -130,9 +135,16 @@
         made.start()
         return made
 
+    def move(self, source, target):
+        source = source.ref if isinstance(source, Staged) else source
+        copy = pltpu.make_async_copy(source, target, self.sems.at[self.used])
+        self.used += 1
+        copy.start()
+        copy.wait()
+
     def finish(self):
         for made in self.made:
-            made.wait_send()
+            made.settle()
 
 
 def block_rows(block, size, part=0, parts=1):
@@ -222,39 +234,133 @@
     return [jax.ShapeDtypeStruct(shape, kind) for shape, kind in entries]
 
 
-def call(kernel, number, outs, scratch, flops, *operands):
-    return pl.pallas_call(
-        kernel,
-        in_specs=vmem(len(operands)),
-        out_specs=vmem(len(outs)),
-        out_shape=shaped(*outs),
-        scratch_shapes=scratch + [pltpu.SemaphoreType.DMA((SEMAPHORES,))],
-        compiler_params=pltpu.CompilerParams(
-            collective_id=number, has_side_effects=True, vmem_limit_bytes=52 * 2**20
-        ),
-        cost_estimate=pl.CostEstimate(flops=flops, bytes_accessed=2**24, transcendentals=0),
-        name=kernel.__name__,
-    )(*operands)
+class Poll:
+    def __init__(self, steps):
+        self.steps = steps
+
+    def __call__(self, times=1):
+        for _ in range(times):
+            for step in list(self.steps):
+                if next(step, "end") == "end":
+                    self.steps.remove(step)
+
+    def enter(self):
+        pass
+
+    def leave(self):
+        pass
+
+    def before(self, what):
+        pass
+
+
+SMALL = 2**16
+
+
+class Staged:
+    def __init__(self, ref, copy, is_result):
+        self.ref, self.copy, self.is_result = ref, copy, is_result
+        self.begun = self.ended = False
+        self.shape, self.dtype = ref.shape, ref.dtype
+
+    def begin(self):
+        self.begun = True
+        self.copy.start()
+
+    def wait(self):
+        if not self.ended:
+            self.ended = True
+            self.copy.wait()
+
+    def check(self):
+        assert self.is_result or self.ended
+
+    @property
+    def at(self):
+        self.check()
+        return self.ref.at
+
+    def __getitem__(self, index):
+        self.check()
+        return self.ref[index]
+
+    def __setitem__(self, index, value):
+        self.ref[index] = value
+
+
+def ready(*refs):
+    for ref in refs:
+        if isinstance(ref, Staged):
+            ref.wait()
+
+
+def done(*refs):
+    for ref in refs:
+        if isinstance(ref, Staged):
+            ref.begin()
 
 
 class Background:
-    def __init__(self, number=None, operands=(), outs=(), scratch=(), steps=None, quad=False, across=False):
+    def __init__(
+        self, number, operands=(), outs=(), scratch=(), steps=None, staged=0, quad=False,
+        across=False, semaphores=24,
+    ):
+        self.semaphores = semaphores
+        self.staged = staged
         self.number, self.operands, self.outs = number, list(operands), list(outs)
         self.scratch, self.steps, self.quad, self.across = list(scratch), steps, quad, across
 
 
+def is_large(shape, kind):
+    return math.prod(shape) * jnp.dtype(kind).itemsize > SMALL
+
+
 def call_with(body, background, outs, scratch, flops, *operands):
-    counts = [
-        len(operands), len(background.operands), len(outs), len(background.outs),
-        len(scratch), len(background.scratch),
+    placed = len(operands)
+    everything = list(operands) + background.operands
+    arrays = [item[0] if isinstance(item, tuple) else item for item in everything]
+    shapes = [
+        (array.shape[1:] if isinstance(item, tuple) else array.shape, array.dtype)
+        for array, item in zip(arrays, everything)
     ]
+    results = list(outs) + background.outs
+    copies_in = [
+        is_large(*shape) and not (background.quad and at >= placed)
+        for at, shape in enumerate(shapes)
+    ]
+    raw_in = [background.quad and at >= placed for at in range(len(shapes))]
+    raw_out = [at >= len(outs) + background.staged for at in range(len(results))]
+    copies_out = [is_large(*shape) and not raw for shape, raw in zip(results, raw_out)]
+    staged = [shape for shape, copied in zip(shapes + results, copies_in + copies_out) if copied]
 
     def kernel(*refs):
-        refs, groups = list(refs), []
-        for count in counts:
-            groups.append(refs[:count])
-            refs = refs[count:]
-        wire = Wire(refs[0])
+        refs = list(refs)
+
+        def take(count):
+            taken = refs[:count]
+            del refs[:count]
+            return taken
+
+        sources, targets = take(len(shapes)), take(len(results))
+        body_scratch, more_scratch = take(len(scratch)), take(len(background.scratch))
+        held = take(len(staged))
+        sems, local = take(2)
+        wire = Wire(sems)
+        number = 0
+        for at, item in enumerate(everything):
+            if copies_in[at]:
+                source = sources[at].at[item[1]] if isinstance(item, tuple) else sources[at]
+                ref = held[number]
+                copy = pltpu.make_async_copy(source, ref, local.at[number])
+                sources[at] = Staged(ref, copy, False)
+                sources[at].begin()
+                number += 1
+        for at in range(len(results)):
+            if copies_out[at]:
+                ref = held[number]
+                copy = pltpu.make_async_copy(ref, targets[at], local.at[number])
+                targets[at] = Staged(ref, copy, True)
+                number += 1
         steps = []
         if background.steps is None:
             wire.barrier()
@@ -264,37 +370,48 @@
                 quad_barrier(wire, place, *([place.across] if background.across else []))
             else:
                 place = Line()
-                wide_barrier(wire, place)
-            steps = [background.steps(wire, place, groups[1], groups[3], groups[5])]
-
-        def poll(times=1):
-            for _ in range(times):
-                for step in list(steps):
-                    if next(step, "end") == "end":
-                        steps.remove(step)
-
-        body(wire, poll, *groups[0], *groups[2], *groups[4])
+                wide_barrier(wire, place, *([Quad().across] if background.across else []))
+            steps = [
+                background.steps(
+                    wire, place, sources[placed:], targets[len(outs) :], more_scratch
+                )
+            ]
+
+        poll = Poll(steps)
+        body(wire, poll, *sources[:placed], *targets[: len(outs)], *body_scratch)
         while steps:
             poll()
+        for ref in sources:
+            ready(ref)
+        for ref in targets:
+            if isinstance(ref, Staged) and not ref.begun:
+                ref.begin()
         wire.finish()
+        for ref in targets:
+            ready(ref)
 
     kernel.__name__ = body.__name__ if background.steps is None else body.__name__ + "_wide"
-    place = anywhere if background.quad else vmem
-    results = pl.pallas_call(
+
+    def spec(apart):
+        return pl.BlockSpec(memory_space=pl.ANY if apart else pltpu.VMEM)
+
+    found = pl.pallas_call(
         kernel,
-        in_specs=vmem(len(operands)) + place(len(background.operands)),
-        out_specs=vmem(len(outs)) + place(len(background.outs)),
-        out_shape=shaped(*outs, *background.outs),
+        in_specs=[spec(raw or copied) for raw, copied in zip(raw_in, copies_in)],
+        out_specs=[spec(raw or copied) for raw, copied in zip(raw_out, copies_out)],
+        out_shape=shaped(*results),
         scratch_shapes=list(scratch)
         + background.scratch
-        + [pltpu.SemaphoreType.DMA((SEMAPHORES,))],
+        + [pltpu.VMEM(*shape) for shape in staged]
+        + [pltpu.SemaphoreType.DMA((background.semaphores,))]
+        + [pltpu.SemaphoreType.DMA((max(len(staged), 1),))],
         compiler_params=pltpu.CompilerParams(
-            collective_id=background.number, has_side_effects=True, vmem_limit_bytes=52 * 2**20
+            collective_id=background.number, has_side_effects=True, vmem_limit_bytes=56 * 2**20
         ),
         cost_estimate=pl.CostEstimate(flops=flops, bytes_accessed=2**24, transcendentals=0),
         name=kernel.__name__,
-    )(*operands, *background.operands)
-    return results[: len(outs)], results[len(outs) :]
+    )(*arrays)
+    return found[: len(outs)], found[len(outs) :]
 
 
 def attend_half_body(
@@ -304,10 +421,11 @@
     held, own,
 ):
     size = x_ref.shape[0]
+    ready(x_ref)
     gather = Gather(wire, a_ref, size)
     for part in range(2):
         rows = pl.ds(part * (size // 2), size // 2)
-        normed = layer_norm(x_ref[rows], gain_ref[0:1], shift_ref[0:1])
+        normed = layer_norm(x_ref[rows].astype(F32), gain_ref[0:1], shift_ref[0:1])
         a_ref[block_rows(wire.at, size, part, 2)] = normed.astype(BF16)
         gather.push(part)
     width = q_ref.shape[1]
@@ -321,6 +439,7 @@
         v_ref[rows] = projected[:, 2 * width :].astype(BF16)
 
     poll()
+    ready(w_qkv_ref, cos_ref, sin_ref)
     project(wire.at)
     gather.wait_near()
     project(wire.near)
@@ -331,7 +450,9 @@
     gather.wait_diagonal(1)
     project(wire.diagonal)
 
+    done(a_ref, q_ref, k_ref, v_ref)
     poll()
+    ready(start_ref, w_out_ref)
     scatter = Scatter(wire, held, own, 1)
     for block in (3, 1, 2, 0):
         rows = slice(block * size, (block + 1) * size)
@@ -374,9 +495,10 @@
         def _():
             own[...] = partial
 
+    done(o_ref, lse_ref)
     branch = scatter.total()
     z_ref[...] = branch
-    middle = x_ref[...] + layer_norm(branch, gain_ref[1:2], shift_ref[1:2])
+    middle = x_ref[...].astype(F32) + layer_norm(branch, gain_ref[1:2], shift_ref[1:2])
     h_ref[...] = middle
     c_ref[...] = layer_norm(middle, gain_ref[2:3], shift_ref[2:3]).astype(BF16)
 
@@ -396,15 +518,15 @@
     )
 
 
-def feed_half_kernel(
+def feed_half_body(
+    wire, poll,
     c_ref, h_ref, gain_ref, shift_ref, w_up_ref, b_up_ref, w_down_ref,
     inner_ref, e_ref, d_ref, w_ref, y_ref,
-    held, own, sems,
+    held, own,
 ):
     size = c_ref.shape[0]
     half = size // 2
-    wire = Wire(sems)
-    wire.barrier()
+    ready(c_ref)
     gather = Gather(wire, inner_ref, size)
     for part in range(2):
         inner_ref[block_rows(wire.at, size, part, 2)] = c_ref[pl.ds(part * half, half)]
@@ -424,6 +546,7 @@
             d_ref[cut] = slope[at * step : (at + 1) * step]
         return dot(active, w_down_ref[...])
 
+    ready(w_up_ref, b_up_ref, w_down_ref)
     own[...] = feed([block_rows(wire.at, size)])
     gather.wait_near()
     scatter.put_near(feed([block_rows(wire.near, size)]))
@@ -435,25 +558,27 @@
         )
         scatter.put_diagonal(partial[:half], part)
         scatter.put_far(partial[half:], part)
+    done(inner_ref, e_ref, d_ref)
+    ready(h_ref)
     second = scatter.total()
     w_ref[...] = second
-    y_ref[...] = h_ref[...] + layer_norm(second, gain_ref[3:4], shift_ref[3:4])
-    wire.finish()
-
-
-def feed_half(inner, middle, gains, shifts, w_up, b_up, w_down):
+    result = h_ref[...] + layer_norm(second, gain_ref[3:4], shift_ref[3:4])
+    y_ref[...] = result.astype(BF16)
+
+
+def feed_half(number, inner, middle, gains, shifts, w_up, b_up, w_down):
     size, width = inner.shape
-    length, hidden = 4 * size, w_up.shape[1]
-    return call(
-        feed_half_kernel,
-        2,
+    length, hidden = 4 * size, b_up.shape[1]
+    return call_with(
+        feed_half_body,
+        Background(number),
         [((length, width), BF16)]
         + [((length, hidden), BF16)] * 2
-        + [((size, width), F32)] * 2,
+        + [((size, width), F32), ((size, width), BF16)],
         [pltpu.VMEM((6, size, width), BF16), pltpu.VMEM((size, width), F32)],
         4 * length * width * hidden,
         inner, middle, gains, shifts, w_up, b_up, w_down,
-    )
+    )[0]
 
 
 def feed_back_body(
@@ -464,11 +589,14 @@
 ):
     size = g_ref.shape[0]
     half = size // 2
+    ready(g_ref, w_ref)
     gather = Gather(wire, second, size)
     norms = [jnp.zeros((1, g_ref.shape[1]), F32)] * 2
     for part in range(2):
         rows = pl.ds(part * half, half)
-        grad, gain, shift = layer_norm_back(w_ref[rows], g_ref[rows], gain_ref[3:4])
+        grad, gain, shift = layer_norm_back(w_ref[rows], g_ref[rows].astype(F32), gain_ref[3:4])
+        if part == 0:
+            poll.enter()
         second[block_rows(wire.at, size, part, 2)] = grad.astype(BF16)
         gather.push(part)
         norms = [norms[0] + gain, norms[1] + shift]
@@ -490,6 +618,7 @@
         grad_b_ref[...] = bias if first else grad_b_ref[...] + bias
         return dot_t(grad, w_up_ref[...])
 
+    ready(d_ref, w_down_ref, w_up_ref)
     own[...] = feed([block_rows(wire.at, size)], True)
     poll()
     gather.wait_near()
@@ -505,29 +634,35 @@
         scatter.put_diagonal(partial[:half], part)
         scatter.put_far(partial[half:], part)
         poll()
+    poll.before("feed")
+    ready(e_ref, inner_ref)
     for at in range(0, e_ref.shape[1], 256):
         cut = slice(at, at + 256)
         grad_down_ref[cut, :] = t_dot(e_ref[:, cut], second[...]).astype(BF16)
         poll()
+    done(grad_down_ref)
     for at in range(0, inner_ref.shape[1], 256):
         cut = slice(at, at + 256)
         grad_up_ref[cut, :] = t_dot(inner_ref[:, cut], hidden[...]).astype(BF16)
         poll()
+    done(grad_up_ref)
     poll(3)
+    ready(h_ref, z_ref)
     grad, gain, shift = layer_norm_back(h_ref[...], scatter.total(), gain_ref[2:3])
     norms_ref[2:3] = gain
     norms_ref[6:7] = shift
-    grad = g_ref[...] + grad
+    grad = g_ref[...].astype(F32) + grad
     dh_ref[...] = grad
     grad, gain, shift = layer_norm_back(z_ref[...], grad, gain_ref[1:2])
     norms_ref[1:2] = gain
     norms_ref[5:6] = shift
     dz_ref[...] = grad.astype(BF16)
+    poll.leave()
 
 
 def feed_back(background, grad, second, middle, branch, gains, inner, active, slope, w_up, w_down):
     size, width = grad.shape
-    length, hidden = 4 * size, w_up.shape[1]
+    length, hidden = 4 * size, active.shape[1]
     return call_with(
         feed_back_body,
         background,
@@ -560,7 +695,9 @@
     size = dz_ref.shape[0]
     length, width = q_ref.shape
     half = size // 2
+    ready(dz_ref)
     gather = Gather(wire, branch, size)
+    poll.enter()
     for part in range(2):
         branch[block_rows(wire.at, size, part, 2)] = dz_ref[pl.ds(part * half, half)]
         gather.push(part)
@@ -572,6 +709,7 @@
     dk[...] = jnp.zeros_like(dk)
     dv[...] = jnp.zeros_like(dv)
     poll()
+    ready(w_out_ref)
     unmix(wire.at)
     gather.wait_near()
     unmix(wire.near)
@@ -584,7 +722,10 @@
     gather.wait_diagonal(0)
     gather.wait_diagonal(1)
     unmix(wire.diagonal)
+    ready(o_ref, q_ref, k_ref, v_ref, lse_ref, start_ref, cos_ref, sin_ref, w_qkv_ref)
+    poll.before("attend")
     grad_out_ref[...] = t_dot(o_ref[...], branch[...]).astype(BF16)
+    done(grad_out_ref)
     poll()
 
     pick_head = (
@@ -643,16 +784,20 @@
     poll()
     scatter.put_near(unproject(block_rows(wire.near, size)))
     own[...] = unproject(block_rows(wire.at, size))
+    ready(a_ref)
     for at in range(0, a_ref.shape[1], 256):
         cut = slice(at, at + 256)
         grad_qkv_ref[cut, :] = t_dot(a_ref[:, cut], projected[...]).astype(BF16)
         poll()
+    done(grad_qkv_ref)
     poll(3)
-    grad, gain, shift = layer_norm_back(x_ref[...], scatter.total(), gain_ref[0:1])
+    ready(x_ref, dh_ref)
+    grad, gain, shift = layer_norm_back(x_ref[...].astype(F32), scatter.total(), gain_ref[0:1])
     norms_ref[...] = jnp.zeros_like(norms_ref)
     norms_ref[0:1] = gain
     norms_ref[4:5] = shift
     dx_ref[...] = (dh_ref[...] + grad).astype(BF16)
+    poll.leave()
 
 
 def attend_back(
@@ -829,6 +974,11 @@
                     total = own.astype(F32) + self.across[pl.ds(at, CHUNK)].astype(F32)
                     self.final[pl.ds(at, CHUNK)] = total.astype(BF16)
 
+        for made in sum(self.copies + self.sides, []):
+            made.settle()
+        if not self.by_side:
+            self.side.settle()
+
 
 class Spread:
     def __init__(self, wire, line, view, rows, by_side):
@@ -993,7 +1143,7 @@
 
         @pl.when(line.at_end)
         def _():
-            slot[...] = final[:, columns(at)]
+            wire.move(final.at[:, columns(at)], slot)
 
     if qkv is not None:
         quarter = qkv.shape[0]
@@ -1015,7 +1165,7 @@
 
         @pl.when(line.at_end)
         def _():
-            full_qkv[rows, columns(2 * odd)] = qkv[:, columns((at + 1) // 2)]
+            wire.move(qkv.at[:, columns((at + 1) // 2)], full_qkv.at[rows, columns(2 * odd)])
 
     @pl.when(line.at_end)
     def _():
@@ -1088,103 +1238,10 @@
     )
 
 
-def place_own(line, spread, final):
+def place_own(wire, line, spread, final):
     @pl.when(line.at_end)
     def _():
-        spread.own()[...] = final[...]
-
-
-def fold_feed_steps(wire, line, refs, outs, scratch):
-    up, down = fold_pair(wire, line, refs, outs, scratch)
-    down.start()
-    sequence = Sequence(line)
-    chunks = up.chunks()
-    sequence.add(chunks).add(down.chunks())
-    sequence.after(chunks[-1], up.start_side)
-    yield from sequence.steps()
-    up.end()
-    down.end()
-
-
-def fold_attend_spread_feed_steps(wire, line, refs, outs, scratch):
-    out, qkv = fold_pair(wire, line, refs[0:2], outs[0:2], scratch)
-    up, down = spread_feed(wire, line, *outs[2:4])
-    place_own(line, up, refs[2])
-    home_wait = home(wire, line, refs[3], None, None, outs[3], None, None)
-    qkv.start()
-    up.start()
-    sequence = Sequence(line)
-    chunks = out.chunks()
-    sequence.add(chunks).before_next(home_wait)
-    sequence.add(down.chunks()).add(up.chunks(), qkv.chunks())
-    sequence.after(chunks[-1], out.start_side)
-    yield from sequence.steps()
-    out.end()
-    qkv.end()
-    down.end()
-
-
-def spread_attend_fold_feed_steps(wire, line, refs, outs, scratch):
-    out, qkv = spread_attend(wire, line, *outs[0:2])
-    up, down = fold_pair(wire, line, refs[2:4], outs[2:4], scratch)
-    home_wait = home(wire, line, None, refs[0], refs[1], None, *outs[0:2])
-    down.start()
-    sequence = Sequence(line)
-    chunks = up.chunks()
-    sequence.add(chunks[:2]).before_next(home_wait, out.start)
-    sequence.add(chunks[2:6], qkv.chunks()).add(chunks[6:], out.chunks()).add(down.chunks())
-    sequence.after(chunks[-1], up.start_side)
-    yield from sequence.steps()
-    up.end()
-    down.end()
-    qkv.end()
-
-
-def tail_steps(wire, line, grads, finals, full_feed, full_attend, own, scratch):
-    out, qkv = fold_pair(wire, line, grads, own, scratch)
-    up, down = spread_feed(wire, line, *full_feed)
-    full_out, full_qkv = spread_attend(wire, line, *full_attend)
-    place_own(line, up, finals[0])
-    home_wait = home(wire, line, finals[1], None, None, full_feed[1], None, None)
-    qkv.start()
-    up.start()
-    waits = []
-
-    def go_home():
-        out.end()
-        qkv.end()
-        waits.append(home(wire, line, None, *own, None, *full_attend))
-
-    sequence = Sequence(line)
-    out_chunks, qkv_chunks = out.chunks(), qkv.chunks()
-    sequence.add(out_chunks).before_next(home_wait)
-    sequence.add(down.chunks()).add(qkv_chunks).add(up.chunks())
-    sequence.before_next(lambda: waits[0](), full_out.start)
-    sequence.add(full_qkv.chunks()).add(full_out.chunks())
-    sequence.after(out_chunks[-1], out.start_side)
-    sequence.after(qkv_chunks[-1], go_home)
-    yield from sequence.steps()
-    down.end()
-    full_qkv.end()
-
-
-def fold_outs(blocks):
-    return [((block.shape[0] // 4, block.shape[1]), BF16) for block in blocks]
-
-
-def fold_scratch(blocks):
-    kinds = zip(blocks, (False, True))
-    return [entry for block, kind in kinds for entry in Fold.scratch(*block.shape, kind)]
-
-
-def feed_full(grads):
-    up, down = grads
-    return [(up.shape, BF16), ((4, down.shape[0], down.shape[1] // 4), BF16)]
-
-
-def attend_full(grads):
-    out, qkv = grads
-    return [((4, out.shape[0], out.shape[1] // 4), BF16), (qkv.shape, BF16)]
+        wire.move(final, spread.own())
 
 
 def swap_across(wire, source, target, first_sends):
@@ -1204,103 +1261,385 @@
         made.wait_recv()
 
 
-def tail_kernel(*refs):
-    sems, refs = refs[-1], refs[:-1]
-    grads, finals, small_refs, away, refs = refs[0:2], refs[2:4], refs[4:8], refs[8], refs[9:]
-    full_feed, full_attend, totals, came = refs[0:2], refs[2:4], refs[4:6], refs[6]
-    scratch = refs[7:]
-    wire, line = Wire(sems), Line()
-    wide_barrier(wire, line, Quad().across)
-    swap = swap_across(wire, away, came, False)
-    next(swap)
-    smalls = [
-        small_steps(wire, line, *small_refs[2 * at : 2 * at + 2], *scratch[4 * at : 4 * at + 4], totals[at])
-        for at in range(2)
+class Flow(Poll):
+    def __init__(self, wire, wide_wire, line, free):
+        super().__init__([])
+        self.wire, self.wide_wire, self.line, self.free = wire, wide_wire, line, free
+        self.sequence, self.done, self.limit, self.limits = Sequence(line), 0, 0, {}
+        self.entered = self.last = False
+        self.walk = None
+
+    def __call__(self, times=1):
+        for _ in range(times):
+            if self.walk is not None and self.done < self.limit:
+                self.done += 1
+                if next(self.walk, "end") == "end":
+                    self.walk = None
+
+    def until(self, count):
+        while self.walk is not None and self.done < min(count, self.limit):
+            self()
+
+    def open(self, limit):
+        self.limit = limit
+
+    def before(self, what):
+        self.until(self.limits.get(what, 0))
+
+    def enter(self):
+        if self.entered:
+            pl.semaphore_wait(self.free.at[0], 1)
+            pl.semaphore_wait(self.free.at[1], 1)
+        self.entered = True
+
+    def leave(self):
+        self.wire.finish()
+        self.wire.made = []
+        if self.last:
+            return
+        for at, peer in enumerate((self.wire.near, self.wire.far)):
+            pl.semaphore_signal(
+                self.free.at[at], inc=1, device_id={"narrow": peer}, device_id_type=MESH
+            )
+
+    def peers(self):
+        line = self.line
+        not_bottom, not_top = line.ways[0][3], line.ways[1][3]
+        return (
+            (2, line.up, not_top, not_bottom),
+            (3, line.down, not_bottom, not_top),
+            (4, line.side, None, None),
+        )
+
+    def greet(self):
+        for at, peer, sends, _ in self.peers():
+            signal = functools.partial(
+                pl.semaphore_signal, self.free.at[at], inc=1, device_id=peer, device_id_type=MESH
+            )
+            signal() if sends is None else pl.when(sends)(lambda signal=signal: signal())
+
+    def greeted(self):
+        for at, _, _, comes in self.peers():
+            wait = functools.partial(pl.semaphore_wait, self.free.at[at], 1)
+            wait() if comes is None else pl.when(comes)(lambda wait=wait: wait())
+
+
+FEED_NAMES = ("w", "h", "z", "inner", "e", "d", "down")
+ATTEND_NAMES = ("x", "a", "q", "k", "v", "o", "qkv", "out")
+
+
+def backward_kernel(shape, *refs):
+    size, length, width, hidden_count, part = shape
+    refs = list(refs)
+
+    def take(count):
+        taken = refs[:count]
+        del refs[:count]
+        return taken
+
+    dy, result, up, cosine, sine, start = take(6)
+    gains, logs, large = [], [], []
+    for _ in range(2):
+        gain, log = take(2)
+        gains.append(gain)
+        logs.append(log)
+        large.append(dict(zip(FEED_NAMES + ATTEND_NAMES, take(15))))
+    dx_out, grad_came, result_came = take(3)
+    totals = take(2)
+    fulls = [dict(zip(("up", "down", "out", "qkv"), take(4))) for _ in range(2)]
+    held_names = ("g", "up", "cos", "sin") + FEED_NAMES + ATTEND_NAMES
+    buffers = dict(zip(held_names, take(len(held_names))))
+    second, hidden, mixture, projected, dk, dv, held, own, dh, dz, dx = take(11)
+    grad_up, grad_down, grad_out, grad_qkv = take(4)
+    feed_scratch, attend_scratch = take(4), take(4)
+    finals = [dict(zip(("up", "down", "out", "qkv"), take(4))) for _ in range(2)]
+    small = [take(4) for _ in range(2)]
+    norms = [take(2) for _ in range(2)]
+    biases = take(2)
+    sems, wide_sems, local, free = take(4)
+
+    loads = {}
+
+    def load(layer, name, source):
+        at = held_names.index(name)
+        copy = pltpu.make_async_copy(source, buffers[name], local.at[at])
+        loads[layer, name] = Staged(buffers[name], copy, False)
+        loads[layer, name].begin()
+
+    def load_feed(layer):
+        load(layer, "up", up.at[layer])
+        for name in ("w", "d", "down", "e", "inner", "h", "z"):
+            load(layer, name, large[layer][name])
+
+    def load_attend(layer):
+        for name in ("out", "o", "q", "k", "v", "qkv", "a", "x"):
+            load(layer, name, large[layer][name])
+
+    load(1, "g", dy)
+    load_feed(1)
+    load_attend(1)
+    load(1, "cos", cosine)
+    load(1, "sin", sine)
+    wire, wide_wire, line = Wire(sems), Wire(wide_sems), Line()
+    wide_barrier(wide_wire, line, Quad().across)
+    result_swap = swap_across(wide_wire, result, result_came, True)
+    next(result_swap)
+
+    flow = Flow(wire, wide_wire, line, free)
+    sequence = flow.sequence
+    folds, spreads, waits = {}, {}, {}
+
+    def fold_feed(layer):
+        folds[layer, "up"], folds[layer, "down"] = fold_pair(
+            wide_wire, line, (grad_up, grad_down),
+            (finals[layer]["up"], finals[layer]["down"]), feed_scratch,
+        )
+
+    def fold_attend(layer):
+        folds[layer, "out"], folds[layer, "qkv"] = fold_pair(
+            wide_wire, line, (grad_out, grad_qkv),
+            (finals[layer]["out"], finals[layer]["qkv"]), attend_scratch,
+        )
+
+    for layer in range(2):
+        fold_feed(layer)
+        fold_attend(layer)
+        full = fulls[layer]
+        spreads[layer, "up"], spreads[layer, "down"] = spread_feed(
+            wide_wire, line, full["up"], full["down"]
+        )
+        spreads[layer, "out"], spreads[layer, "qkv"] = spread_attend(
+            wide_wire, line, full["out"], full["qkv"]
+        )
+
+    def go_home(layer, names):
+        final, full = finals[layer], fulls[layer]
+
+        def action():
+            for name in names:
+                folds[layer, name].end()
+            if names == ("down",):
+                waits[layer, names] = home(
+                    wide_wire, line, final["down"], None, None, full["down"], None, None
+                )
+            else:
+                waits[layer, names] = home(
+                    wide_wire, line, None, final["out"], final["qkv"], None, full["out"], full["qkv"]
+                )
+
+        return action
+
+    def come_home(layer, names):
+        return lambda: waits[layer, names]()
+
+    def spread_up(layer):
+        def action():
+            folds[layer, "up"].end()
+            place_own(wide_wire, line, spreads[layer, "up"], finals[layer]["up"])
+            spreads[layer, "up"].start()
+
+        return action
+
+    def fill(count):
+        while len(sequence.chunks) < count:
+            sequence.add([lambda way, role: None])
+
+    def feed_fold_part(layer):
+        sequence.before_next(folds[layer, "down"].start)
+        chunks = folds[layer, "up"].chunks()
+        sequence.add(chunks).add(folds[layer, "down"].chunks())
+        sequence.after(chunks[-1], folds[layer, "up"].start_side)
+        return len(sequence.chunks)
+
+    def attend_fold_feed_spread_part(layer, feed_end):
+        sequence.before_next(folds[layer, "qkv"].start)
+        chunks = folds[layer, "out"].chunks()
+        sequence.add(chunks)
+        sequence.after(chunks[-1], folds[layer, "out"].start_side)
+        sequence.actions.setdefault(feed_end - 1 + 3 * LATE, []).extend(
+            [go_home(layer, ("down",)), spread_up(layer)]
+        )
+        fill(feed_end + 2 * LATE)
+        qkv_chunks = folds[layer, "qkv"].chunks()
+        sequence.add(qkv_chunks)
+        qkv_end = len(sequence.chunks)
+        fill(feed_end + 3 * LATE + 2)
+        sequence.before_next(come_home(layer, ("down",)))
+        sequence.add(spreads[layer, "down"].chunks()).add(spreads[layer, "up"].chunks())
+        sequence.actions.setdefault(qkv_end - 1 + 3 * LATE, []).append(
+            go_home(layer, ("out", "qkv"))
+        )
+        fill(qkv_end + 3 * LATE + 2)
+        sequence.before_next(come_home(layer, ("out", "qkv")), spreads[layer, "out"].start)
+
+    feed_end = feed_fold_part(1)
+    in_attend_1 = len(sequence.chunks)
+    attend_fold_feed_spread_part(1, feed_end)
+    sequence.actions.setdefault(len(sequence.chunks) - 1, []).append(flow.greet)
+    sequence.add(spreads[1, "qkv"].chunks()).add(spreads[1, "out"].chunks())
+    sequence.before_next(flow.greeted)
+    in_feed_0 = len(sequence.chunks)
+    feed_end = feed_fold_part(0)
+    in_attend_0 = len(sequence.chunks)
+    attend_fold_feed_spread_part(0, feed_end)
+    sequence.add(spreads[0, "qkv"].chunks()).add(spreads[0, "out"].chunks())
+    flow.limits = {}
+
+    def feed(layer, grad):
+        held_now = {name: loads[layer, name] for name in FEED_NAMES + ("up",)}
+        feed_back_body(
+            wire, flow, grad, held_now["w"], held_now["h"], held_now["z"], gains[layer],
+            held_now["inner"], held_now["e"], held_now["d"], held_now["up"], held_now["down"],
+            grad_down, grad_up, biases[layer], norms[layer][0], dh, dz,
+            second, hidden, held, own,
+        )
+
+    def attend(layer):
+        names = {name: loads[layer, name] for name in ATTEND_NAMES}
+        attend_back_body(
+            wire, flow, dz, dh, names["x"], gains[layer], names["a"], names["q"], names["k"],
+            names["v"], names["o"], logs[layer], start, loads[1, "cos"], loads[1, "sin"],
+            names["qkv"], names["out"],
+            grad_qkv, grad_out, norms[layer][1], dx,
+            second, mixture, projected, dk, dv, held, own,
+        )
+        norms[layer][0][...] += norms[layer][1][...]
+
+    feed(1, loads[1, "g"])
+    flow.walk = sequence.steps()
+    flow.open(in_attend_1 - 1)
+    load_feed(0)
+    attend(1)
+    smalls = [small_steps(wide_wire, line, norms[1][0], biases[1], *small[1], totals[1])]
+    flow.open(in_feed_0 - 1)
+    load_attend(0)
+    flow.limits = {"feed": feed_limit(in_attend_1)}
+    feed(0, dx)
+    flow.open(in_attend_0 - 1)
+    flow.limits = {"attend": in_feed_0}
+    flow.last = True
+    attend(0)
+    moved = pltpu.make_async_copy(dx, dx_out, local.at[len(held_names)])
+    moved.start()
+    grad_swap = swap_across(wide_wire, dx, grad_came, False)
+    next(grad_swap)
+    flow.open(len(sequence.chunks) + 3 * LATE + 1)
+    smalls.append(small_steps(wide_wire, line, norms[0][0], biases[0], *small[0], totals[0]))
+    while flow.walk is not None or smalls:
+        flow()
+        for steps in list(smalls):
+            if next(steps, "end") == "end":
+                smalls.remove(steps)
+    for layer in range(2):
+        spreads[layer, "down"].end()
+        spreads[layer, "qkv"].end()
+    next(result_swap, None)
+    next(grad_swap, None)
+    moved.wait()
+    wide_wire.finish()
+    assert wire.used <= sems.shape[0] and wide_wire.used <= wide_sems.shape[0]
+
+
+def feed_limit(feed_end):
+    return feed_end + 3 * LATE + 1
+
+
+def backward_wide(grad, result, saved, weights, start, tables):
+    size, width = grad.shape
+    length, part = saved[0][2].shape
+    hidden_count = saved[0][10].shape[1]
+    shape = (size, length, width, hidden_count, part)
+    operands, specs = [], []
+
+    def give(array, large=True):
+        operands.append(array)
+        specs.append(pl.BlockSpec(memory_space=pl.ANY if large else pltpu.VMEM))
+
+    w_up = weights[0][2][0]
+    for array in (grad, result, w_up) + tables:
+        give(array)
+    give(start[None], False)
+    for layer in range(2):
+        w_qkv, w_out, _, _, w_down, gains, _ = weights[layer]
+        resid, normed, query, keys, values, mixture, logs, branch, middle, inner, active, slope, second = saved[layer]
+        give(gains, False)
+        give(logs, False)
+        for array in (second, middle, branch, inner, active, slope, w_down):
+            give(array)
+        for array in (resid, normed, query, keys, values, mixture, w_qkv, w_out):
+            give(array)
+    rows = ((size, width), BF16)
+    outs = [rows] * 3 + [((16, part), F32)] * 2
+    for _ in range(2):
+        outs += [
+            ((width, hidden_count), BF16),
+            ((4, hidden_count, part), BF16),
+            ((4, part, part), BF16),
+            ((width, 3 * part), BF16),
+        ]
+    out_specs = [pl.BlockSpec(memory_space=pl.ANY)] * 3 + vmem(2)
+    out_specs += [pl.BlockSpec(memory_space=pl.ANY)] * 8
+    line_rows = ((size, width), F32)
+    buffers = [
+        rows, ((width, hidden_count), BF16), (tables[0].shape, F32), (tables[1].shape, F32),
+        line_rows, line_rows, line_rows,
+        ((length, width), BF16), ((length, hidden_count), BF16), ((length, hidden_count), BF16),
+        ((hidden_count, width), BF16),
+        rows, ((length, width), BF16),
     ]
-    own = scratch[12:14]
-    steps = tail_steps(wire, line, grads, finals, full_feed, full_attend, own, scratch[8:12])
-    run(steps, *smalls)
-    next(swap, None)
-    wire.finish()
-
-
-def tail(attend, feed_finals, feed, norms, biases, away):
-    part = norms[0].shape[1] // 4
-    small = [
-        pltpu.VMEM((4, 8, part), F32),
-        pltpu.VMEM((16, part), F32),
-        pltpu.VMEM((16, part), F32),
-        pltpu.VMEM((4, 16, part), F32),
+    buffers += [((length, part), BF16)] * 4
+    buffers += [((width, 3 * part), BF16), ((part, width), BF16)]
+    buffers += [
+        ((length, width), BF16), ((length, hidden_count), BF16), ((length, part), BF16),
+        ((length, 3 * part), BF16), ((length, part), F32), ((length, part), F32),
+        ((6, size, width), BF16), line_rows, line_rows, rows, rows,
     ]
-    return call(
-        tail_kernel,
-        9,
-        feed_full(feed)
-        + attend_full(attend)
-        + [((16, part), F32)] * 2
-        + [(away.shape, away.dtype)],
-        small * 2
-        + fold_scratch(attend)
-        + [pltpu.VMEM(shape, kind) for shape, kind in fold_outs(attend)],
-        0,
-        *attend, *feed_finals, norms[0], biases[0], norms[1], biases[1], away,
-    )
-
-
-def backward_wide(grad, result, saved, weights, start, tables):
-    (grad_feed_1, norms_1, bias_1, grad_middle, grad_branch), (result_came,) = feed_backward(
-        Background(
-            3, [result], [(result.shape, result.dtype)], [],
-            lambda wire, quad, refs, outs, scratch: swap_across(wire, refs[0], outs[0], True),
-            quad=True, across=True,
+    grads = [
+        ((width, hidden_count), BF16), ((hidden_count, width), BF16),
+        ((part, width), BF16), ((width, 3 * part), BF16),
+    ]
+    buffers += grads
+    scratch = [pltpu.VMEM(*entry) for entry in buffers]
+    for (first, _), (last, _) in (grads[0:2], grads[2:4]):
+        scratch += Fold.scratch(*first, False) + Fold.scratch(*last, True)
+    for _ in range(2):
+        scratch += [pltpu.VMEM((rows // 4, columns), BF16) for (rows, columns), _ in grads]
+    for _ in range(2):
+        scratch += [
+            pltpu.VMEM((4, 8, part), F32),
+            pltpu.VMEM((16, part), F32),
+            pltpu.VMEM((16, part), F32),
+            pltpu.VMEM((4, 16, part), F32),
+        ]
+    scratch += [pltpu.VMEM((8, width), F32)] * 4
+    scratch += [pltpu.VMEM((1, hidden_count), F32)] * 2
+    scratch += [
+        pltpu.SemaphoreType.DMA((88,)),
+        pltpu.SemaphoreType.DMA((520,)),
+        pltpu.SemaphoreType.DMA((20,)),
+        pltpu.SemaphoreType.REGULAR((5,)),
+    ]
+    found = pl.pallas_call(
+        functools.partial(backward_kernel, shape),
+        in_specs=specs,
+        out_specs=out_specs,
+        out_shape=shaped(*outs),
+        scratch_shapes=scratch,
+        compiler_params=pltpu.CompilerParams(
+            collective_id=3, has_side_effects=True, vmem_limit_bytes=62 * 2**20
         ),
-        grad, saved[1], weights[1],
-    )
-    (grad_attend_1, norms, grad), finals_1 = attend_backward(
-        Background(
-            4, grad_feed_1, fold_outs(grad_feed_1), fold_scratch(grad_feed_1),
-            fold_feed_steps,
-        ),
-        grad_branch, grad_middle, saved[1], weights[1], start, tables,
-    )
-    norms_1 = norms_1 + norms
-
-    (grad_feed_0, norms_0, bias_0, grad_middle, grad_branch), results = feed_backward(
-        Background(
-            6, list(grad_attend_1) + list(finals_1),
-            fold_outs(grad_attend_1) + feed_full(grad_feed_1), fold_scratch(grad_attend_1),
-            fold_attend_spread_feed_steps,
-        ),
-        grad.astype(F32), saved[0], weights[0],
-    )
-    finals_1, full_feed_1 = results[:2], results[2:]
-
-    (grad_attend_0, norms, grad), results = attend_backward(
-        Background(
-            7, list(finals_1) + list(grad_feed_0),
-            attend_full(grad_attend_1) + fold_outs(grad_feed_0), fold_scratch(grad_feed_0),
-            spread_attend_fold_feed_steps,
-        ),
-        grad_branch, grad_middle, saved[0], weights[0], start, tables,
-    )
-    norms_0 = norms_0 + norms
-    full_attend_1, finals_0 = results[:2], results[2:]
-    results = tail(
-        grad_attend_0, finals_0, grad_feed_0, (norms_0, norms_1), (bias_0, bias_1), grad
-    )
-    full_feed_0, full_attend_0, totals = results[:2], results[2:4], results[4:6]
-    grad_came = results[6]
-
-    def shards(feed, attend, total):
-        up, down = feed
-        out, qkv = attend
+        name="backward",
+    )(*operands)
+    grad, grad_came, result_came = found[:3]
+    totals = found[3:5]
+
+    def shards(layer):
+        up, down, out, qkv = found[5 + 4 * layer : 9 + 4 * layer]
         out, down = (block.reshape(-1, block.shape[2]) for block in (out, down))
+        total = totals[layer]
         return qkv, out, up, total[8:12].reshape(-1), down, total[:4], total[4:8]
 
-    return grad, grad_came, result_came, (
-        shards(full_feed_0, full_attend_0, totals[0]),
-        shards(full_feed_1, full_attend_1, totals[1]),
-    )
+    return grad, grad_came, result_came, (shards(0), shards(1))
 
 
 class Quad:
@@ -1405,14 +1744,28 @@
 
 def begin_kernel(
     blocks_ref, w_qkv_ref, w_out_ref, norms_ref,
-    qkv_ref, out_ref, full_norms_ref, came_ref,
+    qkv_ref, out_ref, full_norms_ref, x_ref, dy_ref,
     local, sems,
 ):
     wire, quad = Wire(sems), Quad()
     quad_barrier(wire, quad, quad.across)
-    size = came_ref.shape[0]
-    away = blocks_ref.at[span(quad.first.astype(jnp.int32) * size, size)]
-    swap = wire.send(away, came_ref, quad.across)
+    size = x_ref.shape[0]
+    blocks = [blocks_ref.at[pl.ds(at * size, size)] for at in range(2)]
+    second = jnp.logical_not(quad.first)
+    x_swap = wire.copy(blocks[1], x_ref, quad.across, quad.first)
+    dy_swap = wire.copy(blocks[0], dy_ref, quad.across, second)
+    kept = local.at[3]
+
+    @pl.when(quad.first)
+    def _():
+        x_swap.start()
+        pltpu.make_async_copy(blocks[0], x_ref, kept).start()
+
+    @pl.when(second)
+    def _():
+        dy_swap.start()
+        pltpu.make_async_copy(blocks[1], dy_ref, kept).start()
+
     fetches = [
         Fetch(wire, w_qkv_ref.at[0], qkv_ref, True),
         Fetch(wire, w_out_ref.at[0], out_ref, False),
@@ -1429,7 +1782,17 @@
     for made in sent:
         made.wait_recv()
     own.wait()
-    swap.wait_recv()
+
+    @pl.when(quad.first)
+    def _():
+        pltpu.make_async_copy(blocks[0], x_ref, kept).wait()
+        dy_swap.wait_recv()
+
+    @pl.when(second)
+    def _():
+        pltpu.make_async_copy(blocks[1], dy_ref, kept).wait()
+        x_swap.wait_recv()
+
     wire.finish()
 
 
@@ -1444,13 +1807,14 @@
         ((w_out.shape[2], width), BF16),
         ((norms.shape[0], width), BF16),
         ((blocks.shape[0] // 2, width), BF16),
+        ((blocks.shape[0] // 2, width), BF16),
     ]
     return pl.pallas_call(
         begin_kernel,
         in_specs=anywhere(4),
-        out_specs=anywhere(4),
+        out_specs=anywhere(5),
         out_shape=shaped(*shapes),
-        scratch_shapes=[pltpu.SemaphoreType.DMA((8,)), pltpu.SemaphoreType.DMA((SEMAPHORES,))],
+        scratch_shapes=[pltpu.SemaphoreType.DMA((8,)), pltpu.SemaphoreType.DMA((40,))],
         compiler_params=pltpu.CompilerParams(collective_id=10, has_side_effects=True),
         name="begin",
     )(blocks, w_qkv, w_out, norms)
@@ -1529,7 +1893,7 @@
     if background is not None:
         w_down = more[0]
     inner, active, slope, second, result = feed_half(
-        inner, middle, gains, shifts, w_up, b_up, w_down
+        20 + w_up[1], inner, middle, gains, shifts, w_up, b_up, w_down
     )
     return result, more, (
         resid, normed, query, keys, values, mixture, logs, branch, middle, inner, active, slope, second
@@ -1557,7 +1921,7 @@
 
 def layer_backward(grad, saved, weights, start, tables):
     ((grad_up, grad_down), norms, grad_b_up, grad_middle, grad_branch), _ = feed_backward(
-        Background(3), grad, saved, weights
+        Background(30 + weights[2][1]), grad, saved, weights
     )
     ((grad_out, grad_qkv), norms_too, grad), _ = attend_backward(
         Background(4), grad_branch, grad_middle, saved, weights, start, tables
@@ -1613,16 +1977,16 @@
     norms = jnp.concatenate([norm_gain, norm_bias]).reshape(16, -1)
 
     if wide == 8:
-        qkv_0, out_0, norms, came = begin(ends, w_qkv, w_out, norms)
+        qkv_0, out_0, norms, resid, upstream = begin(ends, w_qkv, w_out, norms)
     else:
         came = route(jnp.where(first, ends[row_count:], ends[:row_count]))
         norms = lax.all_gather(norms, "narrow", axis=1, tiled=True)
         qkv_0, out_0 = by_heads(w_qkv[0], at), to_rows(w_out[0])
         down_0, down_1 = to_rows(w_down[0]), to_rows(w_down[1])
         qkv_1, out_1 = by_heads(w_qkv[1], at), to_rows(w_out[1])
+        resid = jnp.where(first, ends[:row_count], came)
+        upstream = jnp.where(first, came, ends[row_count:])
     norms = norms.astype(F32)
-    resid = jnp.where(first, ends[:row_count], came).astype(F32)
-    upstream = jnp.where(first, came, ends[row_count:]).astype(F32)
 
     if wide == 8:
         width = ends.shape[1]
@@ -1635,20 +1999,18 @@
                 ((part, width), BF16),
                 ((w_up.shape[2], width), BF16),
             ],
-            [pltpu.SemaphoreType.DMA((4,))] * 2, fetch_rest_steps, quad=True,
+            [pltpu.SemaphoreType.DMA((4,))] * 2, fetch_rest_steps, quad=True, semaphores=72,
         )
-        weights_0 = (qkv_0, out_0, w_up[0], b_up[0], None, norms[0:4], norms[8:12])
+        weights_0 = (qkv_0, out_0, (w_up, 0), b_up[0], None, norms[0:4], norms[8:12])
         middle, more, saved_first = layer_forward(resid, weights_0, start, tables, background)
         down_0, qkv_1, out_1, down_1 = more
         weights_0 = weights_0[:4] + (down_0,) + weights_0[5:]
     else:
-        weights_0 = (qkv_0, out_0, w_up[0], b_up[0], down_0, norms[0:4], norms[8:12])
+        weights_0 = (qkv_0, out_0, (w_up, 0), b_up[0], down_0, norms[0:4], norms[8:12])
         middle, _, saved_first = layer_forward(resid, weights_0, start, tables)
-    weights_1 = (qkv_1, out_1, w_up[1], b_up[1], down_1, norms[4:8], norms[12:16])
+    weights_1 = (qkv_1, out_1, (w_up, 1), b_up[1], down_1, norms[4:8], norms[12:16])
     weights = (weights_0, weights_1)
-    middle = middle.astype(BF16).astype(F32)
     result, _, saved_second = layer_forward(middle, weights_1, start, tables)
-    result = result.astype(BF16)
     if wide == 8:
         grad, grad_came, result_came, (totals_first, totals_second) = backward_wide(
             upstream, result, (saved_first, saved_second), weights, start, tables
@@ -1657,7 +2019,7 @@
         result_came = route(result)
         grad, grads_second = layer_backward(upstream, saved_second, weights_1, start, tables)
         totals_second = reduce_grads(grads_second, at)
-        grad, grads_first = layer_backward(grad.astype(F32), saved_first, weights_0, start, tables)
+        grad, grads_first = layer_backward(grad, saved_first, weights_0, start, tables)
         totals_first = reduce_grads(grads_first, at)
         grad_came = route(grad)
 

time: 679 us -> 553 us (0.81)
  Pallas kernels: 619 us -> 513 us
  local copies, waits for them, and re-layouts: 21.6 us -> 6.16 us
    pallas_call x10 -> x6, Pallas kernels: 619 us -> 513 us  [the longest x1 313 us: backward_wide(): pl.pallas_call(functools.partial(backward_kernel, shape), in_specs=specs,...]
    unnamed x52 -> x30, local copies, waits for them, and re-layouts: 13.5 us -> 1.5 us
    convert_element_type x4 -> x0, other arithmetic: 7.2 us -> none  [the longest x1 2.51 us: on_device(): resid = jnp.where(first, ends[:row_count], came).astype(F32)]
where the time goes in v4:
time: 553 us; the launch traced here: 543 us
  Pallas kernels  513 us (93%)
  other arithmetic  22.5 us (4%)
  local copies, waits for them, and re-layouts  6.16 us (1%)
    pallas_call x1, Pallas kernels, backward_wide(): pl.pallas_call(functools.partial(backward_kernel, shape), in_specs=specs,...  313 us
    pallas_call x4, Pallas kernels, call_with(): pl.pallas_call(kernel, in_specs=[spec(raw or copied) for raw, copied in z...  158 us
    pallas_call x1, Pallas kernels, begin(): pl.pallas_call(begin_kernel, in_specs=anywhere(4), out_specs=anywhere(5),...  41.6 us
    another operation x7, other arithmetic, on_device(): jnp.stack([a.astype(F32), b.astype(F32)])  14.9 us

profile of v4, /device:TPU:0, one launch (start us, length us, event | category | flops | bytes accessed | tf_op | source)
XLA Modules:
  0.0 542.6 jit_solution(16118295491094795198)
XLA Ops:
  0.6 0.0 copy-start
  0.7 0.7 copy-done
  1.3 0.2 dynamic-slice_reduce_fusion
  1.6 0.2 reduce-window.8
  1.7 0.1 select_reduce_fusion
  1.8 0.0 copy-start.11
  1.9 0.7 pad_maximum_fusion.2
  2.6 0.6 reshape.113.norms_ref
  3.2 1.4 fusion.2
  4.6 1.0 copy.22.refs_5_
  5.6 1.9 fusion
  7.5 1.8 pad_maximum_fusion
  9.3 0.0 copy-done.11
  9.3 41.6 %begin.1 = (bf16[1024,768]{1,0:T(8,128)(2,1)}, bf16[256,1024]{1,0:T(8,128)(2,1)}, bf16[16,1024]{1,0:T(8,128)(2,1)}, bf16[256,1024]{1,0:T(8,128)(2,1)}, bf16[256,1024]{1,0:T(8,128)(2,1)}) custom-call(bf16[512,1024]{1,0:T(8,128)(2,1)} %blocks_ref.1, bf16[2,1024,768]{2,1,0:T(8,128)(2,1)} %refs_8_.1, bf16[2,1024,256]{2,1,0:T(8,128)(2,1)} %refs_9_.1, ...), custom_call_target="tpu_custom_call" | custom-call | tf_op jit(solution)/shard_map/begin/pallas_call | solution.py:1812
  50.9 1.4 fusion.1
  52.4 60.0 %attend_half_body_wide.1 = (bf16[1024,1024]{1,0:T(8,128)(2,1)}, bf16[1024,256]{1,0:T(8,128)(2,1)}, bf16[1024,256]{1,0:T(8,128)(2,1)}, bf16[1024,256]{1,0:T(8,128...) custom-call(bf16[256,1024]{1,0:T(8,128)(2,1)} %get-tuple-element.59., ...), custom_call_target="tpu_custom_call" | custom-call | flops 3221225472 | bytes 16777216 | tf_op jit(solution)/shard_map/attend_half_body_wide/pallas_call | solution.py:398
  112.3 29.3 %feed_half_body.2 = (bf16[1024,1024]{1,0:T(8,128)(2,1)}, bf16[1024,1024]{1,0:T(8,128)(2,1)}, bf16[1024,1024]{1,0:T(8,128)(2,1)}, f32[256,1024]{1,0:T(8,128)}, bf16[256,1024]{1,0:T(8,128)(2,1)}) custom-call(bf16[256,1024]{1,0:T(8,128)(2,1)} %get-tuple-element.63.refs_0_, f32[256,1024]{1,0:T(8,128)} %get-tuple-element.64.refs_1_.refs_9_, ...), custom_call_target="tpu_custom_call" | custom-call | flops 4294967296 | bytes 16777216 | tf_op jit(solution)/shard_map/feed_half_body/pallas_call | solution.py:398
  141.7 40.9 %attend_half_body.1 = (bf16[1024,1024]{1,0:T(8,128)(2,1)}, bf16[1024,256]{1,0:T(8,128)(2,1)}, bf16[1024,256]{1,0:T(8,128)(2,1)}, bf16[1024,256]{1,0:T(8,128)(2,1...) custom-call(bf16[256,1024]{1,0:T(8,128)(2,1)} %get-tuple-element.66., ...), custom_call_target="tpu_custom_call" | custom-call | flops 3221225472 | bytes 16777216 | tf_op jit(solution)/shard_map/attend_half_body/pallas_call | solution.py:398
  182.6 27.8 %feed_half_body.3 = (bf16[1024,1024]{1,0:T(8,128)(2,1)}, bf16[1024,1024]{1,0:T(8,128)(2,1)}, bf16[1024,1024]{1,0:T(8,128)(2,1)}, f32[256,1024]{1,0:T(8,128)}, bf16[256,1024]{1,0:T(8,128)(2,1)}) custom-call(bf16[256,1024]{1,0:T(8,128)(2,1)} %get-tuple-element.69.refs_0_, f32[256,1024]{1,0:T(8,128)} %get-tuple-element.70.refs_1_.refs_26_, ...), custom_call_target="tpu_custom_call" | custom-call | flops 4294967296 | bytes 16777216 | tf_op jit(solution)/shard_map/feed_half_body/pallas_call | solution.py:398
  210.4 0.0 copy-start.2
  210.4 313.2 %backward.1 = (bf16[256,1024]{1,0:T(8,128)(2,1)}, bf16[256,1024]{1,0:T(8,128)(2,1)}, bf16[256,1024]{1,0:T(8,128)(2,1)}, f32[16,256]{1,0:T(8,128)}, f32[16,256]{1...) custom-call(bf16[256,1024]{1,0:T(8,128)(2,1)} %get-tuple-element.58., ...), custom_call_target="tpu_custom_call" | custom-call | tf_op jit(solution)/shard_map/backward/pallas_call | solution.py:1622
  523.7 2.9 maximum_select_fusion
  526.6 0.6 pad_maximum_fusion.5
  527.2 0.6 pad_maximum_fusion.4
  527.8 0.6 pad_maximum_fusion.3
  528.4 0.0 copy-done.10
  528.4 1.5 maximum_convert_fusion.3
  529.9 0.0 copy-done.7
  529.9 3.5 maximum_convert_fusion.2
  533.4 0.8 copy-done.6
  534.2 4.2 maximum_convert_fusion
  538.4 3.9 maximum_convert_fusion.1
  (26 shorter events, 0.1 us)
Async XLA Ops:
  0.6 0.7 copy-start
  1.8 7.5 %copy-start.11 = (s32[1024]{0:T(1024)}, s32[1024]{0:T(1024)S(1)}, u32[]{:S(2)}) copy-start(s32[1024]{0:T(1024)S(1)} %select_reduce_fusion) | copy-start | bytes 12292
  210.4 313.3 %copy-start.2 = (bf16[256,1024]{1,0:T(8,128)(2,1)S(1)}, bf16[256,1024]{1,0:T(8,128)(2,1)}, u32[]{:S(2)}) copy-start(bf16[256,1024]{1,0:T(8,128)(2,1)} %get-tuple-element.72.refs_1_) | copy-start | bytes 1572868
  523.6 2.9 copy-start.13
  523.7 2.9 copy-start.12
  523.7 4.8 copy-start.9
  523.7 4.8 copy-start.10
  526.6 3.3 copy-start.7
  526.6 3.3 copy-start.8
  529.9 3.5 copy-start.5
  529.9 4.3 copy-start.6
  534.2 4.2 copy-start.3
  534.2 4.2 copy-start.4
  538.4 3.9 copy-start.1

commit v5 on v4

--- a/solution.py
+++ b/solution.py
@@ -253,6 +253,9 @@
     def before(self, what):
         pass
 
+    def graded(self, name):
+        pass
+
 
 SMALL = 2**16
 
@@ -288,10 +291,32 @@
         self.ref[index] = value
 
 
+class Pending(Staged):
+    def __init__(self, ref, action):
+        super().__init__(ref, None, False)
+        self.action = action
+
+    def wait(self):
+        if not self.ended:
+            self.ended = True
+            self.action()
+
+    def wait_part(self, part):
+        self.ended = True
+        self.action(part)
+
+
 def ready(*refs):
     for ref in refs:
         if isinstance(ref, Staged):
             ref.wait()
+
+
+def ready_part(ref, part):
+    if isinstance(ref, Pending):
+        ref.wait_part(part)
+    else:
+        ready(ref)
 
 
 def done(*refs):
@@ -421,13 +446,15 @@
     held, own,
 ):
     size = x_ref.shape[0]
-    ready(x_ref)
     gather = Gather(wire, a_ref, size)
+    poll.enter()
     for part in range(2):
         rows = pl.ds(part * (size // 2), size // 2)
+        ready_part(x_ref, part)
         normed = layer_norm(x_ref[rows].astype(F32), gain_ref[0:1], shift_ref[0:1])
         a_ref[block_rows(wire.at, size, part, 2)] = normed.astype(BF16)
         gather.push(part)
+        poll()
     width = q_ref.shape[1]
 
     def project(block):
@@ -438,7 +465,6 @@
         k_ref[rows] = turn(projected[:, width : 2 * width], cosine, sine).astype(BF16)
         v_ref[rows] = projected[:, 2 * width :].astype(BF16)
 
-    poll()
     ready(w_qkv_ref, cos_ref, sin_ref)
     project(wire.at)
     gather.wait_near()
@@ -476,7 +502,7 @@
         lse_ref[:, rows] = logs.T[: lse_ref.shape[0]]
         partial = dot(o_ref[rows, :], w_out_ref[...])
 
-        if block in (1, 2):
+        if block == 2:
             poll()
 
         @pl.when(wire.diagonal == block)
@@ -496,11 +522,14 @@
             own[...] = partial
 
     done(o_ref, lse_ref)
+    poll()
     branch = scatter.total()
     z_ref[...] = branch
     middle = x_ref[...].astype(F32) + layer_norm(branch, gain_ref[1:2], shift_ref[1:2])
     h_ref[...] = middle
     c_ref[...] = layer_norm(middle, gain_ref[2:3], shift_ref[2:3]).astype(BF16)
+    done(z_ref, h_ref)
+    poll.leave()
 
 
 def attend_half(background, resid, gains, shifts, cosine, sine, start, w_qkv, w_out):
@@ -528,9 +557,11 @@
     half = size // 2
     ready(c_ref)
     gather = Gather(wire, inner_ref, size)
+    poll.enter()
     for part in range(2):
         inner_ref[block_rows(wire.at, size, part, 2)] = c_ref[pl.ds(part * half, half)]
         gather.push(part)
+    poll()
     scatter = Scatter(wire, held, own, 2)
 
     def feed(cuts):
@@ -564,6 +595,8 @@
     w_ref[...] = second
     result = h_ref[...] + layer_norm(second, gain_ref[3:4], shift_ref[3:4])
     y_ref[...] = result.astype(BF16)
+    done(w_ref, y_ref)
+    poll.leave()
 
 
 def feed_half(number, inner, middle, gains, shifts, w_up, b_up, w_down):
@@ -636,16 +669,18 @@
         poll()
     poll.before("feed")
     ready(e_ref, inner_ref)
+    for at in range(0, inner_ref.shape[1], 256):
+        cut = slice(at, at + 256)
+        grad_up_ref[cut, :] = t_dot(inner_ref[:, cut], hidden[...]).astype(BF16)
+        poll()
+    done(grad_up_ref)
+    poll.graded("up")
     for at in range(0, e_ref.shape[1], 256):
         cut = slice(at, at + 256)
         grad_down_ref[cut, :] = t_dot(e_ref[:, cut], second[...]).astype(BF16)
         poll()
     done(grad_down_ref)
-    for at in range(0, inner_ref.shape[1], 256):
-        cut = slice(at, at + 256)
-        grad_up_ref[cut, :] = t_dot(inner_ref[:, cut], hidden[...]).astype(BF16)
-        poll()
-    done(grad_up_ref)
+    poll.graded("down")
     poll(3)
     ready(h_ref, z_ref)
     grad, gain, shift = layer_norm_back(h_ref[...], scatter.total(), gain_ref[2:3])
@@ -790,6 +825,7 @@
         grad_qkv_ref[cut, :] = t_dot(a_ref[:, cut], projected[...]).astype(BF16)
         poll()
     done(grad_qkv_ref)
+    poll.graded("qkv")
     poll(3)
     ready(x_ref, dh_ref)
     grad, gain, shift = layer_norm_back(x_ref[...].astype(F32), scatter.total(), gain_ref[0:1])
@@ -974,10 +1010,13 @@
                     total = own.astype(F32) + self.across[pl.ds(at, CHUNK)].astype(F32)
                     self.final[pl.ds(at, CHUNK)] = total.astype(BF16)
 
+        self.settle()
+        if not self.by_side:
+            self.side.settle()
+
+    def settle(self):
         for made in sum(self.copies + self.sides, []):
             made.settle()
-        if not self.by_side:
-            self.side.settle()
 
 
 class Spread:
@@ -1267,7 +1306,8 @@
         self.wire, self.wide_wire, self.line, self.free = wire, wide_wire, line, free
         self.sequence, self.done, self.limit, self.limits = Sequence(line), 0, 0, {}
         self.entered = self.last = False
-        self.walk = None
+        self.smalls, self.ticks = [], 0
+        self.walk, self.on_grade = None, {}
 
     def __call__(self, times=1):
         for _ in range(times):
@@ -1275,6 +1315,11 @@
                 self.done += 1
                 if next(self.walk, "end") == "end":
                     self.walk = None
+            self.ticks += 1
+            if self.ticks % 4 == 0 or self.walk is None:
+                for steps in list(self.smalls):
+                    if next(steps, "end") == "end":
+                        self.smalls.remove(steps)
 
     def until(self, count):
         while self.walk is not None and self.done < min(count, self.limit):
@@ -1282,6 +1327,10 @@
 
     def open(self, limit):
         self.limit = limit
+
+    def graded(self, name):
+        for action in self.on_grade.pop(name, []):
+            action()
 
     def before(self, what):
         self.until(self.limits.get(what, 0))
@@ -1445,7 +1494,8 @@
             sequence.add([lambda way, role: None])
 
     def feed_fold_part(layer):
-        sequence.before_next(folds[layer, "down"].start)
+        if layer == 0:
+            sequence.before_next(folds[layer, "down"].start)
         chunks = folds[layer, "up"].chunks()
         sequence.add(chunks).add(folds[layer, "down"].chunks())
         sequence.after(chunks[-1], folds[layer, "up"].start_side)
@@ -1457,15 +1507,15 @@
         sequence.add(chunks)
         sequence.after(chunks[-1], folds[layer, "out"].start_side)
         sequence.actions.setdefault(feed_end - 1 + 3 * LATE, []).extend(
-            [go_home(layer, ("down",)), spread_up(layer)]
+            [go_home(layer, ("down",)), folds[layer, "up"].settle]
         )
-        fill(feed_end + 2 * LATE)
-        qkv_chunks = folds[layer, "qkv"].chunks()
-        sequence.add(qkv_chunks)
-        qkv_end = len(sequence.chunks)
         fill(feed_end + 3 * LATE + 2)
         sequence.before_next(come_home(layer, ("down",)))
-        sequence.add(spreads[layer, "down"].chunks()).add(spreads[layer, "up"].chunks())
+        sequence.add(spreads[layer, "down"].chunks())
+        sequence.before_next(spread_up(layer))
+        sequence.add(folds[layer, "qkv"].chunks())
+        qkv_end = len(sequence.chunks)
+        sequence.add(spreads[layer, "up"].chunks())
         sequence.actions.setdefault(qkv_end - 1 + 3 * LATE, []).append(
             go_home(layer, ("out", "qkv"))
         )
@@ -1505,31 +1555,40 @@
         )
         norms[layer][0][...] += norms[layer][1][...]
 
+    def open_to(limit):
+        return lambda: flow.open(limit)
+
+    def set_out():
+        flow.walk = sequence.steps()
+
+    flow.on_grade = {
+        "down": [set_out, folds[1, "down"].start, open_to(in_attend_1 - 1)],
+        "qkv": [open_to(in_feed_0 - 1)],
+    }
     feed(1, loads[1, "g"])
-    flow.walk = sequence.steps()
-    flow.open(in_attend_1 - 1)
     load_feed(0)
     attend(1)
-    smalls = [small_steps(wide_wire, line, norms[1][0], biases[1], *small[1], totals[1])]
-    flow.open(in_feed_0 - 1)
+    flow.smalls.append(
+        small_steps(wide_wire, line, norms[1][0], biases[1], *small[1], totals[1])
+    )
     load_attend(0)
-    flow.limits = {"feed": feed_limit(in_attend_1)}
+    flow.limits = {"feed": feed_limit(in_attend_1), "attend": in_feed_0}
+    flow.on_grade = {
+        "down": [open_to(in_attend_0 - 1)],
+        "qkv": [open_to(len(sequence.chunks) + 3 * LATE + 1)],
+    }
     feed(0, dx)
-    flow.open(in_attend_0 - 1)
-    flow.limits = {"attend": in_feed_0}
     flow.last = True
     attend(0)
     moved = pltpu.make_async_copy(dx, dx_out, local.at[len(held_names)])
     moved.start()
     grad_swap = swap_across(wide_wire, dx, grad_came, False)
     next(grad_swap)
-    flow.open(len(sequence.chunks) + 3 * LATE + 1)
-    smalls.append(small_steps(wide_wire, line, norms[0][0], biases[0], *small[0], totals[0]))
-    while flow.walk is not None or smalls:
+    flow.smalls.append(
+        small_steps(wide_wire, line, norms[0][0], biases[0], *small[0], totals[0])
+    )
+    while flow.walk is not None or flow.smalls:
         flow()
-        for steps in list(smalls):
-            if next(steps, "end") == "end":
-                smalls.remove(steps)
     for layer in range(2):
         spreads[layer, "down"].end()
         spreads[layer, "qkv"].end()
@@ -1633,13 +1692,16 @@
     grad, grad_came, result_came = found[:3]
     totals = found[3:5]
 
-    def shards(layer):
-        up, down, out, qkv = found[5 + 4 * layer : 9 + 4 * layer]
-        out, down = (block.reshape(-1, block.shape[2]) for block in (out, down))
-        total = totals[layer]
-        return qkv, out, up, total[8:12].reshape(-1), down, total[:4], total[4:8]
-
-    return grad, grad_came, result_came, (shards(0), shards(1))
+    sums = [
+        jnp.stack([block.reshape(-1, block.shape[-1]).astype(F32) for block in pair])
+        for pair in zip(found[5:9], found[9:13])
+    ]
+    bias = jnp.stack([total[8:12].reshape(-1) for total in totals])
+    gains, shifts = (
+        jnp.stack([total[at : at + 4] for total in totals]) for at in (0, 4)
+    )
+    up, down, out, qkv = sums
+    return grad, grad_came, result_came, (qkv, out, up, bias, down, gains, shifts)
 
 
 class Quad:
@@ -1704,7 +1766,7 @@
         for source, target, peer in fetch.far:
             sent.append(wire.send(source(rows), target(rows), {"narrow": peer}))
         nears.append(wire.send(*fetch.near, {"narrow": wire.near}))
-        copies.append(pltpu.make_async_copy(*fetch.own, local.at[at]))
+        copies.append(pltpu.make_async_copy(*fetch.own, local[at]))
         copies[-1].start()
     yield
     for made in sent:
@@ -1742,106 +1804,279 @@
     greet(narrow + [quad.side, quad.mate] + list(others))
 
 
-def begin_kernel(
-    blocks_ref, w_qkv_ref, w_out_ref, norms_ref,
-    qkv_ref, out_ref, full_norms_ref, x_ref, dy_ref,
-    local, sems,
-):
-    wire, quad = Wire(sems), Quad()
-    quad_barrier(wire, quad, quad.across)
-    size = x_ref.shape[0]
-    blocks = [blocks_ref.at[pl.ds(at * size, size)] for at in range(2)]
+class Hand(Poll):
+    def __init__(self, wire, free, actions):
+        super().__init__([])
+        self.wire, self.free, self.actions = wire, free, list(actions)
+        self.entered = self.last = False
+        self.settled = ()
+
+    def __call__(self, times=1):
+        for _ in range(times):
+            if self.actions:
+                for action in self.actions.pop(0):
+                    action()
+
+    def enter(self):
+        if self.entered:
+            pl.semaphore_wait(self.free.at[0], 1)
+            pl.semaphore_wait(self.free.at[1], 1)
+        self.entered = True
+
+    def leave(self):
+        self.wire.finish()
+        self.wire.made = []
+        ready(*self.settled)
+        if self.last:
+            return
+        for at, peer in enumerate((self.wire.near, self.wire.far)):
+            pl.semaphore_signal(
+                self.free.at[at], inc=1, device_id={"narrow": peer}, device_id_type=MESH
+            )
+
+
+WEIGHT_NAMES = ("qkv", "out", "down")
+KEPT_NAMES = ("a", "q", "k", "v", "o", "lse", "z", "h", "inner", "e", "d", "w", "y")
+
+
+def forward_kernel(size, *refs):
+    refs = list(refs)
+
+    def take(count):
+        taken = refs[:count]
+        del refs[:count]
+        return taken
+
+    ends, w_qkv, w_out, w_down, w_up, norms, b_up, cosine, sine, start = take(10)
+    x_out, dy_out = take(2)
+    gains, weights_out, kept_out = take(2), [], []
+    for _ in range(2):
+        weights_out.append(dict(zip(WEIGHT_NAMES, take(3))))
+        kept_out.append(dict(zip(KEPT_NAMES, take(13))))
+    full_norms, shift_0, shift_1, cos_held, sin_held, start_held, up_0, up_1, x_held = take(9)
+    held_weights = [dict(zip(WEIGHT_NAMES, take(3))) for _ in range(2)]
+    kept = dict(zip(KEPT_NAMES, take(13)))
+    result, inner_own, held, own = take(4)
+    sems, quad_sems, local, free = take(4)
+    shifts, ups = (shift_0, shift_1), (up_0, up_1)
+    locals_used = [0]
+
+    def place():
+        locals_used[0] += 1
+        return local.at[locals_used[0] - 1]
+
+    def load(source, ref):
+        staged = Staged(ref, pltpu.make_async_copy(source, ref, place()), False)
+        staged.begin()
+        return staged
+
+    def keep(ref, target):
+        return Staged(ref, pltpu.make_async_copy(ref, target, place()), True)
+
+    cos_held, sin_held = load(cosine, cos_held), load(sine, sin_held)
+    start_held = load(start, start_held)
+    ups = [load(w_up.at[layer], ups[layer]) for layer in range(2)]
+    wire, quad_wire, quad = Wire(sems), Wire(quad_sems), Quad()
     second = jnp.logical_not(quad.first)
-    x_swap = wire.copy(blocks[1], x_ref, quad.across, quad.first)
-    dy_swap = wire.copy(blocks[0], dy_ref, quad.across, second)
-    kept = local.at[3]
+    half = size // 2
+    own_x = pltpu.make_async_copy(ends.at[pl.ds(0, size)], x_held, place())
+    own_dy = pltpu.make_async_copy(ends.at[pl.ds(size, size)], dy_out, place())
 
     @pl.when(quad.first)
     def _():
-        x_swap.start()
-        pltpu.make_async_copy(blocks[0], x_ref, kept).start()
+        own_x.start()
 
     @pl.when(second)
     def _():
-        dy_swap.start()
-        pltpu.make_async_copy(blocks[1], dy_ref, kept).start()
-
-    fetches = [
-        Fetch(wire, w_qkv_ref.at[0], qkv_ref, True),
-        Fetch(wire, w_out_ref.at[0], out_ref, False),
+        own_dy.start()
+
+    quad_barrier(quad_wire, quad, quad.across)
+    x_parts = [
+        quad_wire.copy(
+            ends.at[pl.ds(size + part * half, half)], x_held.at[pl.ds(part * half, half)],
+            quad.across, quad.first,
+        )
+        for part in range(2)
     ]
-    part = norms_ref.shape[1]
-    slot = full_norms_ref.at[:, pl.ds(pl.multiple_of(wire.at * part, part), part)]
+    dy_swap = quad_wire.copy(ends.at[pl.ds(0, size)], dy_out, quad.across, second)
+
+    @pl.when(quad.first)
+    def _():
+        x_parts[0].start()
+
+    def start_later():
+        @pl.when(quad.first)
+        def _():
+            x_parts[0].wait_send()
+            x_parts[1].start()
+
+        x_parts[0].settled = True
+
+        @pl.when(second)
+        def _():
+            dy_swap.start()
+
+    def x_arrives(part):
+        if part == 0:
+
+            @pl.when(quad.first)
+            def _():
+                own_x.wait()
+
+        @pl.when(second)
+        def _():
+            x_parts[part].wait_recv()
+
+    def fetches(layer, names):
+        sources = {"qkv": w_qkv, "out": w_out, "down": w_down}
+        wanted = [
+            Fetch(quad_wire, sources[name].at[layer], held_weights[layer][name], name == "qkv")
+            for name in names
+        ]
+        at = locals_used[0]
+        locals_used[0] += len(names)
+        steps = fetch_steps(quad_wire, quad, wanted, [local.at[at + i] for i in range(len(names))])
+        outs = [keep(held_weights[layer][name], weights_out[layer][name]) for name in names]
+        finished = []
+
+        def step():
+            if not finished and next(steps, "end") == "end":
+                finished.append(True)
+                done(*outs)
+
+        def finish():
+            while not finished:
+                step()
+
+        return step, finish, outs
+
+    begin, begin_all, begin_outs = fetches(0, ("qkv", "out"))
+    down, down_all, down_outs = fetches(0, ("down",))
+    rest, rest_all, rest_outs = fetches(1, WEIGHT_NAMES)
+    begin()
+    part = norms.shape[1]
+    columns = pl.ds(pl.multiple_of(wire.at * part, part), part)
     sent = [
-        wire.send(norms_ref, slot, {"narrow": peer})
+        quad_wire.send(norms, full_norms.at[:, columns], {"narrow": peer})
         for peer in (wire.diagonal, wire.far, wire.near)
     ]
-    own = pltpu.make_async_copy(norms_ref, slot, local.at[len(fetches)])
-    own.start()
-    run(fetch_steps(wire, quad, fetches, local))
+    full_norms[:, columns] = norms[...]
+    begin()
     for made in sent:
         made.wait_recv()
-    own.wait()
+    spread = full_norms[...].astype(F32)
+    for layer in range(2):
+        gains[layer][...] = spread[4 * layer : 4 * layer + 4]
+        shifts[layer][...] = spread[8 + 4 * layer : 12 + 4 * layer]
+
+    actions = [
+        [begin, start_later],
+        [begin_all, down],
+        [down, rest],
+        [down, rest],
+        [down_all, rest],
+        [rest_all],
+    ]
+    hand = Hand(wire, free, actions)
+    x_now = Pending(x_held, x_arrives)
+    before = {}
+    for layer in range(2):
+        now = {name: keep(kept[name], kept_out[layer][name]) for name in KEPT_NAMES}
+        if layer == 0:
+            now["y"] = keep(result, kept_out[layer]["y"])
+        gather_weights = held_weights[layer]
+        waits = {"qkv": begin_all, "out": begin_all, "down": down_all}
+        weights = {
+            name: Pending(ref, waits[name] if layer == 0 else rest_all)
+            for name, ref in gather_weights.items()
+        }
+        ready(*(before[name] for name in ("q", "k", "v", "o", "lse", "z", "h") if before))
+        hand.settled = [before["inner"]] if before else []
+        attend_half_body(
+            wire, hand, x_now, gains[layer], shifts[layer], cos_held, sin_held, start_held,
+            weights["qkv"], weights["out"],
+            now["a"], now["q"], now["k"], now["v"], now["o"], now["lse"], now["z"], now["h"],
+            inner_own, held, own,
+        )
+        ready(*(before[name] for name in ("e", "d", "w") if before))
+        hand.settled = [now["a"]]
+        hand.last = layer == 1
+        feed_half_body(
+            wire, hand, inner_own, kept["h"], gains[layer], shifts[layer], ups[layer],
+            b_up.at[layer], weights["down"],
+            now["inner"], now["e"], now["d"], now["w"], now["y"],
+            held, own,
+        )
+        if layer == 0:
+            x_copy = keep(x_held, x_out)
+            x_copy.begin()
+            x_now = result
+        else:
+            ready(*before.values())
+        before = now
+    ready(x_copy, *before.values(), *begin_outs, *down_outs, *rest_outs)
 
     @pl.when(quad.first)
     def _():
-        pltpu.make_async_copy(blocks[0], x_ref, kept).wait()
         dy_swap.wait_recv()
 
     @pl.when(second)
     def _():
-        pltpu.make_async_copy(blocks[1], dy_ref, kept).wait()
-        x_swap.wait_recv()
-
-    wire.finish()
-
-
-def anywhere(count):
-    return [pl.BlockSpec(memory_space=pl.ANY)] * count
-
-
-def begin(blocks, w_qkv, w_out, norms):
-    width = blocks.shape[1]
-    shapes = [
-        (w_qkv.shape[1:], BF16),
-        ((w_out.shape[2], width), BF16),
-        ((norms.shape[0], width), BF16),
-        ((blocks.shape[0] // 2, width), BF16),
-        ((blocks.shape[0] // 2, width), BF16),
+        own_dy.wait()
+
+    quad_wire.finish()
+    assert wire.used <= sems.shape[0] and quad_wire.used <= quad_sems.shape[0]
+    assert locals_used[0] <= local.shape[0]
+
+
+def forward(ends, w_qkv, w_out, w_down, w_up, norms, b_up, cosine, sine, start):
+    size, width = ends.shape[0] // 2, ends.shape[1]
+    part, hidden = w_out.shape[2], w_up.shape[2]
+    length = cosine.shape[0]
+    rows, line_rows = ((size, width), BF16), ((size, width), F32)
+    weights = [((width, 3 * part), BF16), ((part, width), BF16), ((hidden, width), BF16)]
+    kept = [((length, width), BF16)] + [((length, part), BF16)] * 4
+    kept += [((8, length), F32), line_rows, line_rows]
+    kept += [((length, width), BF16)] + [((length, hidden), BF16)] * 2 + [line_rows, rows]
+    norm = ((4, width), F32)
+    outs = [rows, rows] + [norm] * 2 + (weights + kept) * 2
+    out_specs = [pl.BlockSpec(memory_space=pl.ANY)] * 2 + vmem(2)
+    out_specs += [pl.BlockSpec(memory_space=pl.ANY)] * 32
+    buffers = [
+        ((norms.shape[0], width), BF16), norm, norm,
+        (cosine.shape, F32), (sine.shape, F32), (start.shape, jnp.int32),
+        ((width, hidden), BF16), ((width, hidden), BF16), rows,
     ]
-    return pl.pallas_call(
-        begin_kernel,
-        in_specs=anywhere(4),
-        out_specs=anywhere(5),
-        out_shape=shaped(*shapes),
-        scratch_shapes=[pltpu.SemaphoreType.DMA((8,)), pltpu.SemaphoreType.DMA((40,))],
-        compiler_params=pltpu.CompilerParams(collective_id=10, has_side_effects=True),
-        name="begin",
-    )(blocks, w_qkv, w_out, norms)
-
-
-def fetch_rest_steps(wire, quad, refs, outs, scratch):
-    w_qkv, w_out, w_down = refs
-    down_0, qkv_1, out_1, down_1 = outs
-    first = fetch_steps(wire, quad, [Fetch(wire, w_down.at[0], down_0, False)], scratch[0])
-    rest = [
-        Fetch(wire, w_qkv.at[1], qkv_1, True),
-        Fetch(wire, w_out.at[1], out_1, False),
-        Fetch(wire, w_down.at[1], down_1, False),
-    ]
-    second = fetch_steps(wire, quad, rest, scratch[1])
-    next(first)
-    yield
-    next(first)
-    next(second)
-    yield
-    next(first)
-    next(second)
-    yield
-    next(first, None)
-    next(second)
-    yield
-    next(second, None)
+    buffers += weights * 2 + kept + [rows, rows, ((6, size, width), BF16), line_rows]
+    apart = pl.BlockSpec(memory_space=pl.ANY)
+    found = pl.pallas_call(
+        functools.partial(forward_kernel, size),
+        in_specs=[apart] * 5 + vmem(2) + [apart] * 3,
+        out_specs=out_specs,
+        out_shape=shaped(*outs),
+        scratch_shapes=[pltpu.VMEM(*entry) for entry in buffers]
+        + [
+            pltpu.SemaphoreType.DMA((88,)),
+            pltpu.SemaphoreType.DMA((104,)),
+            pltpu.SemaphoreType.DMA((56,)),
+            pltpu.SemaphoreType.REGULAR((2,)),
+        ],
+        compiler_params=pltpu.CompilerParams(
+            collective_id=1, has_side_effects=True, vmem_limit_bytes=58 * 2**20
+        ),
+        name="forward",
+    )(ends, w_qkv, w_out, w_down, w_up, norms, b_up, cosine, sine, start)
+    x, dy = found[:2]
+    gains, found = found[2:4], found[4:]
+    weights, saved = [], []
+    resid = x
+    for layer in range(2):
+        qkv, out, down = found[16 * layer : 16 * layer + 3]
+        a, q, k, v, o, lse, z, h, inner, e, d, w, y = found[16 * layer + 3 : 16 * layer + 16]
+        weights.append((qkv, out, (w_up, layer), None, down, gains[layer], None))
+        saved.append((resid, a, q, k, v, o, lse, z, h, inner, e, d, w))
+        resid = y
+    return dy, resid, weights, saved
 
 
 def swap(block, distance):
@@ -1885,17 +2120,15 @@
     return lax.all_to_all(block, "narrow", split_axis=1, concat_axis=0, tiled=True)
 
 
-def layer_forward(resid, weights, start, tables, background=None):
+def layer_forward(resid, weights, start, tables):
     w_qkv, w_out, w_up, b_up, w_down, gains, shifts = weights
-    (normed, query, keys, values, mixture, logs, branch, middle, inner), more = attend_half(
-        background or Background(1), resid, gains, shifts, *tables, start[:, None], w_qkv, w_out
+    (normed, query, keys, values, mixture, logs, branch, middle, inner), _ = attend_half(
+        Background(1), resid, gains, shifts, *tables, start[:, None], w_qkv, w_out
     )
-    if background is not None:
-        w_down = more[0]
     inner, active, slope, second, result = feed_half(
         20 + w_up[1], inner, middle, gains, shifts, w_up, b_up, w_down
     )
-    return result, more, (
+    return result, (
         resid, normed, query, keys, values, mixture, logs, branch, middle, inner, active, slope, second
     )
 
@@ -1977,56 +2210,42 @@
     norms = jnp.concatenate([norm_gain, norm_bias]).reshape(16, -1)
 
     if wide == 8:
-        qkv_0, out_0, norms, resid, upstream = begin(ends, w_qkv, w_out, norms)
+        upstream, result, weights, saved = forward(
+            ends, w_qkv, w_out, w_down, w_up, norms, b_up, *tables, start[:, None]
+        )
+        grad, grad_came, result_came, totals = backward_wide(
+            upstream, result, saved, weights, start, tables
+        )
     else:
         came = route(jnp.where(first, ends[row_count:], ends[:row_count]))
-        norms = lax.all_gather(norms, "narrow", axis=1, tiled=True)
-        qkv_0, out_0 = by_heads(w_qkv[0], at), to_rows(w_out[0])
-        down_0, down_1 = to_rows(w_down[0]), to_rows(w_down[1])
-        qkv_1, out_1 = by_heads(w_qkv[1], at), to_rows(w_out[1])
+        norms = lax.all_gather(norms, "narrow", axis=1, tiled=True).astype(F32)
         resid = jnp.where(first, ends[:row_count], came)
         upstream = jnp.where(first, came, ends[row_count:])
-    norms = norms.astype(F32)
-
-    if wide == 8:
-        width = ends.shape[1]
-        part = w_out.shape[2]
-        background = Background(
-            11, [w_qkv, w_out, w_down],
-            [
-                ((w_up.shape[2], width), BF16),
-                (w_qkv.shape[1:], BF16),
-                ((part, width), BF16),
-                ((w_up.shape[2], width), BF16),
-            ],
-            [pltpu.SemaphoreType.DMA((4,))] * 2, fetch_rest_steps, quad=True, semaphores=72,
-        )
-        weights_0 = (qkv_0, out_0, (w_up, 0), b_up[0], None, norms[0:4], norms[8:12])
-        middle, more, saved_first = layer_forward(resid, weights_0, start, tables, background)
-        down_0, qkv_1, out_1, down_1 = more
-        weights_0 = weights_0[:4] + (down_0,) + weights_0[5:]
-    else:
-        weights_0 = (qkv_0, out_0, (w_up, 0), b_up[0], down_0, norms[0:4], norms[8:12])
-        middle, _, saved_first = layer_forward(resid, weights_0, start, tables)
-    weights_1 = (qkv_1, out_1, (w_up, 1), b_up[1], down_1, norms[4:8], norms[12:16])
-    weights = (weights_0, weights_1)
-    result, _, saved_second = layer_forward(middle, weights_1, start, tables)
-    if wide == 8:
-        grad, grad_came, result_came, (totals_first, totals_second) = backward_wide(
-            upstream, result, (saved_first, saved_second), weights, start, tables
-        )
-    else:
+
+        def weights_of(layer):
+            return (
+                by_heads(w_qkv[layer], at), to_rows(w_out[layer]), (w_up, layer), b_up[layer],
+                to_rows(w_down[layer]), norms[4 * layer : 4 * layer + 4],
+                norms[8 + 4 * layer : 12 + 4 * layer],
+            )
+
+        weights = [weights_of(layer) for layer in range(2)]
+        middle, saved_first = layer_forward(resid, weights[0], start, tables)
+        result, saved_second = layer_forward(middle, weights[1], start, tables)
         result_came = route(result)
-        grad, grads_second = layer_backward(upstream, saved_second, weights_1, start, tables)
+        grad, grads_second = layer_backward(upstream, saved_second, weights[1], start, tables)
         totals_second = reduce_grads(grads_second, at)
-        grad, grads_first = layer_backward(grad, saved_first, weights_0, start, tables)
+        grad, grads_first = layer_backward(grad, saved_first, weights[0], start, tables)
         totals_first = reduce_grads(grads_first, at)
         grad_came = route(grad)
+        totals = [
+            jnp.stack([a.astype(F32), b.astype(F32)])
+            for a, b in zip(totals_first, totals_second)
+        ]
 
     ends_out = jnp.where(
         first, jnp.concatenate([grad, grad_came]), jnp.concatenate([result_came, result])
     )
-    totals = [jnp.stack([a.astype(F32), b.astype(F32)]) for a, b in zip(totals_first, totals_second)]
     return (ends_out,) + tuple(totals)
 
 

time: 553 us -> 523 us (0.946)
  Pallas kernels: 513 us -> 486 us
    pallas_call x5 -> x1, Pallas kernels: 200 us -> 160 us  [forward(): pl.pallas_call(functools.partial(forward_kernel, size), in_specs=[apart]...]
    pallas_call x1, Pallas kernels: 313 us -> 326 us  [backward_wide(): pl.pallas_call(functools.partial(backward_kernel, shape), in_specs=specs,...]
where the time goes in v5:
time: 523 us; the launch traced here: 514 us
  Pallas kernels  486 us (93%)
  other arithmetic  22.5 us (4%)
    pallas_call x1, Pallas kernels, backward_wide(): pl.pallas_call(functools.partial(backward_kernel, shape), in_specs=specs,...  326 us
    pallas_call x1, Pallas kernels, forward(): pl.pallas_call(functools.partial(forward_kernel, size), in_specs=[apart]...  160 us
    another operation x4, other arithmetic, backward_wide(): jnp.stack([block.reshape(-1, block.shape[-1]).astype(F32) for block in pa...  13.1 us

profile of v5, /device:TPU:0, one launch (start us, length us, event | category | flops | bytes accessed | tf_op | source)
XLA Modules:
  0.0 514.1 jit_solution(13736168815199497585)
XLA Ops:
  0.6 0.0 copy-start
  0.7 0.7 copy-done
  1.3 0.2 dynamic-slice_reduce_fusion
  1.6 0.2 reduce-window.8
  1.7 0.1 select_reduce_fusion
  1.8 0.0 copy-start.11
  1.9 1.3 reshape.112.refs_6_
  3.2 0.7 pad_maximum_fusion.2
  3.9 0.6 reshape.109.refs_5_
  4.5 1.0 copy.20.refs_9_
  5.5 1.9 fusion
  7.4 1.8 pad_maximum_fusion
  9.3 0.0 copy-done.11
  9.3 160.0 %forward.1 = (bf16[256,1024]{1,0:T(8,128)(2,1)}, bf16[256,1024]{1,0:T(8,128)(2,1)}, f32[4,1024]{1,0:T(4,128)}, f32[4,1024]{1,0:T(4,128)}, bf16[1024,768]{1,0:T(8...) custom-call(bf16[512,1024]{1,0:T(8,128)(2,1)} %refs_0_.1, ...), custom_call_target="tpu_custom_call" | custom-call | tf_op jit(solution)/shard_map/forward/pallas_call | solution.py:2052
  169.3 0.0 copy-start.2
  169.3 325.7 %backward.1 = (bf16[256,1024]{1,0:T(8,128)(2,1)}, bf16[256,1024]{1,0:T(8,128)(2,1)}, bf16[256,1024]{1,0:T(8,128)(2,1)}, f32[16,256]{1,0:T(8,128)}, f32[16,256]{1...) custom-call(bf16[256,1024]{1,0:T(8,128)(2,1)} %get-tuple-element.57., ...), custom_call_target="tpu_custom_call" | custom-call | tf_op jit(solution)/shard_map/backward/pallas_call | solution.py:1681
  494.9 0.0 copy-start.13
  494.9 0.0 copy-start.12
  495.0 0.0 copy-start.9
  495.0 0.0 copy-start.10
  495.0 0.0 copy-done.2
  495.0 2.9 maximum_select_fusion
  497.8 0.0 copy-done.13
  497.9 0.0 copy-done.12
  497.9 0.6 pad_maximum_fusion.5
  498.5 0.6 pad_maximum_fusion.4
  499.1 0.6 pad_maximum_fusion.3
  499.7 1.5 maximum_convert_fusion.3
  501.2 3.5 maximum_convert_fusion.2
  504.7 0.8 copy-done.6
  505.5 4.2 maximum_convert_fusion
  509.7 3.9 maximum_convert_fusion.1
  (21 shorter events, 0.1 us)
Async XLA Ops:
  0.6 0.7 copy-start
  1.8 7.4 %copy-start.11 = (s32[1024]{0:T(1024)}, s32[1024]{0:T(1024)S(1)}, u32[]{:S(2)}) copy-start(s32[1024]{0:T(1024)S(1)} %select_reduce_fusion) | copy-start | bytes 12292
  169.3 325.7 %copy-start.2 = (bf16[256,1024]{1,0:T(8,128)(2,1)S(1)}, bf16[256,1024]{1,0:T(8,128)(2,1)}, u32[]{:S(2)}) copy-start(bf16[256,1024]{1,0:T(8,128)(2,1)} %get-tuple-element.58.refs_1_) | copy-start | bytes 1572868
  494.9 2.9 copy-start.13
  494.9 2.9 copy-start.12
  495.0 4.8 copy-start.9
  495.0 4.8 copy-start.10
  497.9 3.3 copy-start.7
  497.9 3.3 copy-start.8
  501.2 3.5 copy-start.5
  501.2 4.3 copy-start.6
  505.5 4.2 copy-start.3
  505.5 4.2 copy-start.4
  509.7 3.9 copy-start.1

commit v6 on v5

--- a/solution.py
+++ b/solution.py
@@ -914,7 +914,7 @@
 
 
 class Fold:
-    def __init__(self, wire, line, ref, by_side, into, across, final):
+    def __init__(self, wire, line, ref, by_side, into, across, final=None):
         self.wire, self.line, self.ref, self.by_side = wire, line, ref, by_side
         self.into, self.across, self.final = into, across, final
         rows = ref.shape[0]
@@ -925,12 +925,17 @@
         for way, (peer, _, _, _, inner) in enumerate(line.ways):
             cuts = [into.at[way, pl.ds(c * CHUNK, CHUNK)] for c in range(self.count)]
             self.copies.append([wire.copy(cut, cut, peer, inner) for cut in cuts])
+        self.pairs = []
+        if final is None:
+            for cut in (pl.ds(c * CHUNK, CHUNK) for c in range(self.count)):
+                source = into.at[1 - line.upper, cut]
+                self.pairs.append(wire.copy(source, across.at[cut], line.side, line.at_end))
 
     @staticmethod
-    def scratch(rows, columns, by_side):
+    def scratch(rows, columns, by_side, streams=False):
         return [
             pltpu.VMEM((2, rows // 4 if by_side else rows // 2, columns), BF16),
-            pltpu.VMEM((rows // 2 if by_side else rows // 4, columns), BF16),
+            pltpu.VMEM((rows // 2 if by_side or streams else rows // 4, columns), BF16),
         ]
 
     def place(self, way, chunk):
@@ -980,6 +985,8 @@
         self.into[way, cut] = (own() + self.into[way, cut].astype(F32)).astype(BF16)
         if role == "inner":
             made.start()
+        elif self.pairs:
+            self.pairs[chunk].start()
 
     def chunks(self):
         return [functools.partial(self.step, chunk) for chunk in range(self.count)]
@@ -1081,6 +1088,44 @@
         for pair in self.sides:
             for made in pair:
                 made.wait_recv()
+
+
+class Stream(Spread):
+    def __init__(self, wire, line, view, rows, fold):
+        super().__init__(wire, line, view, rows, False)
+        self.fold, self.own_copies = fold, []
+        wire.made.remove(self.side)
+        for way in (0, 1):
+            self.own_copies.append([])
+            for chunk in range(self.count):
+                source = fold.across.at[pl.ds(chunk * CHUNK, CHUNK)]
+                copy = pltpu.make_async_copy(source, self.chunk(way, chunk), wire.sems.at[wire.used])
+                wire.used += 1
+                self.own_copies[way].append(copy)
+
+    def start(self):
+        pass
+
+    def step(self, chunk, way, role):
+        if role != "first":
+            super().step(chunk, way, role)
+            return
+        fold, cut = self.fold, pl.ds(chunk * CHUNK, CHUNK)
+        fold.pairs[chunk].wait_recv()
+        total = fold.into[1 - way, cut].astype(F32) + fold.across[cut].astype(F32)
+        fold.across[cut] = total.astype(BF16)
+        self.copies[way][chunk].start_from(fold.across.at[cut])
+        self.own_copies[way][chunk].start()
+
+    def settle(self):
+        for made in sum(self.copies, []) + self.fold.pairs:
+            made.settle()
+        for way, copies in enumerate(self.own_copies):
+
+            @pl.when(self.line.ways[way][1])
+            def _():
+                for copy in copies:
+                    copy.wait()
 
 
 class Sequence:
@@ -1263,11 +1308,12 @@
     )
 
 
-def spread_feed(wire, line, full_up, full_down):
-    return (
-        Spread(wire, line, lambda rows: full_up.at[rows], full_up.shape[0], False),
-        Spread(wire, line, lambda rows: full_down.at[:, rows], full_down.shape[1], True),
-    )
+def rows_of(ref):
+    return lambda rows: ref.at[rows]
+
+
+def spread_down(wire, line, full_down):
+    return Spread(wire, line, lambda rows: full_down.at[:, rows], full_down.shape[1], True)
 
 
 def spread_attend(wire, line, full_out, full_qkv):
@@ -1275,12 +1321,6 @@
         Spread(wire, line, lambda rows: full_out.at[:, rows], full_out.shape[1], False),
         Spread(wire, line, lambda rows: full_qkv.at[rows], full_qkv.shape[0], True),
     )
-
-
-def place_own(wire, line, spread, final):
-    @pl.when(line.at_end)
-    def _():
-        wire.move(final, spread.own())
 
 
 def swap_across(wire, source, target, first_sends):
@@ -1401,7 +1441,7 @@
     second, hidden, mixture, projected, dk, dv, held, own, dh, dz, dx = take(11)
     grad_up, grad_down, grad_out, grad_qkv = take(4)
     feed_scratch, attend_scratch = take(4), take(4)
-    finals = [dict(zip(("up", "down", "out", "qkv"), take(4))) for _ in range(2)]
+    finals = [dict(zip(("down", "out", "qkv"), take(3))) for _ in range(2)]
     small = [take(4) for _ in range(2)]
     norms = [take(2) for _ in range(2)]
     biases = take(2)
@@ -1440,8 +1480,7 @@
 
     def fold_feed(layer):
         folds[layer, "up"], folds[layer, "down"] = fold_pair(
-            wide_wire, line, (grad_up, grad_down),
-            (finals[layer]["up"], finals[layer]["down"]), feed_scratch,
+            wide_wire, line, (grad_up, grad_down), (None, finals[layer]["down"]), feed_scratch,
         )
 
     def fold_attend(layer):
@@ -1454,9 +1493,10 @@
         fold_feed(layer)
         fold_attend(layer)
         full = fulls[layer]
-        spreads[layer, "up"], spreads[layer, "down"] = spread_feed(
-            wide_wire, line, full["up"], full["down"]
+        spreads[layer, "up"] = Stream(
+            wide_wire, line, rows_of(full["up"]), grad_up.shape[0], folds[layer, "up"]
         )
+        spreads[layer, "down"] = spread_down(wide_wire, line, full["down"])
         spreads[layer, "out"], spreads[layer, "qkv"] = spread_attend(
             wide_wire, line, full["out"], full["qkv"]
         )
@@ -1481,14 +1521,6 @@
     def come_home(layer, names):
         return lambda: waits[layer, names]()
 
-    def spread_up(layer):
-        def action():
-            folds[layer, "up"].end()
-            place_own(wide_wire, line, spreads[layer, "up"], finals[layer]["up"])
-            spreads[layer, "up"].start()
-
-        return action
-
     def fill(count):
         while len(sequence.chunks) < count:
             sequence.add([lambda way, role: None])
@@ -1496,9 +1528,7 @@
     def feed_fold_part(layer):
         if layer == 0:
             sequence.before_next(folds[layer, "down"].start)
-        chunks = folds[layer, "up"].chunks()
-        sequence.add(chunks).add(folds[layer, "down"].chunks())
-        sequence.after(chunks[-1], folds[layer, "up"].start_side)
+        sequence.add(folds[layer, "up"].chunks()).add(folds[layer, "down"].chunks())
         return len(sequence.chunks)
 
     def attend_fold_feed_spread_part(layer, feed_end):
@@ -1509,23 +1539,30 @@
         sequence.actions.setdefault(feed_end - 1 + 3 * LATE, []).extend(
             [go_home(layer, ("down",)), folds[layer, "up"].settle]
         )
+        fill(feed_end + 2 * LATE)
+        stream = spreads[layer, "up"].chunks()
+        sequence.add(stream[:6]).add(folds[layer, "qkv"].chunks())
+        qkv_end = len(sequence.chunks)
+        sequence.add(stream[6:])
         fill(feed_end + 3 * LATE + 2)
         sequence.before_next(come_home(layer, ("down",)))
         sequence.add(spreads[layer, "down"].chunks())
-        sequence.before_next(spread_up(layer))
-        sequence.add(folds[layer, "qkv"].chunks())
-        qkv_end = len(sequence.chunks)
-        sequence.add(spreads[layer, "up"].chunks())
         sequence.actions.setdefault(qkv_end - 1 + 3 * LATE, []).append(
             go_home(layer, ("out", "qkv"))
         )
         fill(qkv_end + 3 * LATE + 2)
         sequence.before_next(come_home(layer, ("out", "qkv")), spreads[layer, "out"].start)
+        sequence.after(stream[-1], spreads[layer, "up"].settle)
 
     feed_end = feed_fold_part(1)
     in_attend_1 = len(sequence.chunks)
     attend_fold_feed_spread_part(1, feed_end)
-    sequence.actions.setdefault(len(sequence.chunks) - 1, []).append(flow.greet)
+    settled = max(
+        at
+        for at, actions in sequence.actions.items()
+        if spreads[1, "up"].settle in actions or at == len(sequence.chunks) - 1
+    )
+    sequence.actions.setdefault(settled, []).append(flow.greet)
     sequence.add(spreads[1, "qkv"].chunks()).add(spreads[1, "out"].chunks())
     sequence.before_next(flow.greeted)
     in_feed_0 = len(sequence.chunks)
@@ -1659,10 +1696,10 @@
     ]
     buffers += grads
     scratch = [pltpu.VMEM(*entry) for entry in buffers]
-    for (first, _), (last, _) in (grads[0:2], grads[2:4]):
-        scratch += Fold.scratch(*first, False) + Fold.scratch(*last, True)
+    for streams, ((first, _), (last, _)) in ((True, grads[0:2]), (False, grads[2:4])):
+        scratch += Fold.scratch(*first, False, streams) + Fold.scratch(*last, True)
     for _ in range(2):
-        scratch += [pltpu.VMEM((rows // 4, columns), BF16) for (rows, columns), _ in grads]
+        scratch += [pltpu.VMEM((rows // 4, columns), BF16) for (rows, columns), _ in grads[1:]]
     for _ in range(2):
         scratch += [
             pltpu.VMEM((4, 8, part), F32),
@@ -1674,7 +1711,7 @@
     scratch += [pltpu.VMEM((1, hidden_count), F32)] * 2
     scratch += [
         pltpu.SemaphoreType.DMA((88,)),
-        pltpu.SemaphoreType.DMA((520,)),
+        pltpu.SemaphoreType.DMA((600,)),
         pltpu.SemaphoreType.DMA((20,)),
         pltpu.SemaphoreType.REGULAR((5,)),
     ]

time: 523 us -> 504 us (0.964)
  Pallas kernels: 486 us -> 468 us
    pallas_call x1, Pallas kernels: 326 us -> 308 us  [backward_wide(): pl.pallas_call(functools.partial(backward_kernel, shape), in_specs=specs,...]
where the time goes in v6:
time: 504 us; the launch traced here: 496 us
  Pallas kernels  468 us (93%)
  other arithmetic  22.5 us (4%)
    pallas_call x1, Pallas kernels, backward_wide(): pl.pallas_call(functools.partial(backward_kernel, shape), in_specs=specs,...  308 us
    pallas_call x1, Pallas kernels, forward(): pl.pallas_call(functools.partial(forward_kernel, size), in_specs=[apart]...  160 us
    another operation x4, other arithmetic, backward_wide(): jnp.stack([block.reshape(-1, block.shape[-1]).astype(F32) for block in pa...  13.1 us

profile of v6, /device:TPU:0, one launch (start us, length us, event | category | flops | bytes accessed | tf_op | source)
XLA Modules:
  0.0 496.0 jit_solution(1544208315447618927)
XLA Ops:
  0.6 0.0 copy-start
  0.7 0.7 copy-done
  1.3 0.2 dynamic-slice_reduce_fusion
  1.6 0.2 reduce-window.8
  1.7 0.1 select_reduce_fusion
  1.8 0.0 copy-start.11
  1.9 1.3 reshape.112.refs_6_
  3.2 0.7 pad_maximum_fusion.2
  3.9 0.6 reshape.109.refs_5_
  4.5 1.0 copy.20.refs_9_
  5.5 1.9 fusion
  7.4 1.8 pad_maximum_fusion
  9.3 160.0 %forward.1 = (bf16[256,1024]{1,0:T(8,128)(2,1)}, bf16[256,1024]{1,0:T(8,128)(2,1)}, f32[4,1024]{1,0:T(4,128)}, f32[4,1024]{1,0:T(4,128)}, bf16[1024,768]{1,0:T(8...) custom-call(bf16[512,1024]{1,0:T(8,128)(2,1)} %refs_0_.1, ...), custom_call_target="tpu_custom_call" | custom-call | tf_op jit(solution)/shard_map/forward/pallas_call | solution.py:2089
  169.3 307.6 %backward.1 = (bf16[256,1024]{1,0:T(8,128)(2,1)}, bf16[256,1024]{1,0:T(8,128)(2,1)}, bf16[256,1024]{1,0:T(8,128)(2,1)}, f32[16,256]{1,0:T(8,128)}, f32[16,256]{1...) custom-call(bf16[256,1024]{1,0:T(8,128)(2,1)} %get-tuple-element.57., ...), custom_call_target="tpu_custom_call" | custom-call | tf_op jit(solution)/shard_map/backward/pallas_call | solution.py:1718
  476.9 0.0 copy-start.13
  476.9 0.0 copy-start.12
  476.9 0.0 copy-start.9
  476.9 0.0 copy-start.10
  476.9 0.0 copy-done.2
  476.9 2.9 maximum_select_fusion
  479.8 0.0 copy-done.12
  479.8 0.6 pad_maximum_fusion.5
  480.4 0.6 pad_maximum_fusion.4
  481.1 0.6 pad_maximum_fusion.3
  481.7 0.0 copy-done.9
  481.7 1.5 maximum_convert_fusion.3
  483.1 0.0 copy-done.8
  483.1 3.5 maximum_convert_fusion.2
  486.7 0.8 copy-done.6
  487.4 4.2 maximum_convert_fusion
  491.6 0.0 copy-done.4
  491.6 3.9 maximum_convert_fusion.1
  (21 shorter events, 0.1 us)
Async XLA Ops:
  0.6 0.7 copy-start
  1.8 7.4 %copy-start.11 = (s32[1024]{0:T(1024)}, s32[1024]{0:T(1024)S(1)}, u32[]{:S(2)}) copy-start(s32[1024]{0:T(1024)S(1)} %select_reduce_fusion) | copy-start | bytes 12292
  169.3 307.7 %copy-start.2 = (bf16[256,1024]{1,0:T(8,128)(2,1)S(1)}, bf16[256,1024]{1,0:T(8,128)(2,1)}, u32[]{:S(2)}) copy-start(bf16[256,1024]{1,0:T(8,128)(2,1)} %get-tuple-element.58.refs_1_) | copy-start | bytes 1572868
  476.9 2.9 copy-start.13
  476.9 2.9 copy-start.12
  476.9 4.8 copy-start.9
  476.9 4.8 copy-start.10
  479.8 3.3 copy-start.7
  479.8 3.3 copy-start.8
  483.1 3.5 copy-start.5
  483.1 4.3 copy-start.6
  487.4 4.2 copy-start.3
  487.4 4.2 copy-start.4
  491.6 3.9 copy-start.1

commit v7 on v6

--- a/solution.py
+++ b/solution.py
@@ -868,7 +868,7 @@
 
 
 CHUNK = 64
-LATE = 2
+LATE = 3
 
 
 class Line:

time: 504 us -> 512 us (1.016)
  Pallas kernels: 468 us -> 475 us
    pallas_call x1, Pallas kernels: 308 us -> 315 us  [backward_wide(): pl.pallas_call(functools.partial(backward_kernel, shape), in_specs=specs,...]
where the time goes in v7:
time: 512 us; the launch traced here: 504 us
  Pallas kernels  475 us (93%)
  other arithmetic  22.5 us (4%)
    pallas_call x1, Pallas kernels, backward_wide(): pl.pallas_call(functools.partial(backward_kernel, shape), in_specs=specs,...  315 us
    pallas_call x1, Pallas kernels, forward(): pl.pallas_call(functools.partial(forward_kernel, size), in_specs=[apart]...  160 us
    another operation x4, other arithmetic, backward_wide(): jnp.stack([block.reshape(-1, block.shape[-1]).astype(F32) for block in pa...  13.1 us

profile of v7, /device:TPU:0, one launch (start us, length us, event | category | flops | bytes accessed | tf_op | source)
XLA Modules:
  0.0 503.7 jit_solution(18392659055889000547)
XLA Ops:
  0.6 0.0 copy-start
  0.7 0.7 copy-done
  1.3 0.2 dynamic-slice_reduce_fusion
  1.6 0.2 reduce-window.8
  1.7 0.1 select_reduce_fusion
  1.8 0.0 copy-start.11
  1.9 1.3 reshape.112.refs_6_
  3.2 0.7 pad_maximum_fusion.2
  3.9 0.6 reshape.109.refs_5_
  4.5 1.0 copy.20.refs_9_
  5.5 1.9 fusion
  7.4 1.8 pad_maximum_fusion
  9.3 0.0 copy-done.11
  9.3 160.0 %forward.1 = (bf16[256,1024]{1,0:T(8,128)(2,1)}, bf16[256,1024]{1,0:T(8,128)(2,1)}, f32[4,1024]{1,0:T(4,128)}, f32[4,1024]{1,0:T(4,128)}, bf16[1024,768]{1,0:T(8...) custom-call(bf16[512,1024]{1,0:T(8,128)(2,1)} %refs_0_.1, ...), custom_call_target="tpu_custom_call" | custom-call | tf_op jit(solution)/shard_map/forward/pallas_call | solution.py:2089
  169.3 0.0 copy-start.2
  169.3 315.3 %backward.1 = (bf16[256,1024]{1,0:T(8,128)(2,1)}, bf16[256,1024]{1,0:T(8,128)(2,1)}, bf16[256,1024]{1,0:T(8,128)(2,1)}, f32[16,256]{1,0:T(8,128)}, f32[16,256]{1...) custom-call(bf16[256,1024]{1,0:T(8,128)(2,1)} %get-tuple-element.57., ...), custom_call_target="tpu_custom_call" | custom-call | tf_op jit(solution)/shard_map/backward/pallas_call | solution.py:1718
  484.6 0.0 copy-start.13
  484.6 0.0 copy-start.12
  484.6 0.0 copy-start.9
  484.6 2.9 maximum_select_fusion
  487.6 0.6 pad_maximum_fusion.5
  488.2 0.6 pad_maximum_fusion.4
  488.8 0.6 pad_maximum_fusion.3
  489.4 0.0 copy-done.10
  489.4 1.5 maximum_convert_fusion.3
  490.8 0.0 copy-done.7
  490.9 3.5 maximum_convert_fusion.2
  494.4 0.8 copy-done.6
  495.2 4.2 maximum_convert_fusion
  499.3 0.0 copy-done.3
  499.3 3.9 maximum_convert_fusion.1
  503.3 0.0 copy-done.1
  (21 shorter events, 0.1 us)
Async XLA Ops:
  0.6 0.7 copy-start
  1.8 7.4 %copy-start.11 = (s32[1024]{0:T(1024)}, s32[1024]{0:T(1024)S(1)}, u32[]{:S(2)}) copy-start(s32[1024]{0:T(1024)S(1)} %select_reduce_fusion) | copy-start | bytes 12292
  169.3 315.4 %copy-start.2 = (bf16[256,1024]{1,0:T(8,128)(2,1)S(1)}, bf16[256,1024]{1,0:T(8,128)(2,1)}, u32[]{:S(2)}) copy-start(bf16[256,1024]{1,0:T(8,128)(2,1)} %get-tuple-element.58.refs_1_) | copy-start | bytes 1572868
  484.6 2.9 copy-start.13
  484.6 2.9 copy-start.12
  484.6 4.8 copy-start.9
  484.6 4.8 copy-start.10
  487.5 3.3 copy-start.7
  487.5 3.3 copy-start.8
  490.8 3.5 copy-start.5
  490.8 4.3 copy-start.6
  495.2 4.2 copy-start.3
  495.2 4.2 copy-start.4
  499.3 3.9 copy-start.1
